TPU v7x, 1024 devices: a whole 4x4x32 slice. The times are simulated.
1024 devices in a mesh: shard: 8 (over x, core), narrow: 4 (over y), wide: 32 (over z).
Axes of the slice: x: 4, y: 4, z: 32, core: 2. Of those that a mesh axis runs over, the one named last changes fastest.
Arguments:
- tokens: bfloat16 [8192, 4096], P(('narrow', 'wide'), 'shard'), may hold values from -6 to 6
- routes: int32 [8192, 8], P(('narrow', 'wide')), may hold values from 0 to 127, all different within a row; in each aligned block of 64 rows (0 to 63, 64 to 127, ...) at most 8 rows name the same one
- route_weight: float32 [8192, 8], P(('narrow', 'wide')), may hold values from 0.1 to 1
- gate_weight: bfloat16 [128, 4096, 1024], P(('narrow', 'wide'), None, 'shard'), may hold values from -0.09375 to 0.09375
- up_weight: bfloat16 [128, 4096, 1024], P(('narrow', 'wide'), None, 'shard'), may hold values from -0.09375 to 0.09375
- down_weight: bfloat16 [128, 1024, 4096], P(('narrow', 'wide'), 'shard'), may hold values from -0.1875 to 0.1875
Outputs:
- mixed: bfloat16 [8192, 4096], P(('narrow', 'wide'), 'shard')
Inputs may be any that keep to these rules, and one draw needn't show every extreme that they name: `routes`: within the 64 rows of one index of narrow and wide, no expert is named more than 8 times; each row names 8 different experts.
All inputs are finite; a program needn't handle non-finite values.
Results may differ from a plain program's by a relative error of at most 0.02.
Values may be sent and summed in bfloat16 or wider, within the bound.
No kernel may reach another device: no remote copies, remote signals or barrier semaphores. Data moves between devices by JAX's collectives and lax.ppermute only.
A program may use at most 64 MiB of HBM per device.

v0:
```python
import jax
import jax.numpy as jnp
from jax import lax
from jax.sharding import PartitionSpec as P


def shards(tokens, routes, route_weight, gate_weight, up_weight, down_weight):
    narrow_count = lax.axis_size("narrow")
    wide_count = lax.axis_size("wide")
    expert_count = narrow_count * wide_count
    token_count, top_count = routes.shape
    capacity = max(token_count // 8, token_count * top_count // expert_count)
    flat_ids = routes.reshape(-1)
    onehot = (flat_ids[:, None] == jnp.arange(expert_count, dtype=jnp.int32)[None, :]).astype(
        jnp.int32
    )
    earlier = jnp.cumsum(onehot, axis=0) - onehot
    slot_rank = jnp.sum(earlier * onehot, axis=1)
    target = flat_ids * capacity + slot_rank
    token_of = jnp.arange(token_count * top_count, dtype=jnp.int32) // top_count
    gate_rows = gate_weight[0]
    up_rows = up_weight[0]
    down_rows = down_weight[0]
    full_tokens = lax.all_gather(tokens, "shard", axis=1, tiled=True)
    row_width = full_tokens.shape[1]
    buffer = (
        jnp.zeros((expert_count * capacity, row_width), full_tokens.dtype)
        .at[target]
        .set(full_tokens[token_of])
    )
    arrived = lax.all_to_all(
        lax.all_to_all(
            buffer.reshape(narrow_count, wide_count, capacity, row_width),
            "narrow",
            split_axis=0,
            concat_axis=0,
            tiled=True,
        ),
        "wide",
        split_axis=1,
        concat_axis=1,
        tiled=True,
    )
    expert_rows = arrived.reshape(-1, arrived.shape[3])
    gate = jnp.dot(expert_rows, gate_rows, preferred_element_type=jnp.float32)
    up = jnp.dot(expert_rows, up_rows, preferred_element_type=jnp.float32)
    hidden = (jax.nn.silu(gate) * up).astype(jnp.bfloat16)
    down_terms = jnp.dot(hidden, down_rows, preferred_element_type=jnp.float32)
    summed = lax.psum_scatter(
        down_terms.astype(jnp.bfloat16), "shard", scatter_dimension=1, tiled=True
    )
    expert_out = summed.reshape(narrow_count, wide_count, capacity, -1)
    returned = lax.all_to_all(
        lax.all_to_all(expert_out, "narrow", split_axis=0, concat_axis=0, tiled=True),
        "wide",
        split_axis=1,
        concat_axis=1,
        tiled=True,
    )
    picked = returned.reshape(expert_count * capacity, -1)[target]
    weighted = picked.astype(jnp.float32) * route_weight.reshape(-1)[:, None]
    mixed = jnp.sum(weighted.reshape(token_count, top_count, -1), axis=1)
    return mixed.astype(jnp.bfloat16)


def solution(mesh):
    placed = (
        P(("narrow", "wide"), "shard"),
        P(("narrow", "wide"), None),
        P(("narrow", "wide"), None),
        P(("narrow", "wide"), None, "shard"),
        P(("narrow", "wide"), None, "shard"),
        P(("narrow", "wide"), "shard", None),
    )
    return jax.shard_map(
        shards,
        mesh=mesh,
        in_specs=placed,
        out_specs=P(("narrow", "wide"), "shard"),
        check_vma=False,
    )
```

profile of v0, /device:TPU:6, one launch (start us, length us, event | category | flops | bytes accessed | tf_op | source)
XLA Modules:
  0.0 1148.2 jit_solution(8152652475611668790)
XLA Ops:
  6.5 0.0 copy-start
  6.5 0.0 reduce-scatter.2.cloned.1.call-start
  6.5 0.9 copy.33
  7.4 0.1 eq.29
  7.5 0.1 eq.25
  7.6 0.7 broadcast_multiply_fusion
  8.3 0.1 copy.35
  8.4 0.2 fusion.17
  8.7 0.1 copy.32
  8.8 0.1 mul.37
  8.9 23.4 %all_gather.3 = bf16[64,4096]{1,0:T(8,128)(2,1)S(1)} all-gather(bf16[64,512]{1,0:T(8,128)(2,1)} %param.6), channel_id=1, replica_groups=mesh['shard'=8,'narrow'=4,'wide'=32] {'shard'}, dimensions={1}, use_global_device_ids=true | all-gather | bytes 589824 | tf_op jit(solution)/shard_map/all_gather | solution.py:24
  32.3 0.2 fusion.15
  32.5 4.4 gather_fusion
  36.9 12.4 %scatter_custom_fusion = bf16[1024,4096]{1,0:T(8,128)(2,1)} fusion(s32[512]{0:T(512)S(1)} %bitcast.44, bf16[512,4096]{1,0:T(8,128)(2,1)} %gather_fusion, bf16[]{:T(256)} %constant.26.clone.1), kind=kCustom, calls=%fused_computation.4 | custom fusion | bytes 8389120 | tf_op jit(solution)/shard_map/scatter | solution.py:29
  49.3 102.1 %all_to_all.20 = bf16[4,32,8,4096]{3,2,1,0:T(8,128)(2,1)} all-to-all(bf16[4,32,8,4096]{3,2,1,0:T(8,128)(2,1)} %bitcast.37), channel_id=1, replica_groups=mesh['shard'=8,'narrow'=4,'wide'=32] {'narrow'}, dimensions={0} | all-to-all | bytes 16777216 | tf_op jit(solution)/shard_map/all_to_all | solution.py:32
  151.4 7.7 copy.37
  159.1 752.5 %all_to_all.21 = bf16[4,32,8,4096]{3,2,0,1:T(8,128)(2,1)} all-to-all(bf16[4,32,8,4096]{3,2,0,1:T(8,128)(2,1)} %copy.37), channel_id=1, replica_groups=mesh['shard'=8,'narrow'=4,'wide'=32] {'wide'}, dimensions={1} | all-to-all | bytes 16777216 | tf_op jit(solution)/shard_map/all_to_all | solution.py:31
  911.6 7.8 copy.38
  919.4 0.0 copy-done.3
  919.4 5.8 fusion.7
  925.2 0.0 copy-done
  925.3 13.1 %convolution_convert_fusion = bf16[1024,4096]{1,0:T(8,128)(2,1)} fusion(bf16[1024,4096]{1,0:T(8,128)(2,1)} %bitcast.36, bf16[1,128,4096]{2,1,0:T(8,128)(2,1)S(1)} %copy-done, bf16[1,4096,128]{2,1,0:T(8,128)(2,1)S(1)} %copy-done.1, f32[1024,128]{1,0:T(8,128)S(1)} %fusion.7), kind=kOutput, calls=%fused_computation.3 | convolution fusion | flops 2152464384 | bytes 19398656 | tf_op jit(solution)/shard_map/dot_general | solution.py:48
  938.4 0.0 reduce-scatter.2.cloned.1.call-update
  938.4 52.3 %reduce-scatter.2.cloned.1.call-done = bf16[1024,512]{1,0:T(8,128)(2,1)} async-done(((bf16[1024,4096]{1,0:T(8,128)(2,1)}), bf16[1024,512]{1,0:T(8,128)(2,1)}) %reduce-scatter.2.cloned.1.call-update) | async-done | bytes 1048592 | tf_op jit(solution)/shard_map/reduce_scatter | solution.py:49
  990.7 20.3 %all_to_all.22 = bf16[4,32,8,512]{3,2,1,0:T(8,128)(2,1)S(1)} all-to-all(bf16[4,32,8,512]{3,2,1,0:T(8,128)(2,1)} %bitcast.40), channel_id=1, replica_groups=mesh['shard'=8,'narrow'=4,'wide'=32] {'narrow'}, dimensions={0} | all-to-all | bytes 2097152 | tf_op jit(solution)/shard_map/all_to_all | solution.py:54
  1011.0 1.1 copy.39
  1012.1 22.2 %all-to-all-start.3 = ((bf16[4,32,8,512]{3,2,0,1:T(8,128)(2,1)}), bf16[4,32,8,512]{3,2,0,1:T(8,128)(2,1)S(1)}, u32[]{:S(2)}, u32[]{:S(2)}) async-start(bf16[4,32,8,512]{3,2,0,1:T(8,128)(2,1)} %copy.39), calls=%async_computation.4 | async-start | bytes 2097152 | tf_op jit(solution)/shard_map/all_to_all | solution.py:53
  1034.3 0.1 copy.41
  1034.4 103.8 %all-to-all-done.3 = bf16[4,32,8,512]{3,2,0,1:T(8,128)(2,1)S(1)} async-done(((bf16[4,32,8,512]{3,2,0,1:T(8,128)(2,1)}), bf16[4,32,8,512]{3,2,0,1:T(8,128)(2,1)S(1)}, u32[]{:S(2)}, u32[]{:S(2)}) %all-to-all-start.3) | async-done | bytes 1048608 | tf_op jit(solution)/shard_map/all_to_all | solution.py:53
  1138.2 0.1 copy.40
  1138.3 2.0 gather_fusion.1
  1140.3 1.0 fusion.3
  (15 shorter events, 0.1 us)
Async XLA Ops:
  6.5 918.7 %copy-start = (bf16[1,128,4096]{2,1,0:T(8,128)(2,1)S(1)}, bf16[1,128,4096]{2,1,0:T(8,128)(2,1)}, u32[]{:S(2)}) copy-start(bf16[1,128,4096]{2,1,0:T(8,128)(2,1)} %param.11) | copy-start | bytes 3145732
  6.5 984.2 %reduce-scatter.2.cloned.1.call-start = ((), (), s32[]{:S(2)}) async-start(), calls=%async_computation.5 | async-start | bytes 9437184 | tf_op jit(solution)/shard_map/reduce_scatter | solution.py:49
  911.6 7.8 copy-start.3
  919.4 5.8 copy-start.1
  938.4 95.9 %copy-start.2 = (f32[64,8]{0,1:T(8,128)S(1)}, f32[64,8]{0,1:T(8,128)}, u32[]{:S(2)}) copy-start(f32[64,8]{0,1:T(8,128)} %param.8) | copy-start | bytes 6148
  1012.1 126.1 %all-to-all-start.3 = ((bf16[4,32,8,512]{3,2,0,1:T(8,128)(2,1)}), bf16[4,32,8,512]{3,2,0,1:T(8,128)(2,1)S(1)}, u32[]{:S(2)}, u32[]{:S(2)}) async-start(bf16[4,32,8,512]{3,2,0,1:T(8,128)(2,1)} %copy.39), calls=%async_computation.4 | async-start | bytes 2097152 | tf_op jit(solution)/shard_map/all_to_all | solution.py:53
Sparse Core Ops, SparseCore 0:
  938.5 52.1 reduce-scatter.1
where the time goes:
time: 1150 us
  blocking collectives  898 us (78%)
  waiting for transfers between devices  156 us (14%)
  local copies, waits for them, and re-layouts  37 us (3%)
  starting transfers between devices  22.2 us (2%)
  matrix products  18.9 us (2%)
  between operations  13.5 us (1%)
    all_to_all x1, blocking collectives, shards(): lax.all_to_all(lax.all_to_all(buffer.reshape(narrow_count, wide_count, ca...  753 us
    all_to_all x1, waiting for transfers between devices, shards(): lax.all_to_all(lax.all_to_all(expert_out, 'narrow', split_axis=0, concat_...  104 us
    all_to_all x1, blocking collectives, shards(): lax.all_to_all(buffer.reshape(narrow_count, wide_count, capacity, row_wid...  102 us
    reduce_scatter x1, waiting for transfers between devices, shards(): lax.psum_scatter(down_terms.astype(jnp.bfloat16), 'shard', scatter_dimens...  52.3 us
    all_gather x1, blocking collectives, shards(): full_tokens = lax.all_gather(tokens, 'shard', axis=1, tiled=True)  23.4 us
  transfers between devices with their start and end apart: 2, of which 2 were waited for; matrix products, arithmetic and copies ran while one was open for 0% of the time, Pallas kernels for 0%

commit v1 on v0

v1 whole, which is shorter than its diff:
```python
import jax
import jax.numpy as jnp
from jax import lax
from jax.experimental import pallas as pl
from jax.experimental.pallas import tpu as pltpu
from jax.sharding import Mesh, PartitionSpec as P

BF = jnp.bfloat16
F32 = jnp.float32
CAP = 8
LOW = 4
VMEM = 56 << 20


def hits(meta, base, n_low, wide_count, n_rows):
    top = meta.shape[0] // 2
    tokens = 64
    row = lax.broadcasted_iota(jnp.int32, (n_rows, tokens), 0)
    slot = row % CAP
    place = row // CAP
    expert = ((place // n_low) * wide_count + place % n_low + base).astype(F32)
    hit = jnp.zeros((n_rows, tokens), F32)
    weight = jnp.zeros((n_rows, tokens), F32)
    for k in range(top):
        same = meta[k : k + 1, :tokens] == expert
        hit = jnp.where(same, 1.0, hit)
        weight = jnp.where(same, meta[top + k : top + k + 1, :tokens], weight)
    earlier = (
        lax.broadcasted_iota(jnp.int32, (tokens, tokens), 0)
        < lax.broadcasted_iota(jnp.int32, (tokens, tokens), 1)
    ).astype(BF)
    rank = jnp.dot(hit.astype(BF), earlier, preferred_element_type=F32)
    chosen = jnp.where(rank == slot.astype(F32), hit, 0.0)
    return chosen, chosen * weight


def select_kernel(n_low, wide_count, base_ref, x_ref, rows_ref):
    tokens = 64
    meta = x_ref[0, tokens:, :].astype(F32)
    chosen, _ = hits(meta, base_ref[0], n_low, wide_count, rows_ref.shape[1])
    rows_ref[0] = jnp.dot(
        chosen.astype(BF), x_ref[0, :tokens, :], preferred_element_type=F32
    ).astype(BF)


def combine_kernel(n_low, wide_count, base_ref, x_ref, back_ref, part_ref):
    meta = x_ref[0].astype(F32)
    _, weight = hits(meta, base_ref[0], n_low, wide_count, back_ref.shape[1])
    part_ref[0] = lax.dot_general(
        weight.astype(BF), back_ref[0], (((0,), (0,)), ((), ())), preferred_element_type=F32
    ).astype(BF)


def expert_kernel(x_ref, w_ref, out_ref, total):
    step = pl.program_id(0)
    pieces, _, piece = x_ref.shape
    d_model = pieces * piece
    ff = w_ref.shape[2] // 2

    both = jnp.zeros((x_ref.shape[1], 2 * ff), F32)
    for s in range(pieces):
        both += jnp.dot(
            x_ref[s], w_ref[0, s * piece : (s + 1) * piece, :], preferred_element_type=F32
        )
    gate, up = both[:, :ff], both[:, ff:]
    hidden = (gate / (1.0 + jnp.exp(-gate)) * up).astype(BF)
    width = w_ref.shape[2]
    for n in range(d_model // width):
        at = d_model + n * ff
        term = jnp.dot(hidden, w_ref[0, at : at + ff, :], preferred_element_type=F32)

        @pl.when(step == 0)
        def _():
            total[:, n * width : (n + 1) * width] = term

        @pl.when(step > 0)
        def _():
            total[:, n * width : (n + 1) * width] += term

    @pl.when(step == pl.num_programs(0) - 1)
    def _():
        for s in range(pieces):
            out_ref[s] = total[:, s * piece : (s + 1) * piece].astype(BF)


def sum_kernel(x_ref, out_ref):
    total = x_ref[0].astype(F32)
    for i in range(1, x_ref.shape[0]):
        total += x_ref[i].astype(F32)
    out_ref[...] = total.astype(BF)


def shards(tokens, routes, route_weight, gate_weight, up_weight, down_weight):
    n_shard, n_narrow = lax.axis_size("shard"), lax.axis_size("narrow")
    n_high, n_low = lax.axis_size("high"), lax.axis_size("low")
    wide_count = n_high * n_low
    token_count, piece = tokens.shape
    top = routes.shape[1]
    d_model, ff = gate_weight.shape[1:]
    slots = n_narrow * n_low * CAP
    params = pltpu.CompilerParams(vmem_limit_bytes=VMEM)
    smem = pl.BlockSpec(memory_space=pltpu.SMEM)

    packed = jnp.concatenate(
        [
            jnp.concatenate([gate_weight[0], up_weight[0]], axis=1),
            down_weight[0]
            .reshape(ff, d_model // (2 * ff), 2 * ff)
            .transpose(1, 0, 2)
            .reshape(d_model // 2, 2 * ff),
        ],
        axis=0,
    )
    weights = lax.all_gather(packed, "shard", axis=0, tiled=False)

    meta = jnp.concatenate([routes.T.astype(BF), route_weight.T.astype(BF)], axis=0)
    meta = jnp.pad(meta, ((0, 0), (0, piece - token_count)))
    near = lax.all_gather(
        jnp.concatenate([tokens, meta], axis=0), "high", axis=0, tiled=False
    )
    base = (lax.axis_index("high") * n_low).reshape(1).astype(jnp.int32)
    full = near.shape[1]
    rows = pl.pallas_call(
        lambda *refs: select_kernel(n_low, wide_count, *refs),
        grid=(n_high,),
        in_specs=[smem, pl.BlockSpec((1, full, piece), lambda h: (h, 0, 0))],
        out_specs=pl.BlockSpec((1, slots, piece), lambda h: (h, 0, 0)),
        out_shape=jax.ShapeDtypeStruct((n_high, slots, piece), BF),
        compiler_params=params,
        name="select",
    )(base, near)
    peers = ("shard", "narrow", "low")
    arrived = lax.all_to_all(
        rows.reshape(-1, CAP, piece), peers, split_axis=0, concat_axis=0, tiled=True
    ).reshape(n_shard, slots, piece)
    out = pl.pallas_call(
        expert_kernel,
        grid=(n_shard,),
        in_specs=[
            pl.BlockSpec(arrived.shape, lambda j: (0, 0, 0)),
            pl.BlockSpec((1,) + packed.shape, lambda j: (j, 0, 0)),
        ],
        out_specs=pl.BlockSpec(arrived.shape, lambda j: (0, 0, 0)),
        out_shape=jax.ShapeDtypeStruct(arrived.shape, BF),
        scratch_shapes=[pltpu.VMEM((slots, d_model), F32)],
        compiler_params=params,
        name="expert",
    )(arrived, weights)
    back = lax.all_to_all(
        out.reshape(-1, CAP, piece), peers, split_axis=0, concat_axis=0, tiled=True
    ).reshape(n_high, slots, piece)
    part = pl.pallas_call(
        lambda *refs: combine_kernel(n_low, wide_count, *refs),
        grid=(n_high,),
        in_specs=[
            smem,
            pl.BlockSpec((1, 2 * top, piece), lambda h: (h, token_count // (2 * top), 0)),
            pl.BlockSpec((1, slots, piece), lambda h: (h, 0, 0)),
        ],
        out_specs=pl.BlockSpec((1, token_count, piece), lambda h: (h, 0, 0)),
        out_shape=jax.ShapeDtypeStruct((n_high, token_count, piece), BF),
        compiler_params=params,
        name="combine",
    )(base, near, back)
    parts = lax.all_to_all(part, "high", split_axis=0, concat_axis=0, tiled=True)
    return pl.pallas_call(
        sum_kernel,
        out_shape=jax.ShapeDtypeStruct((token_count, piece), BF),
        compiler_params=params,
        name="sum",
    )(parts)


def solution(mesh):
    sizes = dict(mesh.shape)
    split = Mesh(
        mesh.devices.reshape(
            sizes["shard"], sizes["narrow"], sizes["wide"] // LOW, LOW
        ),
        ("shard", "narrow", "high", "low"),
    )
    group = ("narrow", "high", "low")
    placed = (
        P(group, "shard"),
        P(group, None),
        P(group, None),
        P(group, None, "shard"),
        P(group, None, "shard"),
        P(group, "shard", None),
    )
    return jax.shard_map(
        shards,
        mesh=split,
        in_specs=placed,
        out_specs=P(group, "shard"),
        check_vma=False,
    )
```

time: 1150 us -> 338 us (0.29)
  the two profiles are of different devices: /device:TPU:6 before, /device:TPU:33 now
where the time goes in v1:
time: 338 us; the launch traced here: 337 us
  blocking collectives  222 us (66%)
  waiting for transfers between devices  50.9 us (15%)
  Pallas kernels  45.5 us (13%)
  between operations  13.5 us (4%)
  other arithmetic  3.59 us (1%)
    all_to_all x1, blocking collectives, shards(): lax.all_to_all(part, 'high', split_axis=0, concat_axis=0, tiled=True)  81.8 us
    all_gather x1, blocking collectives, shards(): lax.all_gather(jnp.concatenate([tokens, meta], axis=0), 'high', axis=0, t...  54.1 us
    all_gather x1, waiting for transfers between devices, shards(): weights = lax.all_gather(packed, 'shard', axis=0, tiled=False)  50.9 us
    all_to_all x1, blocking collectives, shards(): lax.all_to_all(rows.reshape(-1, CAP, piece), peers, split_axis=0, concat_...  45.8 us
    all_to_all x1, blocking collectives, shards(): lax.all_to_all(out.reshape(-1, CAP, piece), peers, split_axis=0, concat_a...  39.9 us
    pallas_call x1, Pallas kernels, shards(): pl.pallas_call(expert_kernel, grid=(n_shard,), in_specs=[pl.BlockSpec(arr...  31 us
  transfers between devices with their start and end apart: 1, of which 1 were waited for; matrix products, arithmetic and copies ran while one was open for 0% of the time, Pallas kernels for 2%

profile of v1, /device:TPU:33, one launch (start us, length us, event | category | flops | bytes accessed | tf_op | source)
XLA Modules:
  0.0 336.9 jit_solution(5542554417373483212)
XLA Ops:
  6.5 0.0 all-gather.4.cloned.1.call-start
  6.5 1.5 copy.8
  8.0 0.0 copy-start.1
  8.0 0.0 copy-start.2
  8.0 0.0 copy-start
  8.1 0.3 copy.7
  8.4 3.6 %pad_maximum_fusion = bf16[6144,256]{1,0:T(8,128)(2,1)} fusion(bf16[2048,256]{1,0:T(8,128)(2,1)S(1)} %bitcast.25, bf16[4096,128]{1,0:T(8,128)(2,1)} %bitcast.29, bf16[4096,128]{1,0:T(8,128)(2,1)} %bitcast.30), kind=kLoop, calls=%fused_computation | loop fusion | flops 9437184 | bytes 6291456 | tf_op jit(solution)/shard_map/concatenate | solution.py:104
  12.0 0.0 all-gather.4.cloned.1.call-update
  12.0 0.0 copy-done.1
  12.0 0.0 copy-done.2
  12.0 0.0 copy-done
  12.1 54.1 %all-gather = bf16[640,512]{1,0:T(8,128)(2,1)} all-gather(bf16[80,512]{1,0:T(8,128)(2,1)S(1)} %pad_maximum_fusion.1), channel_id=2, replica_groups=mesh['shard'=8,'narrow'=4,'high'=8,'low'=4] {'high'}, dimensions={0}, use_global_device_ids=true | all-gather | bytes 737280 | tf_op jit(solution)/shard_map/all_gather | solution.py:118
  66.1 6.2 %select.10 = bf16[8,128,512]{2,1,0:T(8,128)(2,1)} custom-call(s32[1]{0:T(128)} %bitcast.refs_0_, bf16[8,80,512]{2,1,0:T(8,128)(2,1)} %bitcast.20), custom_call_target="tpu_custom_call" | custom-call | tf_op jit(solution)/shard_map/select/pallas_call | solution.py:123
  72.4 45.8 %all_to_all.15 = bf16[128,8,512]{2,1,0:T(8,128)(2,1)} all-to-all(bf16[128,8,512]{2,1,0:T(8,128)(2,1)} %bitcast.23), channel_id=1, replica_groups=mesh['shard'=8,'narrow'=4,'high'=8,'low'=4] {'shard','narrow','low'}, dimensions={0} | all-to-all | bytes 2097152 | tf_op jit(solution)/shard_map/all_to_all | solution.py:133
  118.2 50.9 %all-gather.4.cloned.1.call-done = bf16[49152,256]{1,0:T(8,128)(2,1)} async-done(((bf16[6144,256]{1,0:T(8,128)(2,1)}), bf16[49152,256]{1,0:T(8,128)(2,1)}) %all-gather.4.cloned.1.call-update) | async-done | bytes 25165840 | tf_op jit(solution)/shard_map/all_gather | solution.py:114
  169.1 31.0 %expert.1 = bf16[8,128,512]{2,1,0:T(8,128)(2,1)} custom-call(bf16[8,128,512]{2,1,0:T(8,128)(2,1)} %bitcast.26, bf16[8,6144,256]{2,1,0:T(8,128)(2,1)} %bitcast.19), custom_call_target="tpu_custom_call" | custom-call | tf_op jit(solution)/shard_map/expert/pallas_call | solution.py:136
  200.1 39.9 %all_to_all.16 = bf16[128,8,512]{2,1,0:T(8,128)(2,1)} all-to-all(bf16[128,8,512]{2,1,0:T(8,128)(2,1)} %bitcast.27), channel_id=1, replica_groups=mesh['shard'=8,'narrow'=4,'high'=8,'low'=4] {'shard','narrow','low'}, dimensions={0} | all-to-all | bytes 2097152 | tf_op jit(solution)/shard_map/all_to_all | solution.py:149
  240.0 6.5 %combine.1 = bf16[8,64,512]{2,1,0:T(8,128)(2,1)} custom-call(s32[1]{0:T(128)} %bitcast.refs_0_, bf16[8,80,512]{2,1,0:T(8,128)(2,1)} %bitcast.21, bf16[8,128,512]{2,1,0:T(8,128)(2,1)} %bitcast.22), custom_call_target="tpu_custom_call" | custom-call | tf_op jit(solution)/shard_map/combine/pallas_call | solution.py:152
  246.5 81.8 %all_to_all.17.x_ref = bf16[8,64,512]{2,1,0:T(8,128)(2,1)} all-to-all(bf16[8,64,512]{2,1,0:T(8,128)(2,1)} %combine.1), channel_id=1, replica_groups=mesh['shard'=8,'narrow'=4,'high'=8,'low'=4] {'high'}, dimensions={0} | all-to-all | bytes 1048576 | tf_op jit(solution)/shard_map/all_to_all | solution.py:165
  328.4 1.7 sum.1
  (4 shorter events, 0.0 us)
Async XLA Ops:
  6.5 162.6 %all-gather.4.cloned.1.call-start = ((), (), s32[]{:S(2)}) async-start(), calls=%async_computation.3 | async-start | bytes 28311552 | tf_op jit(solution)/shard_map/all_gather | solution.py:114
  8.0 4.0 %copy-start.1 = (s32[64,8]{0,1:T(8,128)S(1)}, s32[64,8]{0,1:T(8,128)}, u32[]{:S(2)}) copy-start(s32[64,8]{0,1:T(8,128)} %param.7) | copy-start | bytes 6148
  8.0 4.0 %copy-start.2 = (f32[64,8]{0,1:T(8,128)S(1)}, f32[64,8]{0,1:T(8,128)}, u32[]{:S(2)}) copy-start(f32[64,8]{0,1:T(8,128)} %param.8) | copy-start | bytes 6148
  8.0 4.0 %copy-start = (bf16[64,512]{1,0:T(8,128)(2,1)S(1)}, bf16[64,512]{1,0:T(8,128)(2,1)}, u32[]{:S(2)}) copy-start(bf16[64,512]{1,0:T(8,128)(2,1)} %param.6) | copy-start | bytes 196612
Sparse Core Ops, SparseCore 0:
  12.1 156.9 all-gather.3

commit v2 on v1

v2 whole, which is shorter than its diff:
```python
import jax
import jax.numpy as jnp
from jax import lax
from jax.experimental import pallas as pl
from jax.experimental.pallas import tpu as pltpu
from jax.sharding import Mesh, PartitionSpec as P

BF = jnp.bfloat16
F32 = jnp.float32
CAP = 8
LOW = 4
VMEM = 56 << 20


def select_kernel(n_low, wide_count, base_ref, x_ref, rows_ref, weight_ref):
    pair, full, _ = x_ref.shape
    slots, lanes = weight_ref.shape[1:]
    tokens = lanes // pair
    top = (full - tokens) // 2
    meta = x_ref[0, tokens:, :lanes].astype(F32)
    for i in range(1, pair):
        meta += x_ref[i, tokens:, :lanes].astype(F32)
    row = lax.broadcasted_iota(jnp.int32, (slots, lanes), 0)
    lane = lax.broadcasted_iota(jnp.int32, (slots, lanes), 1)
    slot = row % CAP
    place = row // (CAP * pair)
    expert = ((place // n_low) * wide_count + place % n_low + base_ref[0]).astype(F32)
    expert = jnp.where(lane // tokens == (row // CAP) % pair, expert, -1.0)
    hit = jnp.zeros((slots, lanes), F32)
    weight = jnp.zeros((slots, lanes), F32)
    for k in range(top):
        same = meta[k : k + 1, :] == expert
        hit = jnp.where(same, 1.0, hit)
        weight = jnp.where(same, meta[top + k : top + k + 1, :], weight)
    earlier = (
        lax.broadcasted_iota(jnp.int32, (lanes, lanes), 0)
        < lax.broadcasted_iota(jnp.int32, (lanes, lanes), 1)
    ).astype(BF)
    rank = jnp.dot(hit.astype(BF), earlier, preferred_element_type=F32)
    first = rank == slot.astype(F32)
    chosen = jnp.where(first, hit, 0.0).astype(BF)
    weight_ref[0] = jnp.where(first, weight, 0.0).astype(BF)
    both = jnp.concatenate([x_ref[i, :tokens, :] for i in range(pair)], axis=0)
    rows_ref[0] = jnp.dot(chosen, both, preferred_element_type=F32).astype(BF)


def combine_kernel(weight_ref, back_ref, part_ref):
    part_ref[0] = lax.dot_general(
        weight_ref[0], back_ref[0], (((0,), (0,)), ((), ())), preferred_element_type=F32
    ).astype(BF)


def expert_kernel(
    core_ref, own_x, other_x, all_w, keep_ref, send_ref, weights, rows, hidden, total, sems
):
    n_x, n_rows, piece = own_x.shape
    d_model = rows.shape[1]
    width = weights.shape[2]
    ff = width // 2
    core = core_ref[0]
    copies = [
        pltpu.make_async_copy(all_w.at[b], weights.at[b], sems.at[b]) for b in range(n_x)
    ]
    for copy in copies:
        copy.start()
    for x in range(n_x):
        at = pl.multiple_of((2 * x + core) * piece, piece)
        rows[:, pl.ds(at, piece)] = own_x[x]
        at = pl.multiple_of((2 * x + 1 - core) * piece, piece)
        rows[:, pl.ds(at, piece)] = other_x[x]
    for b, copy in enumerate(copies):
        copy.wait()
        both = jnp.dot(rows[...], weights[b, :d_model, :], preferred_element_type=F32)
        gate, up = both[:, :ff], both[:, ff:]
        hidden[:, b * ff : (b + 1) * ff] = (gate / (1.0 + jnp.exp(-gate)) * up).astype(BF)
    for n in range(d_model // width):
        at = d_model + n * ff
        down = jnp.concatenate(
            [weights[b, at : at + ff, :] for b in range(len(copies))], axis=0
        )
        total[:, n * width : (n + 1) * width] = jnp.dot(
            hidden[...], down, preferred_element_type=F32
        ).astype(BF)
    for x in range(n_x):
        at = pl.multiple_of((2 * x + core) * piece, piece)
        keep_ref[x] = total[:, pl.ds(at, piece)]
        at = pl.multiple_of((2 * x + 1 - core) * piece, piece)
        send_ref[x] = total[:, pl.ds(at, piece)]


def shards(tokens, routes, route_weight, gate_weight, up_weight, down_weight):
    n_x, n_narrow = lax.axis_size("x"), lax.axis_size("narrow")
    n_high, n_low = lax.axis_size("high"), lax.axis_size("low")
    token_count, piece = tokens.shape
    d_model, ff = gate_weight.shape[1:]
    pair = n_high // n_x
    lanes = pair * token_count
    slots = n_narrow * n_low * pair * CAP
    params = pltpu.CompilerParams(vmem_limit_bytes=VMEM)
    smem = pl.BlockSpec(memory_space=pltpu.SMEM)
    vmem = pl.BlockSpec(memory_space=pltpu.VMEM)
    hbm = pl.BlockSpec(memory_space=pl.ANY)
    swap = [(0, 1), (1, 0)]

    own_w = jnp.concatenate(
        [
            jnp.concatenate([gate_weight[0], up_weight[0]], axis=1),
            down_weight[0]
            .reshape(ff, d_model // (2 * ff), 2 * ff)
            .transpose(1, 0, 2)
            .reshape(d_model // 2, 2 * ff),
        ],
        axis=0,
    )
    all_w = lax.all_gather(own_w, "x", axis=0, tiled=False)

    high = lax.axis_index("high")
    meta = jnp.concatenate([routes.T.astype(BF), route_weight.T.astype(BF)], axis=0)
    meta = jnp.tile(meta, (1, pair))
    mine = jnp.arange(lanes) // token_count == high % pair
    meta = jnp.where(mine[None, :], meta, jnp.zeros_like(meta))
    meta = jnp.pad(meta, ((0, 0), (0, piece - lanes)))
    near = lax.all_gather(
        jnp.concatenate([tokens, meta], axis=0), "high", axis=0, tiled=False
    )
    base = (high * n_low).reshape(1).astype(jnp.int32)
    core = lax.axis_index("core").reshape(1).astype(jnp.int32)
    full = near.shape[1]
    rows, weight = pl.pallas_call(
        lambda *refs: select_kernel(n_low, n_high * n_low, *refs),
        grid=(n_x,),
        in_specs=[smem, pl.BlockSpec((pair, full, piece), lambda h: (h, 0, 0))],
        out_specs=[
            pl.BlockSpec((1, slots, piece), lambda h: (h, 0, 0)),
            pl.BlockSpec((1, slots, lanes), lambda h: (h, 0, 0)),
        ],
        out_shape=[
            jax.ShapeDtypeStruct((n_x, slots, piece), BF),
            jax.ShapeDtypeStruct((n_x, slots, lanes), BF),
        ],
        compiler_params=params,
        name="select",
    )(base, near)
    peers = ("x", "narrow", "low")
    own_x = lax.all_to_all(
        rows.reshape(-1, pair * CAP, piece), peers, split_axis=0, concat_axis=0, tiled=True
    ).reshape(n_x, slots, piece)
    other_x = lax.ppermute(own_x, "core", swap)
    keep, send = pl.pallas_call(
        expert_kernel,
        in_specs=[smem, vmem, vmem, hbm],
        out_specs=[vmem, vmem],
        out_shape=[jax.ShapeDtypeStruct(own_x.shape, BF)] * 2,
        scratch_shapes=[
            pltpu.VMEM((n_x,) + own_w.shape, BF),
            pltpu.VMEM((slots, d_model), BF),
            pltpu.VMEM((slots, n_x * ff), BF),
            pltpu.VMEM((slots, d_model), BF),
            pltpu.SemaphoreType.DMA((n_x,)),
        ],
        compiler_params=params,
        name="expert",
    )(core, own_x, other_x, all_w)
    got = lax.ppermute(send, "core", swap)
    out = (keep.astype(F32) + got.astype(F32)).astype(BF)
    back = lax.all_to_all(
        out.reshape(-1, pair * CAP, piece), peers, split_axis=0, concat_axis=0, tiled=True
    ).reshape(n_x, slots, piece)
    part = pl.pallas_call(
        combine_kernel,
        grid=(n_x,),
        in_specs=[
            pl.BlockSpec((1, slots, lanes), lambda h: (h, 0, 0)),
            pl.BlockSpec((1, slots, piece), lambda h: (h, 0, 0)),
        ],
        out_specs=pl.BlockSpec((1, lanes, piece), lambda h: (h, 0, 0)),
        out_shape=jax.ShapeDtypeStruct((n_x, lanes, piece), BF),
        compiler_params=params,
        name="combine",
    )(weight, back)
    return lax.psum_scatter(
        part.reshape(n_high, token_count, piece), "high", scatter_dimension=0, tiled=False
    )


def solution(mesh):
    sizes = dict(mesh.shape)
    split = Mesh(
        mesh.devices.reshape(
            sizes["shard"] // 2, 2, sizes["narrow"], sizes["wide"] // LOW, LOW
        ),
        ("x", "core", "narrow", "high", "low"),
    )
    group, shard = ("narrow", "high", "low"), ("x", "core")
    placed = (
        P(group, shard),
        P(group, None),
        P(group, None),
        P(group, None, shard),
        P(group, None, shard),
        P(group, shard, None),
    )
    return jax.shard_map(
        shards,
        mesh=split,
        in_specs=placed,
        out_specs=P(group, shard),
        check_vma=False,
    )
```

time: 338 us -> 305 us (0.902)
  the two profiles are of different devices: /device:TPU:33 before, /device:TPU:6 now
where the time goes in v2:
time: 305 us; the launch traced here: 304 us
  blocking collectives  133 us (44%)
  waiting for transfers between devices  129 us (42%)
  Pallas kernels  18.7 us (6%)
  between operations  13.5 us (4%)
  starting transfers between devices  3.87 us (1%)
  other arithmetic  3.5 us (1%)
    reduce_scatter x1, waiting for transfers between devices, shards(): lax.psum_scatter(part.reshape(n_high, token_count, piece), 'high', scatte...  71.6 us
    all_gather x1, blocking collectives, shards(): lax.all_gather(jnp.concatenate([tokens, meta], axis=0), 'high', axis=0, t...  62.3 us
    all_gather x1, waiting for transfers between devices, shards(): all_w = lax.all_gather(own_w, 'x', axis=0, tiled=False)  51.5 us
    all_to_all x1, blocking collectives, shards(): lax.all_to_all(out.reshape(-1, pair * CAP, piece), peers, split_axis=0, c...  39.4 us
    all_to_all x1, blocking collectives, shards(): lax.all_to_all(rows.reshape(-1, pair * CAP, piece), peers, split_axis=0,...  30.9 us
    pallas_call x1, Pallas kernels, shards(): pl.pallas_call(expert_kernel, in_specs=[smem, vmem, vmem, hbm], out_specs...  11 us
  transfers between devices with their start and end apart: 4, of which 4 were waited for; matrix products, arithmetic and copies ran while one was open for 0% of the time, Pallas kernels for 1%

profile of v2, /device:TPU:6, one launch (start us, length us, event | category | flops | bytes accessed | tf_op | source)
XLA Modules:
  0.0 303.5 jit_solution(7814356672790515011)
XLA Ops:
  6.5 0.0 copy-start.2
  6.5 0.0 copy-start.3
  6.5 0.0 all-gather.4.cloned.1.call-start
  6.5 1.6 copy.8
  8.2 0.3 copy.7
  8.5 0.0 copy-done.2
  8.5 0.0 copy-done.3
  8.5 1.9 pad_maximum_fusion
  10.5 0.0 copy-start.5
  10.5 0.0 copy-start.6
  10.5 0.0 all-gather.4.cloned.1.call-update
  10.5 0.0 reduce-scatter.2.cloned.1.call-start
  10.6 0.6 copy-done.5
  11.2 0.0 copy-done.6
  11.2 0.1 tile.10
  11.3 0.0 copy-done.4
  11.3 62.3 %all-gather = bf16[640,512]{1,0:T(8,128)(2,1)} all-gather(bf16[80,512]{1,0:T(8,128)(2,1)S(1)} %fusion.1), channel_id=2, replica_groups=mesh['x'=4,'core'=2,'narrow'=4,'high'=8,'low'=4] {'high'}, dimensions={0}, use_global_device_ids=true | all-gather | bytes 737280 | tf_op jit(solution)/shard_map/all_gather | solution.py:123
  73.6 4.0 %select.16 = (bf16[4,256,512]{2,1,0:T(8,128)(2,1)}, bf16[4,256,128]{2,1,0:T(8,128)(2,1)}) custom-call(s32[1]{0:T(128)} %bitcast.refs_0_, bf16[8,80,512]{2,1,0:T(8,128)(2,1)} %bitcast.29), custom_call_target="tpu_custom_call" | custom-call | tf_op jit(solution)/shard_map/select/pallas_call | solution.py:129
  77.7 30.9 %all_to_all.10 = bf16[64,16,512]{2,1,0:T(8,128)(2,1)S(1)} all-to-all(bf16[64,16,512]{2,1,0:T(8,128)(2,1)} %bitcast.32), channel_id=1, replica_groups=mesh['x'=4,'core'=2,'narrow'=4,'high'=8,'low'=4] {'x','narrow','low'}, dimensions={0} | all-to-all | bytes 2097152 | tf_op jit(solution)/shard_map/all_to_all | solution.py:145
  108.6 1.9 collective-permute-start
  110.5 2.6 collective-permute-done.other_x
  113.2 51.5 %all-gather.4.cloned.1.call-done = bf16[24576,256]{1,0:T(8,128)(2,1)} async-done(((bf16[6144,256]{1,0:T(8,128)(2,1)}), bf16[24576,256]{1,0:T(8,128)(2,1)}) %all-gather.4.cloned.1.call-update) | async-done | bytes 12582928 | tf_op jit(solution)/shard_map/all_gather | solution.py:115
  164.6 0.0 copy-done
  164.7 0.0 copy-done.1
  164.7 11.0 %expert.1 = (bf16[4,256,512]{2,1,0:T(8,128)(2,1)}, bf16[4,256,512]{2,1,0:T(8,128)(2,1)}) custom-call(s32[1]{0:T(128)} %bitcast.4.core_ref, bf16[4,256,512]{2,1,0:T(8,128)(2,1)} %bitcast.24, bf16[4,256,512]{2,1,0:T(8,128)(2,1)} %copy-done.1, bf16[4,6144,256]{2,1,0:T(8,128)(2,1)} %bitcast.22), custom_call_target="tpu_custom_call" | custom-call | tf_op jit(solution)/shard_map/expert/pallas_call | solution.py:149
  175.6 1.9 collective-permute-start.1
  177.5 2.8 collective-permute-done.1
  180.4 1.5 add_convert_fusion
  181.9 39.4 %all_to_all.11 = bf16[64,16,512]{2,1,0:T(8,128)(2,1)} all-to-all(bf16[64,16,512]{2,1,0:T(8,128)(2,1)S(1)} %bitcast.25), channel_id=1, replica_groups=mesh['x'=4,'core'=2,'narrow'=4,'high'=8,'low'=4] {'x','narrow','low'}, dimensions={0} | all-to-all | bytes 2097152 | tf_op jit(solution)/shard_map/all_to_all | solution.py:166
  221.3 3.7 %combine.1 = bf16[4,128,512]{2,1,0:T(8,128)(2,1)} custom-call(bf16[4,256,128]{2,1,0:T(8,128)(2,1)} %get-tuple-element.9.weight_ref, bf16[4,256,512]{2,1,0:T(8,128)(2,1)} %bitcast.26), custom_call_target="tpu_custom_call" | custom-call | tf_op jit(solution)/shard_map/combine/pallas_call | solution.py:169
  225.0 0.0 reduce-scatter.2.cloned.1.call-update
  225.1 71.6 %reduce-scatter.2.cloned.1.call-done = bf16[1,64,512]{2,1,0:T(8,128)(2,1)} async-done(((bf16[8,64,512]{2,1,0:T(8,128)(2,1)}), bf16[1,64,512]{2,1,0:T(8,128)(2,1)}) %reduce-scatter.2.cloned.1.call-update) | async-done | bytes 65552 | tf_op jit(solution)/shard_map/reduce_scatter | solution.py:181
  (10 shorter events, 0.1 us)
Async XLA Ops:
  6.5 2.0 copy-start.2
  6.5 2.0 copy-start.3
  6.5 158.1 %all-gather.4.cloned.1.call-start = ((), (), s32[]{:S(2)}) async-start(), calls=%async_computation.4 | async-start | bytes 15728640 | tf_op jit(solution)/shard_map/all_gather | solution.py:115
  10.5 0.7 copy-start.5
  10.5 0.7 copy-start.6
  10.5 0.9 copy-start.4
  10.5 286.2 %reduce-scatter.2.cloned.1.call-start = ((), (), s32[]{:S(2)}) async-start(), calls=%async_computation.3 | async-start | bytes 589824 | tf_op jit(solution)/shard_map/reduce_scatter | solution.py:181
  108.6 56.0 %copy-start = (bf16[64,16,512]{2,1,0:T(8,128)(2,1)}, bf16[64,16,512]{2,1,0:T(8,128)(2,1)S(1)}, u32[]{:S(2)}) copy-start(bf16[64,16,512]{2,1,0:T(8,128)(2,1)S(1)} %all_to_all.10) | copy-start | bytes 3145732
  108.6 4.5 %collective-permute-start = (bf16[4,256,512]{2,1,0:T(8,128)(2,1)S(1)}, bf16[4,256,512]{2,1,0:T(8,128)(2,1)S(1)}, u32[]{:S(2)}, u32[]{:S(2)}) collective-permute-start(bf16[4,256,512]{2,1,0:T(8,128)(2,1)S(1)} %bitcast.23), channel_id=1, source_target_pairs={{0,128},{128,0},{1,129},{129,1},{2,130},{130,2},{3,131},{131,3},{4... | collective-permute-start | bytes 3145736 | tf_op jit(solution)/shard_map/ppermute | solution.py:148
  113.2 51.5 %copy-start.1 = (bf16[4,256,512]{2,1,0:T(8,128)(2,1)}, bf16[4,256,512]{2,1,0:T(8,128)(2,1)S(1)}, u32[]{:S(2)}) copy-start(bf16[4,256,512]{2,1,0:T(8,128)(2,1)S(1)} %collective-permute-done.other_x) | copy-start | bytes 3145732
  175.6 4.8 %collective-permute-start.1 = (bf16[4,256,512]{2,1,0:T(8,128)(2,1)}, bf16[4,256,512]{2,1,0:T(8,128)(2,1)S(1)}, u32[]{:S(2)}, u32[]{:S(2)}) collective-permute-start(bf16[4,256,512]{2,1,0:T(8,128)(2,1)} %get-tuple-element.12), channel_id=1, source_target_pairs={{0,128},{128,0},{1,129},{129,1},{2,130},{130,2},{3,131},{131,3},{4... | collective-permute-start | bytes 3145736 | tf_op jit(solution)/shard_map/ppermute | solution.py:164
Sparse Core Ops, SparseCore 0:
  10.6 153.9 all-gather.3
  225.2 71.4 reduce-scatter.1

commit v3 on v2

--- a/solution.py
+++ b/solution.py
@@ -51,15 +51,20 @@
 
 
 def expert_kernel(
-    core_ref, own_x, other_x, all_w, keep_ref, send_ref, weights, rows, hidden, total, sems
+    core_ref, own_x, other_x, *refs
 ):
+    parts, (keep_ref, send_ref, weights, rows, hidden, total, sems) = refs[:-7], refs[-7:]
     n_x, n_rows, piece = own_x.shape
     d_model = rows.shape[1]
     width = weights.shape[2]
     ff = width // 2
     core = core_ref[0]
+    half = parts[0].shape[0]
     copies = [
-        pltpu.make_async_copy(all_w.at[b], weights.at[b], sems.at[b]) for b in range(n_x)
+        pltpu.make_async_copy(
+            part, weights.at[i // 2, (i % 2) * half : (i % 2 + 1) * half], sems.at[i]
+        )
+        for i, part in enumerate(parts)
     ]
     for copy in copies:
         copy.start()
@@ -68,15 +73,16 @@
         rows[:, pl.ds(at, piece)] = own_x[x]
         at = pl.multiple_of((2 * x + 1 - core) * piece, piece)
         rows[:, pl.ds(at, piece)] = other_x[x]
-    for b, copy in enumerate(copies):
-        copy.wait()
+    for b in range(n_x):
+        copies[2 * b].wait()
+        copies[2 * b + 1].wait()
         both = jnp.dot(rows[...], weights[b, :d_model, :], preferred_element_type=F32)
         gate, up = both[:, :ff], both[:, ff:]
         hidden[:, b * ff : (b + 1) * ff] = (gate / (1.0 + jnp.exp(-gate)) * up).astype(BF)
     for n in range(d_model // width):
         at = d_model + n * ff
         down = jnp.concatenate(
-            [weights[b, at : at + ff, :] for b in range(len(copies))], axis=0
+            [weights[b, at : at + ff, :] for b in range(n_x)], axis=0
         )
         total[:, n * width : (n + 1) * width] = jnp.dot(
             hidden[...], down, preferred_element_type=F32
@@ -101,6 +107,8 @@
     vmem = pl.BlockSpec(memory_space=pltpu.VMEM)
     hbm = pl.BlockSpec(memory_space=pl.ANY)
     swap = [(0, 1), (1, 0)]
+    up_x = [(i, (i + 1) % n_x) for i in range(n_x)]
+    down_x = [(i, (i - 1) % n_x) for i in range(n_x)]
 
     own_w = jnp.concatenate(
         [
@@ -112,7 +120,12 @@
         ],
         axis=0,
     )
-    all_w = lax.all_gather(own_w, "x", axis=0, tiled=False)
+    half = own_w.shape[0] // 2
+    own_a, own_b = own_w[:half], own_w[half:]
+    prev_a = lax.ppermute(own_a, "x", up_x)
+    next_b = lax.ppermute(own_b, "x", down_x)
+    prev_b = lax.ppermute(own_b, "x", up_x)
+    next_a = lax.ppermute(own_a, "x", down_x)
 
     high = lax.axis_index("high")
     meta = jnp.concatenate([routes.T.astype(BF), route_weight.T.astype(BF)], axis=0)
@@ -123,6 +136,9 @@
     near = lax.all_gather(
         jnp.concatenate([tokens, meta], axis=0), "high", axis=0, tiled=False
     )
+    near, prev_a, next_b = lax.optimization_barrier((near, prev_a, next_b))
+    far_a = lax.ppermute(prev_a, "x", up_x)
+    far_b = lax.ppermute(next_b, "x", down_x)
     base = (high * n_low).reshape(1).astype(jnp.int32)
     core = lax.axis_index("core").reshape(1).astype(jnp.int32)
     full = near.shape[1]
@@ -141,6 +157,7 @@
         compiler_params=params,
         name="select",
     )(base, near)
+    rows, prev_b, next_a = lax.optimization_barrier((rows, prev_b, next_a))
     peers = ("x", "narrow", "low")
     own_x = lax.all_to_all(
         rows.reshape(-1, pair * CAP, piece), peers, split_axis=0, concat_axis=0, tiled=True
@@ -148,7 +165,7 @@
     other_x = lax.ppermute(own_x, "core", swap)
     keep, send = pl.pallas_call(
         expert_kernel,
-        in_specs=[smem, vmem, vmem, hbm],
+        in_specs=[smem, vmem, vmem] + [hbm] * (2 * n_x),
         out_specs=[vmem, vmem],
         out_shape=[jax.ShapeDtypeStruct(own_x.shape, BF)] * 2,
         scratch_shapes=[
@@ -156,11 +173,11 @@
             pltpu.VMEM((slots, d_model), BF),
             pltpu.VMEM((slots, n_x * ff), BF),
             pltpu.VMEM((slots, d_model), BF),
-            pltpu.SemaphoreType.DMA((n_x,)),
+            pltpu.SemaphoreType.DMA((2 * n_x,)),
         ],
         compiler_params=params,
         name="expert",
-    )(core, own_x, other_x, all_w)
+    )(core, own_x, other_x, own_a, own_b, prev_a, prev_b, next_a, next_b, far_a, far_b)
     got = lax.ppermute(send, "core", swap)
     out = (keep.astype(F32) + got.astype(F32)).astype(BF)
     back = lax.all_to_all(

time: 305 us -> 288 us (0.944)
  blocking collectives: 133 us -> 87.8 us
  starting transfers between devices: 3.87 us -> 42.9 us
  waiting for transfers between devices: 129 us -> 117 us
    all_gather x1 -> x0, waiting for transfers between devices: 51.5 us -> none  [shards(): all_w = lax.all_gather(own_w, 'x', axis=0, tiled=False)]
    all_to_all x1 -> x0, blocking collectives: 30.9 us -> none  [shards(): lax.all_to_all(rows.reshape(-1, pair * CAP, piece), peers, split_axis=0,...]
    ppermute x0 -> x6, starting transfers between devices: none -> 28.6 us  [the longest x1 14.2 us: shards(): prev_a = lax.ppermute(own_a, 'x', up_x)]
    all_to_all x0 -> x1, waiting for transfers between devices: none -> 20.2 us  [shards(): lax.all_to_all(rows.reshape(-1, pair * CAP, piece), peers, split_axis=0,...]
    ppermute x0 -> x6, waiting for transfers between devices: none -> 17.2 us  [the longest x1 17 us: shards(): far_a = lax.ppermute(prev_a, 'x', up_x)]
    all_gather x1, blocking collectives: 62.3 us -> 50 us  [shards(): lax.all_gather(jnp.concatenate([tokens, meta], axis=0), 'high', axis=0, t...]
    all_to_all x0 -> x1, starting transfers between devices: none -> 10.4 us  [shards(): lax.all_to_all(rows.reshape(-1, pair * CAP, piece), peers, split_axis=0,...]
    reduce_scatter x1, waiting for transfers between devices: 71.6 us -> 77 us  [shards(): lax.psum_scatter(part.reshape(n_high, token_count, piece), 'high', scatte...]
  transfers between devices with their start and end apart: 4 -> 10, of which waited for: 4 -> 5; matrix products, arithmetic and copies ran while one was open for 0% -> 0% of each run, Pallas kernels for 1% -> 1%
where the time goes in v3:
time: 288 us; the launch traced here: 287 us
  waiting for transfers between devices  117 us (41%)
  blocking collectives  87.8 us (30%)
  starting transfers between devices  42.9 us (15%)
  Pallas kernels  18.7 us (6%)
  between operations  13.6 us (5%)
  local copies, waits for them, and re-layouts  4.57 us (2%)
    reduce_scatter x1, waiting for transfers between devices, shards(): lax.psum_scatter(part.reshape(n_high, token_count, piece), 'high', scatte...  77 us
    all_gather x1, blocking collectives, shards(): lax.all_gather(jnp.concatenate([tokens, meta], axis=0), 'high', axis=0, t...  50 us
    all_to_all x1, blocking collectives, shards(): lax.all_to_all(out.reshape(-1, pair * CAP, piece), peers, split_axis=0, c...  37.8 us
    all_to_all x1, waiting for transfers between devices, shards(): lax.all_to_all(rows.reshape(-1, pair * CAP, piece), peers, split_axis=0,...  20.2 us
    ppermute x1, waiting for transfers between devices, shards(): far_a = lax.ppermute(prev_a, 'x', up_x)  17 us
    ppermute x1, starting transfers between devices, shards(): prev_a = lax.ppermute(own_a, 'x', up_x)  14.2 us
    pallas_call x1, Pallas kernels, shards(): pl.pallas_call(expert_kernel, in_specs=[smem, vmem, vmem] + [hbm] * (2 *...  11 us
    all_to_all x1, starting transfers between devices, shards(): lax.all_to_all(rows.reshape(-1, pair * CAP, piece), peers, split_axis=0,...  10.4 us
  transfers between devices with their start and end apart: 10, of which 5 were waited for; matrix products, arithmetic and copies ran while one was open for 0% of the time, Pallas kernels for 1%

profile of v3, /device:TPU:6, one launch (start us, length us, event | category | flops | bytes accessed | tf_op | source)
XLA Modules:
  0.0 286.8 jit_solution(8629231948239267569)
XLA Ops:
  6.5 1.5 copy.8
  8.0 0.0 copy-start.4
  8.0 0.0 copy-start.5
  8.0 0.3 copy.7
  8.4 0.9 copy-done.4
  9.2 0.3 copy-done.5
  9.6 0.3 pad_maximum_fusion
  9.9 2.7 collective-permute-start.1
  12.6 14.2 %collective-permute-start = (bf16[3072,256]{1,0:T(8,128)(2,1)S(1)}, bf16[3072,256]{1,0:T(8,128)(2,1)}, u32[]{:S(2)}, u32[]{:S(2)}) collective-permute-start(bf16[3072,256]{1,0:T(8,128)(2,1)S(1)} %get-tuple-element.26.refs_0_), channel_id=1, source_target_pairs={{0,256},{256,512},{512,768},{768,0},{1,257},{257,513},{513,769},{7... | collective-permute-start | bytes 4718600 | tf_op jit(solution)/shard_map/ppermute | solution.py:125
  26.9 3.9 %collective-permute-start.2 = (bf16[3072,256]{1,0:T(8,128)(2,1)S(1)}, bf16[3072,256]{1,0:T(8,128)(2,1)}, u32[]{:S(2)}, u32[]{:S(2)}) collective-permute-start(bf16[3072,256]{1,0:T(8,128)(2,1)S(1)} %get-tuple-element.25.refs_1_), channel_id=1, source_target_pairs={{0,256},{256,512},{512,768},{768,0},{1,257},{257,513},{513,769},{7... | collective-permute-start | bytes 4718600 | tf_op jit(solution)/shard_map/ppermute | solution.py:127
  30.8 1.9 collective-permute-start.3
  32.8 0.1 tile.10
  32.9 50.0 %all-gather = bf16[640,512]{1,0:T(8,128)(2,1)} all-gather(bf16[80,512]{1,0:T(8,128)(2,1)S(1)} %fusion.1), channel_id=2, replica_groups=mesh['x'=4,'core'=2,'narrow'=4,'high'=8,'low'=4] {'high'}, dimensions={0}, use_global_device_ids=true | all-gather | bytes 737280 | tf_op jit(solution)/shard_map/all_gather | solution.py:136
  82.9 4.0 %select.16 = (bf16[4,256,512]{2,1,0:T(8,128)(2,1)}, bf16[4,256,128]{2,1,0:T(8,128)(2,1)}) custom-call(s32[1]{0:T(128)} %bitcast.refs_0_, bf16[8,80,512]{2,1,0:T(8,128)(2,1)} %bitcast.25), custom_call_target="tpu_custom_call" | custom-call | tf_op jit(solution)/shard_map/select/pallas_call | solution.py:145
  87.0 10.4 %all-to-all-start = ((bf16[64,16,512]{2,1,0:T(8,128)(2,1)}), bf16[64,16,512]{2,1,0:T(8,128)(2,1)}, u32[]{:S(2)}, u32[]{:S(2)}) async-start(bf16[64,16,512]{2,1,0:T(8,128)(2,1)} %bitcast.28), calls=%async_computation | async-start | bytes 2097152 | tf_op jit(solution)/shard_map/all_to_all | solution.py:162
  97.3 0.0 reduce-scatter.2.cloned.1.call-start
  97.4 2.2 collective-permute-start.5
  99.6 3.6 %collective-permute-start.6 = (bf16[3072,256]{1,0:T(8,128)(2,1)}, bf16[3072,256]{1,0:T(8,128)(2,1)S(1)}, u32[]{:S(2)}, u32[]{:S(2)}) collective-permute-start(bf16[3072,256]{1,0:T(8,128)(2,1)} %collective-permute-done.1.refs_5_), channel_id=1, source_target_pairs={{0,768},{256,0},{512,256},{768,512},{1,769},{257,1},{513,257},{769... | collective-permute-start | bytes 4718600 | tf_op jit(solution)/shard_map/ppermute | solution.py:141
  103.2 20.2 %all-to-all-done = bf16[64,16,512]{2,1,0:T(8,128)(2,1)} async-done(((bf16[64,16,512]{2,1,0:T(8,128)(2,1)}), bf16[64,16,512]{2,1,0:T(8,128)(2,1)}, u32[]{:S(2)}, u32[]{:S(2)}) %all-to-all-start) | async-done | bytes 1048608 | tf_op jit(solution)/shard_map/all_to_all | solution.py:162
  123.4 1.9 collective-permute-start.4
  125.3 17.0 %collective-permute-done.5.refs_6_ = bf16[3072,256]{1,0:T(8,128)(2,1)S(1)} collective-permute-done((bf16[3072,256]{1,0:T(8,128)(2,1)}, bf16[3072,256]{1,0:T(8,128)(2,1)S(1)}, u32[]{:S(2)}, u32[]{:S(2)}) %collective-permute-start.5) | collective-permute-done | bytes 1572896 | tf_op jit(solution)/shard_map/ppermute | solution.py:140
  142.4 0.2 collective-permute-done.6.refs_7_
  142.6 0.9 copy-done.2
  143.5 0.5 copy-done.3
  144.0 11.0 %expert.1 = (bf16[4,256,512]{2,1,0:T(8,128)(2,1)}, bf16[4,256,512]{2,1,0:T(8,128)(2,1)}) custom-call(s32[1]{0:T(128)} %bitcast.8.core_ref, bf16[4,256,512]{2,1,0:T(8,128)(2,1)} %bitcast.10.own_x, bf16[4,256,512]{2,1,0:T(8,128)(2,1)} %collective-permute-done.4.other_x, bf16[3072,256]{1,0:T(8,128)(2,1)} %copy-done.1, bf16[3072,256]{1,0:T(8,128)(2,1)} %copy-done, ...), custom_call_target="tpu_custom_call" | custom-call | tf_op jit(solution)/shard_map/expert/pallas_call | solution.py:166
  155.0 1.9 collective-permute-start.7
  156.9 2.8 collective-permute-done.7
  159.8 1.5 add_convert_fusion
  161.3 37.8 %all_to_all.10 = bf16[64,16,512]{2,1,0:T(8,128)(2,1)} all-to-all(bf16[64,16,512]{2,1,0:T(8,128)(2,1)S(1)} %bitcast.21), channel_id=1, replica_groups=mesh['x'=4,'core'=2,'narrow'=4,'high'=8,'low'=4] {'x','narrow','low'}, dimensions={0} | all-to-all | bytes 2097152 | tf_op jit(solution)/shard_map/all_to_all | solution.py:183
  199.1 3.7 %combine.1 = bf16[4,128,512]{2,1,0:T(8,128)(2,1)} custom-call(bf16[4,256,128]{2,1,0:T(8,128)(2,1)} %get-tuple-element.16.weight_ref, bf16[4,256,512]{2,1,0:T(8,128)(2,1)} %bitcast.22), custom_call_target="tpu_custom_call" | custom-call | tf_op jit(solution)/shard_map/combine/pallas_call | solution.py:186
  202.9 0.0 reduce-scatter.2.cloned.1.call-update
  202.9 77.0 %reduce-scatter.2.cloned.1.call-done = bf16[1,64,512]{2,1,0:T(8,128)(2,1)} async-done(((bf16[8,64,512]{2,1,0:T(8,128)(2,1)}), bf16[1,64,512]{2,1,0:T(8,128)(2,1)}) %reduce-scatter.2.cloned.1.call-update) | async-done | bytes 65552 | tf_op jit(solution)/shard_map/reduce_scatter | solution.py:198
  (24 shorter events, 0.1 us)
Async XLA Ops:
  8.0 1.2 copy-start.4
  8.0 1.5 copy-start.5
  9.6 23.2 %copy-start.7 = (s32[64,8]{0,1:T(8,128)S(1)}, s32[64,8]{0,1:T(8,128)}, u32[]{:S(2)}) copy-start(s32[64,8]{0,1:T(8,128)} %param.7) | copy-start | bytes 6148
  9.6 23.2 %copy-start.8 = (f32[64,8]{0,1:T(8,128)S(1)}, f32[64,8]{0,1:T(8,128)}, u32[]{:S(2)}) copy-start(f32[64,8]{0,1:T(8,128)} %param.8) | copy-start | bytes 6148
  9.6 23.3 %copy-start.6 = (bf16[64,512]{1,0:T(8,128)(2,1)S(1)}, bf16[64,512]{1,0:T(8,128)(2,1)}, u32[]{:S(2)}) copy-start(bf16[64,512]{1,0:T(8,128)(2,1)} %param.6) | copy-start | bytes 196612
  9.9 77.1 %copy-start = (bf16[3072,256]{1,0:T(8,128)(2,1)}, bf16[3072,256]{1,0:T(8,128)(2,1)S(1)}, u32[]{:S(2)}) copy-start(bf16[3072,256]{1,0:T(8,128)(2,1)S(1)} %get-tuple-element.25.refs_1_) | copy-start | bytes 4718596
  9.9 77.1 %copy-start.1 = (bf16[3072,256]{1,0:T(8,128)(2,1)}, bf16[3072,256]{1,0:T(8,128)(2,1)S(1)}, u32[]{:S(2)}) copy-start(bf16[3072,256]{1,0:T(8,128)(2,1)S(1)} %get-tuple-element.26.refs_0_) | copy-start | bytes 4718596
  9.9 73.0 %collective-permute-start.1 = (bf16[3072,256]{1,0:T(8,128)(2,1)S(1)}, bf16[3072,256]{1,0:T(8,128)(2,1)}, u32[]{:S(2)}, u32[]{:S(2)}) collective-permute-start(bf16[3072,256]{1,0:T(8,128)(2,1)S(1)} %get-tuple-element.25.refs_1_), channel_id=1, source_target_pairs={{0,768},{256,0},{512,256},{768,512},{1,769},{257,1},{513,257},{769... | collective-permute-start | bytes 4718600 | tf_op jit(solution)/shard_map/ppermute | solution.py:126
  12.6 70.3 %collective-permute-start = (bf16[3072,256]{1,0:T(8,128)(2,1)S(1)}, bf16[3072,256]{1,0:T(8,128)(2,1)}, u32[]{:S(2)}, u32[]{:S(2)}) collective-permute-start(bf16[3072,256]{1,0:T(8,128)(2,1)S(1)} %get-tuple-element.26.refs_0_), channel_id=1, source_target_pairs={{0,256},{256,512},{512,768},{768,0},{1,257},{257,513},{513,769},{7... | collective-permute-start | bytes 4718600 | tf_op jit(solution)/shard_map/ppermute | solution.py:125
  26.9 60.1 %collective-permute-start.2 = (bf16[3072,256]{1,0:T(8,128)(2,1)S(1)}, bf16[3072,256]{1,0:T(8,128)(2,1)}, u32[]{:S(2)}, u32[]{:S(2)}) collective-permute-start(bf16[3072,256]{1,0:T(8,128)(2,1)S(1)} %get-tuple-element.25.refs_1_), channel_id=1, source_target_pairs={{0,256},{256,512},{512,768},{768,0},{1,257},{257,513},{513,769},{7... | collective-permute-start | bytes 4718600 | tf_op jit(solution)/shard_map/ppermute | solution.py:127
  30.8 56.1 %collective-permute-start.3 = (bf16[3072,256]{1,0:T(8,128)(2,1)S(1)}, bf16[3072,256]{1,0:T(8,128)(2,1)}, u32[]{:S(2)}, u32[]{:S(2)}) collective-permute-start(bf16[3072,256]{1,0:T(8,128)(2,1)S(1)} %get-tuple-element.26.refs_0_), channel_id=1, source_target_pairs={{0,768},{256,0},{512,256},{768,512},{1,769},{257,1},{513,257},{769... | collective-permute-start | bytes 4718600 | tf_op jit(solution)/shard_map/ppermute | solution.py:128
  87.0 36.4 %all-to-all-start = ((bf16[64,16,512]{2,1,0:T(8,128)(2,1)}), bf16[64,16,512]{2,1,0:T(8,128)(2,1)}, u32[]{:S(2)}, u32[]{:S(2)}) async-start(bf16[64,16,512]{2,1,0:T(8,128)(2,1)} %bitcast.28), calls=%async_computation | async-start | bytes 2097152 | tf_op jit(solution)/shard_map/all_to_all | solution.py:162
  97.3 182.6 %reduce-scatter.2.cloned.1.call-start = ((), (), s32[]{:S(2)}) async-start(), calls=%async_computation.3 | async-start | bytes 589824 | tf_op jit(solution)/shard_map/reduce_scatter | solution.py:198
  97.4 45.0 %collective-permute-start.5 = (bf16[3072,256]{1,0:T(8,128)(2,1)}, bf16[3072,256]{1,0:T(8,128)(2,1)S(1)}, u32[]{:S(2)}, u32[]{:S(2)}) collective-permute-start(bf16[3072,256]{1,0:T(8,128)(2,1)} %collective-permute-done.refs_2_), channel_id=1, source_target_pairs={{0,256},{256,512},{512,768},{768,0},{1,257},{257,513},{513,769},{7... | collective-permute-start | bytes 4718600 | tf_op jit(solution)/shard_map/ppermute | solution.py:140
  99.6 42.9 %collective-permute-start.6 = (bf16[3072,256]{1,0:T(8,128)(2,1)}, bf16[3072,256]{1,0:T(8,128)(2,1)S(1)}, u32[]{:S(2)}, u32[]{:S(2)}) collective-permute-start(bf16[3072,256]{1,0:T(8,128)(2,1)} %collective-permute-done.1.refs_5_), channel_id=1, source_target_pairs={{0,768},{256,0},{512,256},{768,512},{1,769},{257,1},{513,257},{769... | collective-permute-start | bytes 4718600 | tf_op jit(solution)/shard_map/ppermute | solution.py:141
  123.4 19.2 %collective-permute-start.4 = (bf16[4,256,512]{2,1,0:T(8,128)(2,1)}, bf16[4,256,512]{2,1,0:T(8,128)(2,1)}, u32[]{:S(2)}, u32[]{:S(2)}) collective-permute-start(bf16[4,256,512]{2,1,0:T(8,128)(2,1)} %bitcast.10.own_x), channel_id=1, source_target_pairs={{0,128},{128,0},{1,129},{129,1},{2,130},{130,2},{3,131},{131,3},{4... | collective-permute-start | bytes 3145736 | tf_op jit(solution)/shard_map/ppermute | solution.py:165
  142.4 1.1 copy-start.2
  142.6 1.5 copy-start.3
  155.0 4.8 %collective-permute-start.7 = (bf16[4,256,512]{2,1,0:T(8,128)(2,1)}, bf16[4,256,512]{2,1,0:T(8,128)(2,1)S(1)}, u32[]{:S(2)}, u32[]{:S(2)}) collective-permute-start(bf16[4,256,512]{2,1,0:T(8,128)(2,1)} %get-tuple-element.24), channel_id=1, source_target_pairs={{0,128},{128,0},{1,129},{129,1},{2,130},{130,2},{3,131},{131,3},{4... | collective-permute-start | bytes 3145736 | tf_op jit(solution)/shard_map/ppermute | solution.py:181
Sparse Core Ops, SparseCore 0:
  203.0 76.8 reduce-scatter.1

commit v4 on v3

--- a/solution.py
+++ b/solution.py
@@ -195,9 +195,24 @@
         compiler_params=params,
         name="combine",
     )(weight, back)
-    return lax.psum_scatter(
-        part.reshape(n_high, token_count, piece), "high", scatter_dimension=0, tiled=False
-    )
+    part = part.reshape(n_high, token_count, piece)
+    up_z = [(i, (i + 1) % n_high) for i in range(n_high)]
+    down_z = [(i, (i - 1) % n_high) for i in range(n_high)]
+
+    def mine_for(step):
+        block = lax.rem(high + step, n_high)
+        return lax.dynamic_slice_in_dim(part, block, 1, 0)[0].astype(F32)
+
+    reach = n_high // 2
+    rising = lax.ppermute(mine_for(reach).astype(BF), "high", up_z)
+    falling = lax.ppermute(mine_for(reach + 1).astype(BF), "high", down_z)
+    for step in range(1, reach):
+        rising = (rising.astype(F32) + mine_for(reach - step)).astype(BF)
+        rising = lax.ppermute(rising, "high", up_z)
+        if step < reach - 1:
+            falling = (falling.astype(F32) + mine_for(reach + 1 + step)).astype(BF)
+            falling = lax.ppermute(falling, "high", down_z)
+    return (mine_for(0) + rising.astype(F32) + falling.astype(F32)).astype(BF)
 
 
 def solution(mesh):

time: 288 us -> 271 us (0.941)
  the two profiles are of different devices: /device:TPU:6 before, /device:TPU:8 now
where the time goes in v4:
time: 271 us; the launch traced here: 270 us
  waiting for transfers between devices  94.5 us (35%)
  starting transfers between devices  81.6 us (30%)
  blocking collectives  61 us (23%)
  Pallas kernels  18.8 us (7%)
  other arithmetic  7.01 us (3%)
  local copies, waits for them, and re-layouts  6.64 us (2%)
    all_gather x1, blocking collectives, shards(): lax.all_gather(jnp.concatenate([tokens, meta], axis=0), 'high', axis=0, t...  61 us
    all_to_all x1, waiting for transfers between devices, shards(): lax.all_to_all(out.reshape(-1, pair * CAP, piece), peers, split_axis=0, c...  28.8 us
    all_to_all x1, waiting for transfers between devices, shards(): lax.all_to_all(rows.reshape(-1, pair * CAP, piece), peers, split_axis=0,...  20.2 us
    ppermute x1, waiting for transfers between devices, shards(): far_a = lax.ppermute(prev_a, 'x', up_x)  17.8 us
    ppermute x3, waiting for transfers between devices, shards(): rising = lax.ppermute(rising, 'high', up_z)  16.6 us
    ppermute x2, starting transfers between devices, shards(): falling = lax.ppermute(falling, 'high', down_z)  14.4 us
    pallas_call x1, Pallas kernels, shards(): pl.pallas_call(expert_kernel, in_specs=[smem, vmem, vmem] + [hbm] * (2 *...  11 us
    ppermute x1, starting transfers between devices, shards(): falling = lax.ppermute(mine_for(reach + 1).astype(BF), 'high', down_z)  10.1 us
  transfers between devices with their start and end apart: 17, of which 10 were waited for; matrix products, arithmetic and copies ran while one was open for 0% of the time, Pallas kernels for 2%

profile of v4, /device:TPU:8, one launch (start us, length us, event | category | flops | bytes accessed | tf_op | source)
XLA Modules:
  0.0 270.0 jit_solution(10902992102037649690)
XLA Ops:
  0.0 1.5 copy.8
  3.3 3.4 %collective-permute-start = (bf16[3072,256]{1,0:T(8,128)(2,1)S(1)}, bf16[3072,256]{1,0:T(8,128)(2,1)}, u32[]{:S(2)}, u32[]{:S(2)}) collective-permute-start(bf16[3072,256]{1,0:T(8,128)(2,1)S(1)} %get-tuple-element.26.refs_0_), channel_id=1, source_target_pairs={{0,256},{256,512},{512,768},{768,0},{1,257},{257,513},{513,769},{7... | collective-permute-start | bytes 4718600 | tf_op jit(solution)/shard_map/ppermute | solution.py:125
  6.8 3.7 %collective-permute-start.1 = (bf16[3072,256]{1,0:T(8,128)(2,1)S(1)}, bf16[3072,256]{1,0:T(8,128)(2,1)}, u32[]{:S(2)}, u32[]{:S(2)}) collective-permute-start(bf16[3072,256]{1,0:T(8,128)(2,1)S(1)} %get-tuple-element.25.refs_1_), channel_id=1, source_target_pairs={{0,768},{256,0},{512,256},{768,512},{1,769},{257,1},{513,257},{769... | collective-permute-start | bytes 4718600 | tf_op jit(solution)/shard_map/ppermute | solution.py:126
  10.4 2.2 collective-permute-start.2
  12.6 4.9 %collective-permute-start.3 = (bf16[3072,256]{1,0:T(8,128)(2,1)S(1)}, bf16[3072,256]{1,0:T(8,128)(2,1)}, u32[]{:S(2)}, u32[]{:S(2)}) collective-permute-start(bf16[3072,256]{1,0:T(8,128)(2,1)S(1)} %get-tuple-element.26.refs_0_), channel_id=1, source_target_pairs={{0,768},{256,0},{512,256},{768,512},{1,769},{257,1},{513,257},{769... | collective-permute-start | bytes 4718600 | tf_op jit(solution)/shard_map/ppermute | solution.py:128
  17.7 61.0 %all-gather = bf16[640,512]{1,0:T(8,128)(2,1)} all-gather(bf16[80,512]{1,0:T(8,128)(2,1)S(1)} %fusion.8), channel_id=2, replica_groups=mesh['x'=4,'core'=2,'narrow'=4,'high'=8,'low'=4] {'high'}, dimensions={0}, use_global_device_ids=true | all-gather | bytes 737280 | tf_op jit(solution)/shard_map/all_gather | solution.py:136
  78.7 4.1 %select.32 = (bf16[4,256,512]{2,1,0:T(8,128)(2,1)}, bf16[4,256,128]{2,1,0:T(8,128)(2,1)}) custom-call(s32[1]{0:T(128)} %bitcast.refs_0_, bf16[8,80,512]{2,1,0:T(8,128)(2,1)} %bitcast.45), custom_call_target="tpu_custom_call" | custom-call | tf_op jit(solution)/shard_map/select/pallas_call | solution.py:145
  82.8 7.6 %all-to-all-start = ((bf16[64,16,512]{2,1,0:T(8,128)(2,1)}), bf16[64,16,512]{2,1,0:T(8,128)(2,1)}, u32[]{:S(2)}, u32[]{:S(2)}) async-start(bf16[64,16,512]{2,1,0:T(8,128)(2,1)} %bitcast.52), calls=%async_computation | async-start | bytes 2097152 | tf_op jit(solution)/shard_map/all_to_all | solution.py:162
  90.5 3.4 %collective-permute-start.5 = (bf16[3072,256]{1,0:T(8,128)(2,1)}, bf16[3072,256]{1,0:T(8,128)(2,1)S(1)}, u32[]{:S(2)}, u32[]{:S(2)}) collective-permute-start(bf16[3072,256]{1,0:T(8,128)(2,1)} %collective-permute-done.refs_2_), channel_id=1, source_target_pairs={{0,256},{256,512},{512,768},{768,0},{1,257},{257,513},{513,769},{7... | collective-permute-start | bytes 4718600 | tf_op jit(solution)/shard_map/ppermute | solution.py:140
  93.8 3.7 %collective-permute-start.6 = (bf16[3072,256]{1,0:T(8,128)(2,1)}, bf16[3072,256]{1,0:T(8,128)(2,1)S(1)}, u32[]{:S(2)}, u32[]{:S(2)}) collective-permute-start(bf16[3072,256]{1,0:T(8,128)(2,1)} %collective-permute-done.1.refs_5_), channel_id=1, source_target_pairs={{0,768},{256,0},{512,256},{768,512},{1,769},{257,1},{513,257},{769... | collective-permute-start | bytes 4718600 | tf_op jit(solution)/shard_map/ppermute | solution.py:141
  97.5 20.2 %all-to-all-done = bf16[64,16,512]{2,1,0:T(8,128)(2,1)} async-done(((bf16[64,16,512]{2,1,0:T(8,128)(2,1)}), bf16[64,16,512]{2,1,0:T(8,128)(2,1)}, u32[]{:S(2)}, u32[]{:S(2)}) %all-to-all-start) | async-done | bytes 1048608 | tf_op jit(solution)/shard_map/all_to_all | solution.py:162
  117.8 1.9 collective-permute-start.4
  119.7 17.8 %collective-permute-done.5.refs_6_ = bf16[3072,256]{1,0:T(8,128)(2,1)S(1)} collective-permute-done((bf16[3072,256]{1,0:T(8,128)(2,1)}, bf16[3072,256]{1,0:T(8,128)(2,1)S(1)}, u32[]{:S(2)}, u32[]{:S(2)}) %collective-permute-start.5) | collective-permute-done | bytes 1572896 | tf_op jit(solution)/shard_map/ppermute | solution.py:140
  139.1 11.0 %expert.1 = (bf16[4,256,512]{2,1,0:T(8,128)(2,1)}, bf16[4,256,512]{2,1,0:T(8,128)(2,1)}) custom-call(s32[1]{0:T(128)} %bitcast.8.core_ref, bf16[4,256,512]{2,1,0:T(8,128)(2,1)} %bitcast.10.own_x, bf16[4,256,512]{2,1,0:T(8,128)(2,1)} %collective-permute-done.4.other_x, bf16[3072,256]{1,0:T(8,128)(2,1)} %copy-done.1, bf16[3072,256]{1,0:T(8,128)(2,1)} %copy-done, ...), custom_call_target="tpu_custom_call" | custom-call | tf_op jit(solution)/shard_map/expert/pallas_call | solution.py:166
  150.2 1.9 collective-permute-start.7
  152.1 2.8 %collective-permute-done.7 = bf16[4,256,512]{2,1,0:T(8,128)(2,1)S(1)} collective-permute-done((bf16[4,256,512]{2,1,0:T(8,128)(2,1)}, bf16[4,256,512]{2,1,0:T(8,128)(2,1)S(1)}, u32[]{:S(2)}, u32[]{:S(2)}) %collective-permute-start.7) | collective-permute-done | bytes 1048608 | tf_op jit(solution)/shard_map/ppermute | solution.py:181
  154.9 2.5 add_convert_fusion
  157.5 8.4 %all-to-all-start.1 = ((bf16[64,16,512]{2,1,0:T(8,128)(2,1)}), bf16[64,16,512]{2,1,0:T(8,128)(2,1)S(1)}, u32[]{:S(2)}, u32[]{:S(2)}) async-start(bf16[64,16,512]{2,1,0:T(8,128)(2,1)} %bitcast.11), calls=%async_computation.1 | async-start | bytes 2097152 | tf_op jit(solution)/shard_map/all_to_all | solution.py:183
  165.8 28.8 %all-to-all-done.1 = bf16[64,16,512]{2,1,0:T(8,128)(2,1)S(1)} async-done(((bf16[64,16,512]{2,1,0:T(8,128)(2,1)}), bf16[64,16,512]{2,1,0:T(8,128)(2,1)S(1)}, u32[]{:S(2)}, u32[]{:S(2)}) %all-to-all-start.1) | async-done | bytes 1048608 | tf_op jit(solution)/shard_map/all_to_all | solution.py:183
  195.7 3.7 %combine.1 = bf16[4,128,512]{2,1,0:T(8,128)(2,1)} custom-call(bf16[4,256,128]{2,1,0:T(8,128)(2,1)} %get-tuple-element.16.weight_ref, bf16[4,256,512]{2,1,0:T(8,128)(2,1)} %bitcast.42), custom_call_target="tpu_custom_call" | custom-call | tf_op jit(solution)/shard_map/combine/pallas_call | solution.py:186
  200.3 9.1 %collective-permute-start.8 = (bf16[64,512]{1,0:T(8,128)(2,1)S(1)}, bf16[64,512]{1,0:T(8,128)(2,1)S(1)}, u32[]{:S(2)}, u32[]{:S(2)}) collective-permute-start(bf16[64,512]{1,0:T(8,128)(2,1)S(1)} %get-tuple-element.31), channel_id=1, source_target_pairs={{0,4},{4,8},{8,12},{12,16},{16,20},{20,24},{24,28},{28,0},{1,5},{5... | collective-permute-start | bytes 196616 | tf_op jit(solution)/shard_map/ppermute | solution.py:207
  209.4 10.1 %collective-permute-start.12 = (bf16[64,512]{1,0:T(8,128)(2,1)S(1)}, bf16[64,512]{1,0:T(8,128)(2,1)S(1)}, u32[]{:S(2)}, u32[]{:S(2)}) collective-permute-start(bf16[64,512]{1,0:T(8,128)(2,1)S(1)} %get-tuple-element.32), channel_id=1, source_target_pairs={{0,28},{4,0},{8,4},{12,8},{16,12},{20,16},{24,20},{28,24},{1,29},{... | collective-permute-start | bytes 196616 | tf_op jit(solution)/shard_map/ppermute | solution.py:208
  219.5 4.4 %collective-permute-done.8 = bf16[64,512]{1,0:T(8,128)(2,1)S(1)} collective-permute-done((bf16[64,512]{1,0:T(8,128)(2,1)S(1)}, bf16[64,512]{1,0:T(8,128)(2,1)S(1)}, u32[]{:S(2)}, u32[]{:S(2)}) %collective-permute-start.8) | collective-permute-done | bytes 65568 | tf_op jit(solution)/shard_map/ppermute | solution.py:207
  224.8 1.9 collective-permute-start.9
  226.8 9.2 %collective-permute-done.9 = bf16[64,512]{1,0:T(8,128)(2,1)S(1)} collective-permute-done((bf16[64,512]{1,0:T(8,128)(2,1)S(1)}, bf16[64,512]{1,0:T(8,128)(2,1)S(1)}, u32[]{:S(2)}, u32[]{:S(2)}) %collective-permute-start.9) | collective-permute-done | bytes 65568 | tf_op jit(solution)/shard_map/ppermute | solution.py:211
  236.9 2.4 collective-permute-start.10
  239.3 7.4 %collective-permute-start.13 = (bf16[64,512]{1,0:T(8,128)(2,1)S(1)}, bf16[64,512]{1,0:T(8,128)(2,1)S(1)}, u32[]{:S(2)}, u32[]{:S(2)}) collective-permute-start(bf16[64,512]{1,0:T(8,128)(2,1)S(1)} %get-tuple-element.30), channel_id=1, source_target_pairs={{0,28},{4,0},{8,4},{12,8},{16,12},{20,16},{24,20},{28,24},{1,29},{... | collective-permute-start | bytes 196616 | tf_op jit(solution)/shard_map/ppermute | solution.py:214
  247.0 3.5 %collective-permute-done.13 = bf16[64,512]{1,0:T(8,128)(2,1)S(1)} collective-permute-done((bf16[64,512]{1,0:T(8,128)(2,1)S(1)}, bf16[64,512]{1,0:T(8,128)(2,1)S(1)}, u32[]{:S(2)}, u32[]{:S(2)}) %collective-permute-start.13) | collective-permute-done | bytes 65568 | tf_op jit(solution)/shard_map/ppermute | solution.py:214
  251.4 7.0 %collective-permute-start.14 = (bf16[64,512]{1,0:T(8,128)(2,1)S(1)}, bf16[64,512]{1,0:T(8,128)(2,1)S(1)}, u32[]{:S(2)}, u32[]{:S(2)}) collective-permute-start(bf16[64,512]{1,0:T(8,128)(2,1)S(1)} %get-tuple-element.28), channel_id=1, source_target_pairs={{0,28},{4,0},{8,4},{12,8},{16,12},{20,16},{24,20},{28,24},{1,29},{... | collective-permute-start | bytes 196616 | tf_op jit(solution)/shard_map/ppermute | solution.py:214
  258.4 2.7 %collective-permute-start.11 = (bf16[64,512]{1,0:T(8,128)(2,1)S(1)}, bf16[64,512]{1,0:T(8,128)(2,1)S(1)}, u32[]{:S(2)}, u32[]{:S(2)}) collective-permute-start(bf16[64,512]{1,0:T(8,128)(2,1)S(1)} %get-tuple-element.27), channel_id=1, source_target_pairs={{0,4},{4,8},{8,12},{12,16},{16,20},{20,24},{24,28},{28,0},{1,5},{5... | collective-permute-start | bytes 196616 | tf_op jit(solution)/shard_map/ppermute | solution.py:211
  261.5 7.0 %collective-permute-done.11 = bf16[64,512]{1,0:T(8,128)(2,1)S(1)} collective-permute-done((bf16[64,512]{1,0:T(8,128)(2,1)S(1)}, bf16[64,512]{1,0:T(8,128)(2,1)S(1)}, u32[]{:S(2)}, u32[]{:S(2)}) %collective-permute-start.11) | collective-permute-done | bytes 65568 | tf_op jit(solution)/shard_map/ppermute | solution.py:211
  268.5 1.5 fusion.7
  (43 shorter events, 8.8 us)
Async XLA Ops:
  1.5 1.2 copy-start.5
  1.5 1.5 copy-start.6
  3.0 14.5 %copy-start.8 = (f32[64,8]{0,1:T(8,128)S(1)}, f32[64,8]{0,1:T(8,128)}, u32[]{:S(2)}) copy-start(f32[64,8]{0,1:T(8,128)} %param.8) | copy-start | bytes 6148
  3.0 14.5 %copy-start.9 = (s32[64,8]{0,1:T(8,128)S(1)}, s32[64,8]{0,1:T(8,128)}, u32[]{:S(2)}) copy-start(s32[64,8]{0,1:T(8,128)} %param.7) | copy-start | bytes 6148
  3.0 14.6 %copy-start.7 = (bf16[64,512]{1,0:T(8,128)(2,1)S(1)}, bf16[64,512]{1,0:T(8,128)(2,1)}, u32[]{:S(2)}) copy-start(bf16[64,512]{1,0:T(8,128)(2,1)} %param.6) | copy-start | bytes 196612
  3.3 79.5 %copy-start = (bf16[3072,256]{1,0:T(8,128)(2,1)}, bf16[3072,256]{1,0:T(8,128)(2,1)S(1)}, u32[]{:S(2)}) copy-start(bf16[3072,256]{1,0:T(8,128)(2,1)S(1)} %get-tuple-element.25.refs_1_) | copy-start | bytes 4718596
  3.3 79.5 %copy-start.1 = (bf16[3072,256]{1,0:T(8,128)(2,1)}, bf16[3072,256]{1,0:T(8,128)(2,1)S(1)}, u32[]{:S(2)}) copy-start(bf16[3072,256]{1,0:T(8,128)(2,1)S(1)} %get-tuple-element.26.refs_0_) | copy-start | bytes 4718596
  3.3 75.4 %collective-permute-start = (bf16[3072,256]{1,0:T(8,128)(2,1)S(1)}, bf16[3072,256]{1,0:T(8,128)(2,1)}, u32[]{:S(2)}, u32[]{:S(2)}) collective-permute-start(bf16[3072,256]{1,0:T(8,128)(2,1)S(1)} %get-tuple-element.26.refs_0_), channel_id=1, source_target_pairs={{0,256},{256,512},{512,768},{768,0},{1,257},{257,513},{513,769},{7... | collective-permute-start | bytes 4718600 | tf_op jit(solution)/shard_map/ppermute | solution.py:125
  6.8 72.0 %collective-permute-start.1 = (bf16[3072,256]{1,0:T(8,128)(2,1)S(1)}, bf16[3072,256]{1,0:T(8,128)(2,1)}, u32[]{:S(2)}, u32[]{:S(2)}) collective-permute-start(bf16[3072,256]{1,0:T(8,128)(2,1)S(1)} %get-tuple-element.25.refs_1_), channel_id=1, source_target_pairs={{0,768},{256,0},{512,256},{768,512},{1,769},{257,1},{513,257},{769... | collective-permute-start | bytes 4718600 | tf_op jit(solution)/shard_map/ppermute | solution.py:126
  10.4 72.4 %collective-permute-start.2 = (bf16[3072,256]{1,0:T(8,128)(2,1)S(1)}, bf16[3072,256]{1,0:T(8,128)(2,1)}, u32[]{:S(2)}, u32[]{:S(2)}) collective-permute-start(bf16[3072,256]{1,0:T(8,128)(2,1)S(1)} %get-tuple-element.25.refs_1_), channel_id=1, source_target_pairs={{0,256},{256,512},{512,768},{768,0},{1,257},{257,513},{513,769},{7... | collective-permute-start | bytes 4718600 | tf_op jit(solution)/shard_map/ppermute | solution.py:127
  12.6 70.2 %collective-permute-start.3 = (bf16[3072,256]{1,0:T(8,128)(2,1)S(1)}, bf16[3072,256]{1,0:T(8,128)(2,1)}, u32[]{:S(2)}, u32[]{:S(2)}) collective-permute-start(bf16[3072,256]{1,0:T(8,128)(2,1)S(1)} %get-tuple-element.26.refs_0_), channel_id=1, source_target_pairs={{0,768},{256,0},{512,256},{768,512},{1,769},{257,1},{513,257},{769... | collective-permute-start | bytes 4718600 | tf_op jit(solution)/shard_map/ppermute | solution.py:128
  82.8 34.9 %all-to-all-start = ((bf16[64,16,512]{2,1,0:T(8,128)(2,1)}), bf16[64,16,512]{2,1,0:T(8,128)(2,1)}, u32[]{:S(2)}, u32[]{:S(2)}) async-start(bf16[64,16,512]{2,1,0:T(8,128)(2,1)} %bitcast.52), calls=%async_computation | async-start | bytes 2097152 | tf_op jit(solution)/shard_map/all_to_all | solution.py:162
  90.5 47.0 %collective-permute-start.5 = (bf16[3072,256]{1,0:T(8,128)(2,1)}, bf16[3072,256]{1,0:T(8,128)(2,1)S(1)}, u32[]{:S(2)}, u32[]{:S(2)}) collective-permute-start(bf16[3072,256]{1,0:T(8,128)(2,1)} %collective-permute-done.refs_2_), channel_id=1, source_target_pairs={{0,256},{256,512},{512,768},{768,0},{1,257},{257,513},{513,769},{7... | collective-permute-start | bytes 4718600 | tf_op jit(solution)/shard_map/ppermute | solution.py:140
  93.8 43.6 %collective-permute-start.6 = (bf16[3072,256]{1,0:T(8,128)(2,1)}, bf16[3072,256]{1,0:T(8,128)(2,1)S(1)}, u32[]{:S(2)}, u32[]{:S(2)}) collective-permute-start(bf16[3072,256]{1,0:T(8,128)(2,1)} %collective-permute-done.1.refs_5_), channel_id=1, source_target_pairs={{0,768},{256,0},{512,256},{768,512},{1,769},{257,1},{513,257},{769... | collective-permute-start | bytes 4718600 | tf_op jit(solution)/shard_map/ppermute | solution.py:141
  117.8 19.7 %collective-permute-start.4 = (bf16[4,256,512]{2,1,0:T(8,128)(2,1)}, bf16[4,256,512]{2,1,0:T(8,128)(2,1)}, u32[]{:S(2)}, u32[]{:S(2)}) collective-permute-start(bf16[4,256,512]{2,1,0:T(8,128)(2,1)} %bitcast.10.own_x), channel_id=1, source_target_pairs={{0,128},{128,0},{1,129},{129,1},{2,130},{130,2},{3,131},{131,3},{4... | collective-permute-start | bytes 3145736 | tf_op jit(solution)/shard_map/ppermute | solution.py:165
  137.5 1.2 copy-start.3
  137.5 1.7 copy-start.4
  150.2 4.8 %collective-permute-start.7 = (bf16[4,256,512]{2,1,0:T(8,128)(2,1)}, bf16[4,256,512]{2,1,0:T(8,128)(2,1)S(1)}, u32[]{:S(2)}, u32[]{:S(2)}) collective-permute-start(bf16[4,256,512]{2,1,0:T(8,128)(2,1)} %get-tuple-element.24), channel_id=1, source_target_pairs={{0,128},{128,0},{1,129},{129,1},{2,130},{130,2},{3,131},{131,3},{4... | collective-permute-start | bytes 3145736 | tf_op jit(solution)/shard_map/ppermute | solution.py:181
  157.5 37.2 %all-to-all-start.1 = ((bf16[64,16,512]{2,1,0:T(8,128)(2,1)}), bf16[64,16,512]{2,1,0:T(8,128)(2,1)S(1)}, u32[]{:S(2)}, u32[]{:S(2)}) async-start(bf16[64,16,512]{2,1,0:T(8,128)(2,1)} %bitcast.11), calls=%async_computation.1 | async-start | bytes 2097152 | tf_op jit(solution)/shard_map/all_to_all | solution.py:183
  194.7 1.0 copy-start.2
  200.3 23.7 %collective-permute-start.8 = (bf16[64,512]{1,0:T(8,128)(2,1)S(1)}, bf16[64,512]{1,0:T(8,128)(2,1)S(1)}, u32[]{:S(2)}, u32[]{:S(2)}) collective-permute-start(bf16[64,512]{1,0:T(8,128)(2,1)S(1)} %get-tuple-element.31), channel_id=1, source_target_pairs={{0,4},{4,8},{8,12},{12,16},{16,20},{20,24},{24,28},{28,0},{1,5},{5... | collective-permute-start | bytes 196616 | tf_op jit(solution)/shard_map/ppermute | solution.py:207
  209.4 17.4 %collective-permute-start.12 = (bf16[64,512]{1,0:T(8,128)(2,1)S(1)}, bf16[64,512]{1,0:T(8,128)(2,1)S(1)}, u32[]{:S(2)}, u32[]{:S(2)}) collective-permute-start(bf16[64,512]{1,0:T(8,128)(2,1)S(1)} %get-tuple-element.32), channel_id=1, source_target_pairs={{0,28},{4,0},{8,4},{12,8},{16,12},{20,16},{24,20},{28,24},{1,29},{... | collective-permute-start | bytes 196616 | tf_op jit(solution)/shard_map/ppermute | solution.py:208
  224.8 11.2 %collective-permute-start.9 = (bf16[64,512]{1,0:T(8,128)(2,1)S(1)}, bf16[64,512]{1,0:T(8,128)(2,1)S(1)}, u32[]{:S(2)}, u32[]{:S(2)}) collective-permute-start(bf16[64,512]{1,0:T(8,128)(2,1)S(1)} %fusion.5), channel_id=1, source_target_pairs={{0,4},{4,8},{8,12},{12,16},{16,20},{20,24},{24,28},{28,0},{1,5},{5... | collective-permute-start | bytes 196616 | tf_op jit(solution)/shard_map/ppermute | solution.py:211
  236.9 10.1 %collective-permute-start.10 = (bf16[64,512]{1,0:T(8,128)(2,1)S(1)}, bf16[64,512]{1,0:T(8,128)(2,1)S(1)}, u32[]{:S(2)}, u32[]{:S(2)}) collective-permute-start(bf16[64,512]{1,0:T(8,128)(2,1)S(1)} %get-tuple-element.29), channel_id=1, source_target_pairs={{0,4},{4,8},{8,12},{12,16},{16,20},{20,24},{24,28},{28,0},{1,5},{5... | collective-permute-start | bytes 196616 | tf_op jit(solution)/shard_map/ppermute | solution.py:211
  239.3 11.2 %collective-permute-start.13 = (bf16[64,512]{1,0:T(8,128)(2,1)S(1)}, bf16[64,512]{1,0:T(8,128)(2,1)S(1)}, u32[]{:S(2)}, u32[]{:S(2)}) collective-permute-start(bf16[64,512]{1,0:T(8,128)(2,1)S(1)} %get-tuple-element.30), channel_id=1, source_target_pairs={{0,28},{4,0},{8,4},{12,8},{16,12},{20,16},{24,20},{28,24},{1,29},{... | collective-permute-start | bytes 196616 | tf_op jit(solution)/shard_map/ppermute | solution.py:214
  251.4 10.1 %collective-permute-start.14 = (bf16[64,512]{1,0:T(8,128)(2,1)S(1)}, bf16[64,512]{1,0:T(8,128)(2,1)S(1)}, u32[]{:S(2)}, u32[]{:S(2)}) collective-permute-start(bf16[64,512]{1,0:T(8,128)(2,1)S(1)} %get-tuple-element.28), channel_id=1, source_target_pairs={{0,28},{4,0},{8,4},{12,8},{16,12},{20,16},{24,20},{28,24},{1,29},{... | collective-permute-start | bytes 196616 | tf_op jit(solution)/shard_map/ppermute | solution.py:214
  258.4 10.1 %collective-permute-start.11 = (bf16[64,512]{1,0:T(8,128)(2,1)S(1)}, bf16[64,512]{1,0:T(8,128)(2,1)S(1)}, u32[]{:S(2)}, u32[]{:S(2)}) collective-permute-start(bf16[64,512]{1,0:T(8,128)(2,1)S(1)} %get-tuple-element.27), channel_id=1, source_target_pairs={{0,4},{4,8},{8,12},{12,16},{16,20},{20,24},{24,28},{28,0},{1,5},{5... | collective-permute-start | bytes 196616 | tf_op jit(solution)/shard_map/ppermute | solution.py:211

commit v5 on v4

--- a/solution.py
+++ b/solution.py
@@ -45,24 +45,22 @@
 
 
 def combine_kernel(weight_ref, back_ref, part_ref):
+    back = back_ref[:, 0].reshape(weight_ref.shape[1], back_ref.shape[3])
     part_ref[0] = lax.dot_general(
-        weight_ref[0], back_ref[0], (((0,), (0,)), ((), ())), preferred_element_type=F32
+        weight_ref[0], back, (((0,), (0,)), ((), ())), preferred_element_type=F32
     ).astype(BF)
 
 
-def expert_kernel(
-    core_ref, own_x, other_x, *refs
-):
-    parts, (keep_ref, send_ref, weights, rows, hidden, total, sems) = refs[:-7], refs[-7:]
+def hidden_kernel(place_ref, own_x, other_x, *refs):
+    parts, (out_ref, weights, rows, hidden, sems) = refs[:-5], refs[-5:]
     n_x, n_rows, piece = own_x.shape
     d_model = rows.shape[1]
-    width = weights.shape[2]
-    ff = width // 2
-    core = core_ref[0]
-    half = parts[0].shape[0]
+    half = d_model // 2
+    ff = weights.shape[2] // 2
+    core, chip = place_ref[0], place_ref[1]
     copies = [
         pltpu.make_async_copy(
-            part, weights.at[i // 2, (i % 2) * half : (i % 2 + 1) * half], sems.at[i]
+            part.at[:half], weights.at[i // 2, (i % 2) * half : (i % 2 + 1) * half], sems.at[i]
         )
         for i, part in enumerate(parts)
     ]
@@ -73,25 +71,52 @@
         rows[:, pl.ds(at, piece)] = own_x[x]
         at = pl.multiple_of((2 * x + 1 - core) * piece, piece)
         rows[:, pl.ds(at, piece)] = other_x[x]
-    for b in range(n_x):
+    for b, shift in enumerate((0, n_x - 1, 1, 2)):
         copies[2 * b].wait()
         copies[2 * b + 1].wait()
-        both = jnp.dot(rows[...], weights[b, :d_model, :], preferred_element_type=F32)
+        both = jnp.dot(rows[...], weights[b], preferred_element_type=F32)
         gate, up = both[:, :ff], both[:, ff:]
-        hidden[:, b * ff : (b + 1) * ff] = (gate / (1.0 + jnp.exp(-gate)) * up).astype(BF)
-    for n in range(d_model // width):
-        at = d_model + n * ff
-        down = jnp.concatenate(
-            [weights[b, at : at + ff, :] for b in range(n_x)], axis=0
-        )
-        total[:, n * width : (n + 1) * width] = jnp.dot(
-            hidden[...], down, preferred_element_type=F32
-        ).astype(BF)
+        at = pl.multiple_of(lax.rem(chip + shift, n_x) * ff, ff)
+        hidden[:, pl.ds(at, ff)] = (gate / (1.0 + jnp.exp(-gate)) * up).astype(BF)
     for x in range(n_x):
-        at = pl.multiple_of((2 * x + core) * piece, piece)
-        keep_ref[x] = total[:, pl.ds(at, piece)]
-        at = pl.multiple_of((2 * x + 1 - core) * piece, piece)
-        send_ref[x] = total[:, pl.ds(at, piece)]
+        out_ref[x] = hidden[...]
+
+
+def down_kernel(place_ref, hidden_ref, own, prev, nxt, far_a, far_b, keep_ref, send_ref, weights, sems):
+    n_x, n_rows, units = hidden_ref.shape
+    n_cols, _, width = weights.shape
+    ff = units // n_x
+    core, chip = place_ref[0], place_ref[1]
+    first = far_a.shape[0] - (n_cols // 2) * ff
+    start = prev.shape[0] - n_cols * ff
+    copies = []
+    for b, (shift, piece) in enumerate(((0, own), (n_x - 1, prev), (1, nxt), (2, None))):
+        at = pl.multiple_of(lax.rem(chip + shift, n_x) * ff, ff)
+        for n in range(n_cols):
+            if piece is None:
+                part = far_a if n < n_cols // 2 else far_b
+                low = first + (n % (n_cols // 2)) * ff
+            else:
+                part = piece
+                low = n * ff + (0 if shift == 0 else start)
+            copies.append(
+                pltpu.make_async_copy(
+                    part.at[low : low + ff], weights.at[n, pl.ds(at, ff)], sems.at[b * n_cols + n]
+                )
+            )
+    for copy in copies:
+        copy.start()
+    for copy in copies:
+        copy.wait()
+    mine = n_cols // 2
+    rows = hidden_ref[...].reshape(n_x * n_rows, units)
+    for ref, side in ((send_ref, 1 - core), (keep_ref, core)):
+        for i in range(mine):
+            out = jnp.dot(rows, weights[side * mine + i], preferred_element_type=F32).astype(BF)
+            for x in range(n_x):
+                ref[:, x, :, i * width : (i + 1) * width] = out[
+                    x * n_rows : (x + 1) * n_rows
+                ].reshape(ref.shape[0], ref.shape[2], width)
 
 
 def shards(tokens, routes, route_weight, gate_weight, up_weight, down_weight):
@@ -110,22 +135,27 @@
     up_x = [(i, (i + 1) % n_x) for i in range(n_x)]
     down_x = [(i, (i - 1) % n_x) for i in range(n_x)]
 
-    own_w = jnp.concatenate(
-        [
-            jnp.concatenate([gate_weight[0], up_weight[0]], axis=1),
-            down_weight[0]
-            .reshape(ff, d_model // (2 * ff), 2 * ff)
-            .transpose(1, 0, 2)
-            .reshape(d_model // 2, 2 * ff),
-        ],
-        axis=0,
-    )
-    half = own_w.shape[0] // 2
-    own_a, own_b = own_w[:half], own_w[half:]
-    prev_a = lax.ppermute(own_a, "x", up_x)
-    next_b = lax.ppermute(own_b, "x", down_x)
-    prev_b = lax.ppermute(own_b, "x", up_x)
-    next_a = lax.ppermute(own_a, "x", down_x)
+    chip = lax.axis_index("x")
+    half, width = d_model // 2, 2 * ff
+    n_cols = d_model // n_x // width
+    own_g = jnp.concatenate([gate_weight[0], up_weight[0]], axis=1)
+    down = (
+        down_weight[0]
+        .reshape(ff, n_x, n_cols, width)
+        .transpose(1, 2, 0, 3)
+        .reshape(n_x, n_cols * ff, width)
+    )
+
+    def columns_of(shift):
+        return lax.dynamic_slice_in_dim(down, lax.rem(chip + shift, n_x), 1, 0)[0]
+
+    beyond = columns_of(2)
+    cut = beyond.shape[0] // 2
+    own_a, own_b = own_g[:half], own_g[half:]
+    prev_a = lax.ppermute(jnp.concatenate([own_a, beyond[:cut]], axis=0), "x", up_x)
+    next_b = lax.ppermute(jnp.concatenate([own_b, beyond[cut:]], axis=0), "x", down_x)
+    prev_b = lax.ppermute(jnp.concatenate([own_b, columns_of(1)], axis=0), "x", up_x)
+    next_a = lax.ppermute(jnp.concatenate([own_a, columns_of(n_x - 1)], axis=0), "x", down_x)
 
     high = lax.axis_index("high")
     meta = jnp.concatenate([routes.T.astype(BF), route_weight.T.astype(BF)], axis=0)
@@ -140,7 +170,7 @@
     far_a = lax.ppermute(prev_a, "x", up_x)
     far_b = lax.ppermute(next_b, "x", down_x)
     base = (high * n_low).reshape(1).astype(jnp.int32)
-    core = lax.axis_index("core").reshape(1).astype(jnp.int32)
+    place = jnp.stack([lax.axis_index("core"), chip]).astype(jnp.int32)
     full = near.shape[1]
     rows, weight = pl.pallas_call(
         lambda *refs: select_kernel(n_low, n_high * n_low, *refs),
@@ -163,32 +193,45 @@
         rows.reshape(-1, pair * CAP, piece), peers, split_axis=0, concat_axis=0, tiled=True
     ).reshape(n_x, slots, piece)
     other_x = lax.ppermute(own_x, "core", swap)
-    keep, send = pl.pallas_call(
-        expert_kernel,
+    hidden = pl.pallas_call(
+        hidden_kernel,
         in_specs=[smem, vmem, vmem] + [hbm] * (2 * n_x),
-        out_specs=[vmem, vmem],
-        out_shape=[jax.ShapeDtypeStruct(own_x.shape, BF)] * 2,
+        out_specs=vmem,
+        out_shape=jax.ShapeDtypeStruct((n_x, slots, n_x * ff), BF),
         scratch_shapes=[
-            pltpu.VMEM((n_x,) + own_w.shape, BF),
+            pltpu.VMEM((n_x, d_model, width), BF),
             pltpu.VMEM((slots, d_model), BF),
             pltpu.VMEM((slots, n_x * ff), BF),
-            pltpu.VMEM((slots, d_model), BF),
             pltpu.SemaphoreType.DMA((2 * n_x,)),
         ],
         compiler_params=params,
-        name="expert",
-    )(core, own_x, other_x, own_a, own_b, prev_a, prev_b, next_a, next_b, far_a, far_b)
+        name="hidden",
+    )(place, own_x, other_x, own_a, own_b, prev_a, prev_b, next_a, next_b, far_a, far_b)
+    hidden = lax.all_to_all(hidden, "x", split_axis=0, concat_axis=0, tiled=True)
+    n_near = n_narrow * n_low
+    keep, send = pl.pallas_call(
+        down_kernel,
+        in_specs=[smem, vmem] + [hbm] * 5,
+        out_specs=[vmem, vmem],
+        out_shape=[jax.ShapeDtypeStruct((n_near, n_x, pair * CAP, piece), BF)] * 2,
+        scratch_shapes=[
+            pltpu.VMEM((n_cols, n_x * ff, width), BF),
+            pltpu.SemaphoreType.DMA((n_x * n_cols,)),
+        ],
+        compiler_params=params,
+        name="down",
+    )(place, hidden, columns_of(0), prev_b, next_a, far_a, far_b)
     got = lax.ppermute(send, "core", swap)
     out = (keep.astype(F32) + got.astype(F32)).astype(BF)
     back = lax.all_to_all(
-        out.reshape(-1, pair * CAP, piece), peers, split_axis=0, concat_axis=0, tiled=True
-    ).reshape(n_x, slots, piece)
+        out.reshape(n_near, -1, piece), ("narrow", "low"), split_axis=0, concat_axis=0, tiled=True
+    ).reshape(n_near, n_x, pair * CAP, piece)
     part = pl.pallas_call(
         combine_kernel,
         grid=(n_x,),
         in_specs=[
             pl.BlockSpec((1, slots, lanes), lambda h: (h, 0, 0)),
-            pl.BlockSpec((1, slots, piece), lambda h: (h, 0, 0)),
+            pl.BlockSpec((n_near, 1, pair * CAP, piece), lambda h: (0, h, 0, 0)),
         ],
         out_specs=pl.BlockSpec((1, lanes, piece), lambda h: (h, 0, 0)),
         out_shape=jax.ShapeDtypeStruct((n_x, lanes, piece), BF),

time: 271 us -> 280 us (1.033)
  the two profiles are of different devices: /device:TPU:8 before, /device:TPU:6 now
where the time goes in v5:
time: 280 us; the launch traced here: 278 us
  starting transfers between devices  87.7 us (31%)
  waiting for transfers between devices  80.9 us (29%)
  blocking collectives  67.1 us (24%)
  Pallas kernels  22.1 us (8%)
  other arithmetic  13.8 us (5%)
  local copies, waits for them, and re-layouts  6.02 us (2%)
    all_gather x1, blocking collectives, shards(): lax.all_gather(jnp.concatenate([tokens, meta], axis=0), 'high', axis=0, t...  49.2 us
    all_to_all x1, waiting for transfers between devices, shards(): lax.all_to_all(out.reshape(n_near, -1, piece), ('narrow', 'low'), split_a...  28.1 us
    all_to_all x1, blocking collectives, shards(): lax.all_to_all(hidden, 'x', split_axis=0, concat_axis=0, tiled=True)  17.9 us
    ppermute x3, waiting for transfers between devices, shards(): rising = lax.ppermute(rising, 'high', up_z)  17.7 us
    all_to_all x1, waiting for transfers between devices, shards(): lax.all_to_all(rows.reshape(-1, pair * CAP, piece), peers, split_axis=0,...  16.5 us
    ppermute x2, starting transfers between devices, shards(): falling = lax.ppermute(falling, 'high', down_z)  15.1 us
    ppermute x1, starting transfers between devices, shards(): lax.ppermute(jnp.concatenate([own_a, beyond[:cut]], axis=0), 'x', up_x)  15 us
    ppermute x1, starting transfers between devices, shards(): falling = lax.ppermute(mine_for(reach + 1).astype(BF), 'high', down_z)  10.9 us
  transfers between devices with their start and end apart: 17, of which 11 were waited for; matrix products, arithmetic and copies ran while one was open for 2% of the time, Pallas kernels for 2%

profile of v5, /device:TPU:6, one launch (start us, length us, event | category | flops | bytes accessed | tf_op | source)
XLA Modules:
  0.0 278.0 jit_solution(2485413425721829727)
XLA Ops:
  0.0 1.8 reshape_squeeze.3
  5.2 15.0 %collective-permute-start = (bf16[2304,256]{1,0:T(8,128)(2,1)}, bf16[2304,256]{1,0:T(8,128)(2,1)}, u32[]{:S(2)}, u32[]{:S(2)}) collective-permute-start(bf16[2304,256]{1,0:T(8,128)(2,1)} %pad_maximum_fusion.2), channel_id=1, source_target_pairs={{0,256},{256,512},{512,768},{768,0},{1,257},{257,513},{513,769},{7... | collective-permute-start | bytes 3538952 | tf_op jit(solution)/shard_map/ppermute | solution.py:155
  22.2 1.9 collective-permute-start.2
  25.3 4.0 %collective-permute-start.3 = (bf16[2560,256]{1,0:T(8,128)(2,1)}, bf16[2560,256]{1,0:T(8,128)(2,1)}, u32[]{:S(2)}, u32[]{:S(2)}) collective-permute-start(bf16[2560,256]{1,0:T(8,128)(2,1)} %pad_maximum_fusion.1), channel_id=1, source_target_pairs={{0,768},{256,0},{512,256},{768,512},{1,769},{257,1},{513,257},{769... | collective-permute-start | bytes 3932168 | tf_op jit(solution)/shard_map/ppermute | solution.py:158
  30.5 1.9 collective-permute-start.1
  32.6 49.2 %all-gather = bf16[640,512]{1,0:T(8,128)(2,1)} all-gather(bf16[80,512]{1,0:T(8,128)(2,1)S(1)} %fusion.9), channel_id=2, replica_groups=mesh['x'=4,'core'=2,'narrow'=4,'high'=8,'low'=4] {'high'}, dimensions={0}, use_global_device_ids=true | all-gather | bytes 737280 | tf_op jit(solution)/shard_map/all_gather | solution.py:166
  81.8 4.3 %select.40 = (bf16[4,256,512]{2,1,0:T(8,128)(2,1)}, bf16[4,256,128]{2,1,0:T(8,128)(2,1)}) custom-call(s32[1]{0:T(128)} %bitcast.refs_0_, bf16[8,80,512]{2,1,0:T(8,128)(2,1)} %bitcast.53), custom_call_target="tpu_custom_call" | custom-call | tf_op jit(solution)/shard_map/select/pallas_call | solution.py:175
  86.1 9.3 %all-to-all-start = ((bf16[64,16,512]{2,1,0:T(8,128)(2,1)}), bf16[64,16,512]{2,1,0:T(8,128)(2,1)}, u32[]{:S(2)}, u32[]{:S(2)}) async-start(bf16[64,16,512]{2,1,0:T(8,128)(2,1)} %bitcast.59), calls=%async_computation | async-start | bytes 2097152 | tf_op jit(solution)/shard_map/all_to_all | solution.py:192
  95.4 2.2 collective-permute-start.5
  97.6 3.6 %collective-permute-start.6 = (bf16[2304,256]{1,0:T(8,128)(2,1)}, bf16[2304,256]{1,0:T(8,128)(2,1)}, u32[]{:S(2)}, u32[]{:S(2)}) collective-permute-start(bf16[2304,256]{1,0:T(8,128)(2,1)} %copy-done.5), channel_id=1, source_target_pairs={{0,768},{256,0},{512,256},{768,512},{1,769},{257,1},{513,257},{769... | collective-permute-start | bytes 3538952 | tf_op jit(solution)/shard_map/ppermute | solution.py:171
  101.2 16.5 %all-to-all-done = bf16[64,16,512]{2,1,0:T(8,128)(2,1)} async-done(((bf16[64,16,512]{2,1,0:T(8,128)(2,1)}), bf16[64,16,512]{2,1,0:T(8,128)(2,1)}, u32[]{:S(2)}, u32[]{:S(2)}) %all-to-all-start) | async-done | bytes 1048608 | tf_op jit(solution)/shard_map/all_to_all | solution.py:192
  117.8 1.9 collective-permute-start.4
  120.3 8.3 %collective-permute-done.5.refs_6_.far_a = bf16[2304,256]{1,0:T(8,128)(2,1)S(1)} collective-permute-done((bf16[2304,256]{1,0:T(8,128)(2,1)}, bf16[2304,256]{1,0:T(8,128)(2,1)S(1)}, u32[]{:S(2)}, u32[]{:S(2)}) %collective-permute-start.5) | collective-permute-done | bytes 1179680 | tf_op jit(solution)/shard_map/ppermute | solution.py:170
  130.7 9.2 %hidden.1 = bf16[4,256,512]{2,1,0:T(8,128)(2,1)} custom-call(s32[2]{0:T(128)} %pad_add_fusion.place_ref, bf16[4,256,512]{2,1,0:T(8,128)(2,1)} %bitcast.16.own_x, bf16[4,256,512]{2,1,0:T(8,128)(2,1)} %copy-done.6, bf16[2048,256]{1,0:T(8,128)(2,1)} %copy-done.1, bf16[2048,256]{1,0:T(8,128)(2,1)} %copy-done, bf16[2304,256]{1,0:T(8,128)(2,1)} %collective-permute-done.refs_2_, ...), custom_call_target="tpu_custom_call" | custom-call | tf_op jit(solution)/shard_map/hidden/pallas_call | solution.py:196
  139.9 17.9 %all_to_all.15.hidden_ref = bf16[4,256,512]{2,1,0:T(8,128)(2,1)} all-to-all(bf16[4,256,512]{2,1,0:T(8,128)(2,1)} %hidden.1), channel_id=1, replica_groups=mesh['x'=4,'core'=2,'narrow'=4,'high'=8,'low'=4] {'x'}, dimensions={0} | all-to-all | bytes 2097152 | tf_op jit(solution)/shard_map/all_to_all | solution.py:210
  157.8 4.9 %down.1 = (bf16[16,4,16,512]{3,2,1,0:T(8,128)(2,1)}, bf16[16,4,16,512]{3,2,1,0:T(8,128)(2,1)}) custom-call(s32[2]{0:T(128)} %pad_add_fusion.place_ref, bf16[4,256,512]{2,1,0:T(8,128)(2,1)} %all_to_all.15.hidden_ref, bf16[512,256]{1,0:T(8,128)(2,1)} %get-tuple-element.27.own, bf16[2560,256]{1,0:T(8,128)(2,1)} %copy-done.2, ...), custom_call_target="tpu_custom_call" | custom-call | tf_op jit(solution)/shard_map/down/pallas_call | solution.py:212
  162.7 1.9 collective-permute-start.7
  164.6 2.8 %collective-permute-done.7 = bf16[16,4,16,512]{3,2,1,0:T(8,128)(2,1)S(1)} collective-permute-done((bf16[16,4,16,512]{3,2,1,0:T(8,128)(2,1)}, bf16[16,4,16,512]{3,2,1,0:T(8,128)(2,1)S(1)}, u32[]{:S(2)}, u32[]{:S(2)}) %collective-permute-start.7) | collective-permute-done | bytes 1048608 | tf_op jit(solution)/shard_map/ppermute | solution.py:224
  167.5 2.6 add_convert_fusion
  170.1 6.3 %all-to-all-start.2 = ((bf16[16,64,512]{2,1,0:T(8,128)(2,1)}), bf16[16,64,512]{2,1,0:T(8,128)(2,1)S(1)}, u32[]{:S(2)}, u32[]{:S(2)}) async-start(bf16[16,64,512]{2,1,0:T(8,128)(2,1)} %bitcast.18), calls=%async_computation.2 | async-start | bytes 2097152 | tf_op jit(solution)/shard_map/all_to_all | solution.py:226
  176.4 28.1 %all-to-all-done.2 = bf16[16,64,512]{2,1,0:T(8,128)(2,1)S(1)} async-done(((bf16[16,64,512]{2,1,0:T(8,128)(2,1)}), bf16[16,64,512]{2,1,0:T(8,128)(2,1)S(1)}, u32[]{:S(2)}, u32[]{:S(2)}) %all-to-all-start.2) | async-done | bytes 1048608 | tf_op jit(solution)/shard_map/all_to_all | solution.py:226
  205.5 3.7 %combine.1 = bf16[4,128,512]{2,1,0:T(8,128)(2,1)} custom-call(bf16[4,256,128]{2,1,0:T(8,128)(2,1)} %get-tuple-element.16.weight_ref, bf16[16,4,16,512]{3,2,1,0:T(8,128)(2,1)} %bitcast.52), custom_call_target="tpu_custom_call" | custom-call | tf_op jit(solution)/shard_map/combine/pallas_call | solution.py:229
  210.1 7.2 %collective-permute-start.8 = (bf16[64,512]{1,0:T(8,128)(2,1)S(1)}, bf16[64,512]{1,0:T(8,128)(2,1)S(1)}, u32[]{:S(2)}, u32[]{:S(2)}) collective-permute-start(bf16[64,512]{1,0:T(8,128)(2,1)S(1)} %get-tuple-element.36), channel_id=1, source_target_pairs={{0,4},{4,8},{8,12},{12,16},{16,20},{20,24},{24,28},{28,0},{1,5},{5... | collective-permute-start | bytes 196616 | tf_op jit(solution)/shard_map/ppermute | solution.py:250
  217.3 10.9 %collective-permute-start.12 = (bf16[64,512]{1,0:T(8,128)(2,1)S(1)}, bf16[64,512]{1,0:T(8,128)(2,1)S(1)}, u32[]{:S(2)}, u32[]{:S(2)}) collective-permute-start(bf16[64,512]{1,0:T(8,128)(2,1)S(1)} %get-tuple-element.37), channel_id=1, source_target_pairs={{0,28},{4,0},{8,4},{12,8},{16,12},{20,16},{24,20},{28,24},{1,29},{... | collective-permute-start | bytes 196616 | tf_op jit(solution)/shard_map/ppermute | solution.py:251
  228.3 4.1 %collective-permute-done.8 = bf16[64,512]{1,0:T(8,128)(2,1)S(1)} collective-permute-done((bf16[64,512]{1,0:T(8,128)(2,1)S(1)}, bf16[64,512]{1,0:T(8,128)(2,1)S(1)}, u32[]{:S(2)}, u32[]{:S(2)}) %collective-permute-start.8) | collective-permute-done | bytes 65568 | tf_op jit(solution)/shard_map/ppermute | solution.py:250
  233.3 1.9 collective-permute-start.9
  235.2 9.5 %collective-permute-done.9 = bf16[64,512]{1,0:T(8,128)(2,1)S(1)} collective-permute-done((bf16[64,512]{1,0:T(8,128)(2,1)S(1)}, bf16[64,512]{1,0:T(8,128)(2,1)S(1)}, u32[]{:S(2)}, u32[]{:S(2)}) %collective-permute-start.9) | collective-permute-done | bytes 65568 | tf_op jit(solution)/shard_map/ppermute | solution.py:254
  245.6 1.9 collective-permute-start.10
  247.5 7.8 %collective-permute-start.13 = (bf16[64,512]{1,0:T(8,128)(2,1)S(1)}, bf16[64,512]{1,0:T(8,128)(2,1)S(1)}, u32[]{:S(2)}, u32[]{:S(2)}) collective-permute-start(bf16[64,512]{1,0:T(8,128)(2,1)S(1)} %get-tuple-element.35), channel_id=1, source_target_pairs={{0,28},{4,0},{8,4},{12,8},{16,12},{20,16},{24,20},{28,24},{1,29},{... | collective-permute-start | bytes 196616 | tf_op jit(solution)/shard_map/ppermute | solution.py:257
  259.1 7.3 %collective-permute-start.14 = (bf16[64,512]{1,0:T(8,128)(2,1)S(1)}, bf16[64,512]{1,0:T(8,128)(2,1)S(1)}, u32[]{:S(2)}, u32[]{:S(2)}) collective-permute-start(bf16[64,512]{1,0:T(8,128)(2,1)S(1)} %get-tuple-element.33), channel_id=1, source_target_pairs={{0,28},{4,0},{8,4},{12,8},{16,12},{20,16},{24,20},{28,24},{1,29},{... | collective-permute-start | bytes 196616 | tf_op jit(solution)/shard_map/ppermute | solution.py:257
  266.5 2.4 collective-permute-start.11
  269.4 7.2 %collective-permute-done.11 = bf16[64,512]{1,0:T(8,128)(2,1)S(1)} collective-permute-done((bf16[64,512]{1,0:T(8,128)(2,1)S(1)}, bf16[64,512]{1,0:T(8,128)(2,1)S(1)}, u32[]{:S(2)}, u32[]{:S(2)}) %collective-permute-start.11) | collective-permute-done | bytes 65568 | tf_op jit(solution)/shard_map/ppermute | solution.py:254
  (52 shorter events, 19.7 us)
Async XLA Ops:
  4.0 20.1 %copy-start.1 = (bf16[2048,256]{1,0:T(8,128)(2,1)}, bf16[2048,256]{1,0:T(8,128)(2,1)S(1)}, u32[]{:S(2)}) copy-start(bf16[2048,256]{1,0:T(8,128)(2,1)S(1)} %get-tuple-element.26.refs_0_) | copy-start | bytes 3145732
  4.0 25.3 %copy-start = (bf16[2048,256]{1,0:T(8,128)(2,1)}, bf16[2048,256]{1,0:T(8,128)(2,1)S(1)}, u32[]{:S(2)}) copy-start(bf16[2048,256]{1,0:T(8,128)(2,1)S(1)} %get-tuple-element.25.refs_1_) | copy-start | bytes 3145732
  5.2 76.6 %collective-permute-start = (bf16[2304,256]{1,0:T(8,128)(2,1)}, bf16[2304,256]{1,0:T(8,128)(2,1)}, u32[]{:S(2)}, u32[]{:S(2)}) collective-permute-start(bf16[2304,256]{1,0:T(8,128)(2,1)} %pad_maximum_fusion.2), channel_id=1, source_target_pairs={{0,256},{256,512},{512,768},{768,0},{1,257},{257,513},{513,769},{7... | collective-permute-start | bytes 3538952 | tf_op jit(solution)/shard_map/ppermute | solution.py:155
  22.2 63.9 %collective-permute-start.2 = (bf16[2560,256]{1,0:T(8,128)(2,1)}, bf16[2560,256]{1,0:T(8,128)(2,1)S(1)}, u32[]{:S(2)}, u32[]{:S(2)}) collective-permute-start(bf16[2560,256]{1,0:T(8,128)(2,1)} %pad_maximum_fusion), channel_id=1, source_target_pairs={{0,256},{256,512},{512,768},{768,0},{1,257},{257,513},{513,769},{7... | collective-permute-start | bytes 3932168 | tf_op jit(solution)/shard_map/ppermute | solution.py:157
  25.2 7.2 %copy-start.8 = (f32[64,8]{0,1:T(8,128)S(1)}, f32[64,8]{0,1:T(8,128)}, u32[]{:S(2)}) copy-start(f32[64,8]{0,1:T(8,128)} %param.8) | copy-start | bytes 6148
  25.3 7.2 %copy-start.9 = (s32[64,8]{0,1:T(8,128)S(1)}, s32[64,8]{0,1:T(8,128)}, u32[]{:S(2)}) copy-start(s32[64,8]{0,1:T(8,128)} %param.7) | copy-start | bytes 6148
  25.3 7.3 %copy-start.7 = (bf16[64,512]{1,0:T(8,128)(2,1)S(1)}, bf16[64,512]{1,0:T(8,128)(2,1)}, u32[]{:S(2)}) copy-start(bf16[64,512]{1,0:T(8,128)(2,1)} %param.6) | copy-start | bytes 196612
  25.3 60.8 %collective-permute-start.3 = (bf16[2560,256]{1,0:T(8,128)(2,1)}, bf16[2560,256]{1,0:T(8,128)(2,1)}, u32[]{:S(2)}, u32[]{:S(2)}) collective-permute-start(bf16[2560,256]{1,0:T(8,128)(2,1)} %pad_maximum_fusion.1), channel_id=1, source_target_pairs={{0,768},{256,0},{512,256},{768,512},{1,769},{257,1},{513,257},{769... | collective-permute-start | bytes 3932168 | tf_op jit(solution)/shard_map/ppermute | solution.py:158
  30.5 51.3 %collective-permute-start.1 = (bf16[2304,256]{1,0:T(8,128)(2,1)}, bf16[2304,256]{1,0:T(8,128)(2,1)S(1)}, u32[]{:S(2)}, u32[]{:S(2)}) collective-permute-start(bf16[2304,256]{1,0:T(8,128)(2,1)} %pad_maximum_fusion.3), channel_id=1, source_target_pairs={{0,768},{256,0},{512,256},{768,512},{1,769},{257,1},{513,257},{769... | collective-permute-start | bytes 3538952 | tf_op jit(solution)/shard_map/ppermute | solution.py:156
  81.8 4.3 %copy-start.5 = (bf16[2304,256]{1,0:T(8,128)(2,1)}, bf16[2304,256]{1,0:T(8,128)(2,1)S(1)}, u32[]{:S(2)}) copy-start(bf16[2304,256]{1,0:T(8,128)(2,1)S(1)} %collective-permute-done.1.refs_5_) | copy-start | bytes 3538948
  86.1 43.6 %copy-start.2 = (bf16[2560,256]{1,0:T(8,128)(2,1)}, bf16[2560,256]{1,0:T(8,128)(2,1)S(1)}, u32[]{:S(2)}) copy-start(bf16[2560,256]{1,0:T(8,128)(2,1)S(1)} %collective-permute-done.2.refs_3_.prev) | copy-start | bytes 3932164
  86.1 31.7 %all-to-all-start = ((bf16[64,16,512]{2,1,0:T(8,128)(2,1)}), bf16[64,16,512]{2,1,0:T(8,128)(2,1)}, u32[]{:S(2)}, u32[]{:S(2)}) async-start(bf16[64,16,512]{2,1,0:T(8,128)(2,1)} %bitcast.59), calls=%async_computation | async-start | bytes 2097152 | tf_op jit(solution)/shard_map/all_to_all | solution.py:192
  95.4 33.3 %collective-permute-start.5 = (bf16[2304,256]{1,0:T(8,128)(2,1)}, bf16[2304,256]{1,0:T(8,128)(2,1)S(1)}, u32[]{:S(2)}, u32[]{:S(2)}) collective-permute-start(bf16[2304,256]{1,0:T(8,128)(2,1)} %collective-permute-done.refs_2_), channel_id=1, source_target_pairs={{0,256},{256,512},{512,768},{768,0},{1,257},{257,513},{513,769},{7... | collective-permute-start | bytes 3538952 | tf_op jit(solution)/shard_map/ppermute | solution.py:170
  97.6 32.0 %collective-permute-start.6 = (bf16[2304,256]{1,0:T(8,128)(2,1)}, bf16[2304,256]{1,0:T(8,128)(2,1)}, u32[]{:S(2)}, u32[]{:S(2)}) collective-permute-start(bf16[2304,256]{1,0:T(8,128)(2,1)} %copy-done.5), channel_id=1, source_target_pairs={{0,768},{256,0},{512,256},{768,512},{1,769},{257,1},{513,257},{769... | collective-permute-start | bytes 3538952 | tf_op jit(solution)/shard_map/ppermute | solution.py:171
  117.8 11.9 %collective-permute-start.4 = (bf16[4,256,512]{2,1,0:T(8,128)(2,1)}, bf16[4,256,512]{2,1,0:T(8,128)(2,1)S(1)}, u32[]{:S(2)}, u32[]{:S(2)}) collective-permute-start(bf16[4,256,512]{2,1,0:T(8,128)(2,1)} %bitcast.16.own_x), channel_id=1, source_target_pairs={{0,128},{128,0},{1,129},{129,1},{2,130},{130,2},{3,131},{131,3},{4... | collective-permute-start | bytes 3145736 | tf_op jit(solution)/shard_map/ppermute | solution.py:195
  128.6 1.0 copy-start.3
  129.6 1.0 copy-start.6
  162.7 4.8 %collective-permute-start.7 = (bf16[16,4,16,512]{3,2,1,0:T(8,128)(2,1)}, bf16[16,4,16,512]{3,2,1,0:T(8,128)(2,1)S(1)}, u32[]{:S(2)}, u32[]{:S(2)}) collective-permute-start(bf16[16,4,16,512]{3,2,1,0:T(8,128)(2,1)} %get-tuple-element.24), channel_id=1, source_target_pairs={{0,128},{128,0},{1,129},{129,1},{2,130},{130,2},{3,131},{131,3},{4... | collective-permute-start | bytes 3145736 | tf_op jit(solution)/shard_map/ppermute | solution.py:224
  170.1 34.4 %all-to-all-start.2 = ((bf16[16,64,512]{2,1,0:T(8,128)(2,1)}), bf16[16,64,512]{2,1,0:T(8,128)(2,1)S(1)}, u32[]{:S(2)}, u32[]{:S(2)}) async-start(bf16[16,64,512]{2,1,0:T(8,128)(2,1)} %bitcast.18), calls=%async_computation.2 | async-start | bytes 2097152 | tf_op jit(solution)/shard_map/all_to_all | solution.py:226
  204.5 1.0 copy-start.4
  210.1 22.3 %collective-permute-start.8 = (bf16[64,512]{1,0:T(8,128)(2,1)S(1)}, bf16[64,512]{1,0:T(8,128)(2,1)S(1)}, u32[]{:S(2)}, u32[]{:S(2)}) collective-permute-start(bf16[64,512]{1,0:T(8,128)(2,1)S(1)} %get-tuple-element.36), channel_id=1, source_target_pairs={{0,4},{4,8},{8,12},{12,16},{16,20},{20,24},{24,28},{28,0},{1,5},{5... | collective-permute-start | bytes 196616 | tf_op jit(solution)/shard_map/ppermute | solution.py:250
  217.3 17.9 %collective-permute-start.12 = (bf16[64,512]{1,0:T(8,128)(2,1)S(1)}, bf16[64,512]{1,0:T(8,128)(2,1)S(1)}, u32[]{:S(2)}, u32[]{:S(2)}) collective-permute-start(bf16[64,512]{1,0:T(8,128)(2,1)S(1)} %get-tuple-element.37), channel_id=1, source_target_pairs={{0,28},{4,0},{8,4},{12,8},{16,12},{20,16},{24,20},{28,24},{1,29},{... | collective-permute-start | bytes 196616 | tf_op jit(solution)/shard_map/ppermute | solution.py:251
  233.3 11.4 %collective-permute-start.9 = (bf16[64,512]{1,0:T(8,128)(2,1)S(1)}, bf16[64,512]{1,0:T(8,128)(2,1)S(1)}, u32[]{:S(2)}, u32[]{:S(2)}) collective-permute-start(bf16[64,512]{1,0:T(8,128)(2,1)S(1)} %fusion.6), channel_id=1, source_target_pairs={{0,4},{4,8},{8,12},{12,16},{16,20},{20,24},{24,28},{28,0},{1,5},{5... | collective-permute-start | bytes 196616 | tf_op jit(solution)/shard_map/ppermute | solution.py:254
  245.6 10.9 %collective-permute-start.10 = (bf16[64,512]{1,0:T(8,128)(2,1)S(1)}, bf16[64,512]{1,0:T(8,128)(2,1)S(1)}, u32[]{:S(2)}, u32[]{:S(2)}) collective-permute-start(bf16[64,512]{1,0:T(8,128)(2,1)S(1)} %get-tuple-element.34), channel_id=1, source_target_pairs={{0,4},{4,8},{8,12},{12,16},{16,20},{20,24},{24,28},{28,0},{1,5},{5... | collective-permute-start | bytes 196616 | tf_op jit(solution)/shard_map/ppermute | solution.py:254
  247.5 10.7 %collective-permute-start.13 = (bf16[64,512]{1,0:T(8,128)(2,1)S(1)}, bf16[64,512]{1,0:T(8,128)(2,1)S(1)}, u32[]{:S(2)}, u32[]{:S(2)}) collective-permute-start(bf16[64,512]{1,0:T(8,128)(2,1)S(1)} %get-tuple-element.35), channel_id=1, source_target_pairs={{0,28},{4,0},{8,4},{12,8},{16,12},{20,16},{24,20},{28,24},{1,29},{... | collective-permute-start | bytes 196616 | tf_op jit(solution)/shard_map/ppermute | solution.py:257
  259.1 10.2 %collective-permute-start.14 = (bf16[64,512]{1,0:T(8,128)(2,1)S(1)}, bf16[64,512]{1,0:T(8,128)(2,1)S(1)}, u32[]{:S(2)}, u32[]{:S(2)}) collective-permute-start(bf16[64,512]{1,0:T(8,128)(2,1)S(1)} %get-tuple-element.33), channel_id=1, source_target_pairs={{0,28},{4,0},{8,4},{12,8},{16,12},{20,16},{24,20},{28,24},{1,29},{... | collective-permute-start | bytes 196616 | tf_op jit(solution)/shard_map/ppermute | solution.py:257
  266.5 10.1 %collective-permute-start.11 = (bf16[64,512]{1,0:T(8,128)(2,1)S(1)}, bf16[64,512]{1,0:T(8,128)(2,1)S(1)}, u32[]{:S(2)}, u32[]{:S(2)}) collective-permute-start(bf16[64,512]{1,0:T(8,128)(2,1)S(1)} %get-tuple-element.32), channel_id=1, source_target_pairs={{0,4},{4,8},{8,12},{12,16},{16,20},{20,24},{24,28},{28,0},{1,5},{5... | collective-permute-start | bytes 196616 | tf_op jit(solution)/shard_map/ppermute | solution.py:254

commit v6 on v4

--- a/solution.py
+++ b/solution.py
@@ -50,16 +50,13 @@
     ).astype(BF)
 
 
-def expert_kernel(
-    core_ref, own_x, other_x, *refs
-):
-    parts, (keep_ref, send_ref, weights, rows, hidden, total, sems) = refs[:-7], refs[-7:]
-    n_x, n_rows, piece = own_x.shape
+def expert_work(core_ref, own_x, other_x, parts, weights, rows, hidden, sems):
+    n_x, _, piece = own_x.shape
     d_model = rows.shape[1]
-    width = weights.shape[2]
+    blocks, _, width = weights.shape
     ff = width // 2
+    half = parts[0].shape[0]
     core = core_ref[0]
-    half = parts[0].shape[0]
     copies = [
         pltpu.make_async_copy(
             part, weights.at[i // 2, (i % 2) * half : (i % 2 + 1) * half], sems.at[i]
@@ -73,7 +70,7 @@
         rows[:, pl.ds(at, piece)] = own_x[x]
         at = pl.multiple_of((2 * x + 1 - core) * piece, piece)
         rows[:, pl.ds(at, piece)] = other_x[x]
-    for b in range(n_x):
+    for b in range(blocks):
         copies[2 * b].wait()
         copies[2 * b + 1].wait()
         both = jnp.dot(rows[...], weights[b, :d_model, :], preferred_element_type=F32)
@@ -81,12 +78,24 @@
         hidden[:, b * ff : (b + 1) * ff] = (gate / (1.0 + jnp.exp(-gate)) * up).astype(BF)
     for n in range(d_model // width):
         at = d_model + n * ff
-        down = jnp.concatenate(
-            [weights[b, at : at + ff, :] for b in range(n_x)], axis=0
+        down = jnp.concatenate([weights[b, at : at + ff, :] for b in range(blocks)], axis=0)
+        yield slice(n * width, (n + 1) * width), jnp.dot(
+            hidden[...], down, preferred_element_type=F32
         )
-        total[:, n * width : (n + 1) * width] = jnp.dot(
-            hidden[...], down, preferred_element_type=F32
-        ).astype(BF)
+
+
+def near_kernel(core_ref, own_x, other_x, *refs):
+    parts, (total_ref, weights, rows, hidden, sems) = refs[:-5], refs[-5:]
+    for at, term in expert_work(core_ref, own_x, other_x, parts, weights, rows, hidden, sems):
+        total_ref[:, at] = term
+
+
+def far_kernel(core_ref, own_x, other_x, near_ref, *refs):
+    parts, (keep_ref, send_ref, weights, rows, hidden, total, sems) = refs[:-7], refs[-7:]
+    n_x, _, piece = own_x.shape
+    core = core_ref[0]
+    for at, term in expert_work(core_ref, own_x, other_x, parts, weights, rows, hidden, sems):
+        total[:, at] = (near_ref[:, at] + term).astype(BF)
     for x in range(n_x):
         at = pl.multiple_of((2 * x + core) * piece, piece)
         keep_ref[x] = total[:, pl.ds(at, piece)]
@@ -163,21 +172,32 @@
         rows.reshape(-1, pair * CAP, piece), peers, split_axis=0, concat_axis=0, tiled=True
     ).reshape(n_x, slots, piece)
     other_x = lax.ppermute(own_x, "core", swap)
+    def scratch(blocks):
+        return [
+            pltpu.VMEM((blocks,) + own_w.shape, BF),
+            pltpu.VMEM((slots, d_model), BF),
+            pltpu.VMEM((slots, blocks * ff), BF),
+        ]
+
+    near_sum = pl.pallas_call(
+        near_kernel,
+        in_specs=[smem, vmem, vmem] + [hbm] * 6,
+        out_specs=vmem,
+        out_shape=jax.ShapeDtypeStruct((slots, d_model), F32),
+        scratch_shapes=scratch(3) + [pltpu.SemaphoreType.DMA((6,))],
+        compiler_params=params,
+        name="near",
+    )(core, own_x, other_x, own_a, own_b, prev_a, prev_b, next_a, next_b)
     keep, send = pl.pallas_call(
-        expert_kernel,
-        in_specs=[smem, vmem, vmem] + [hbm] * (2 * n_x),
+        far_kernel,
+        in_specs=[smem, vmem, vmem, vmem] + [hbm] * 2,
         out_specs=[vmem, vmem],
         out_shape=[jax.ShapeDtypeStruct(own_x.shape, BF)] * 2,
-        scratch_shapes=[
-            pltpu.VMEM((n_x,) + own_w.shape, BF),
-            pltpu.VMEM((slots, d_model), BF),
-            pltpu.VMEM((slots, n_x * ff), BF),
-            pltpu.VMEM((slots, d_model), BF),
-            pltpu.SemaphoreType.DMA((2 * n_x,)),
-        ],
-        compiler_params=params,
-        name="expert",
-    )(core, own_x, other_x, own_a, own_b, prev_a, prev_b, next_a, next_b, far_a, far_b)
+        scratch_shapes=scratch(1)
+        + [pltpu.VMEM((slots, d_model), BF), pltpu.SemaphoreType.DMA((2,))],
+        compiler_params=params,
+        name="far",
+    )(core, own_x, other_x, near_sum, far_a, far_b)
     got = lax.ppermute(send, "core", swap)
     out = (keep.astype(F32) + got.astype(F32)).astype(BF)
     back = lax.all_to_all(

time: 271 us -> 269 us (level)
  waiting for transfers between devices: 94.5 us -> 82.8 us
  Pallas kernels: 18.8 us -> 27.2 us
    ppermute x1, waiting for transfers between devices: 17.8 us -> 3.37 us  [shards(): far_a = lax.ppermute(prev_a, 'x', up_x)]
    pallas_call x1 -> x2, Pallas kernels: 11 us -> 19.4 us  [the longest x1 10.8 us: shards(): pl.pallas_call(near_kernel, in_specs=[smem, vmem, vmem] + [hbm] * 6, out_...]
  transfers between devices with their start and end apart: 17 -> 17, of which waited for: 10 -> 11; matrix products, arithmetic and copies ran while one was open for 0% -> 0% of each run, Pallas kernels for 2% -> 6%
where the time goes in v6:
time: 269 us; the launch traced here: 268 us
  waiting for transfers between devices  82.8 us (31%)
  starting transfers between devices  82.1 us (31%)
  blocking collectives  61 us (23%)
  Pallas kernels  27.2 us (10%)
  other arithmetic  8.21 us (3%)
  local copies, waits for them, and re-layouts  5.92 us (2%)
    all_gather x1, blocking collectives, shards(): lax.all_gather(jnp.concatenate([tokens, meta], axis=0), 'high', axis=0, t...  61 us
    all_to_all x1, waiting for transfers between devices, shards(): lax.all_to_all(out.reshape(-1, pair * CAP, piece), peers, split_axis=0, c...  28.8 us
    all_to_all x1, waiting for transfers between devices, shards(): lax.all_to_all(rows.reshape(-1, pair * CAP, piece), peers, split_axis=0,...  20.3 us
    ppermute x3, waiting for transfers between devices, shards(): rising = lax.ppermute(rising, 'high', up_z)  16.6 us
    ppermute x2, starting transfers between devices, shards(): falling = lax.ppermute(falling, 'high', down_z)  14.4 us
    pallas_call x1, Pallas kernels, shards(): pl.pallas_call(near_kernel, in_specs=[smem, vmem, vmem] + [hbm] * 6, out_...  10.8 us
    ppermute x1, starting transfers between devices, shards(): falling = lax.ppermute(mine_for(reach + 1).astype(BF), 'high', down_z)  10.1 us
    ppermute x1, starting transfers between devices, shards(): rising = lax.ppermute(mine_for(reach).astype(BF), 'high', up_z)  9.1 us
  transfers between devices with their start and end apart: 17, of which 11 were waited for; matrix products, arithmetic and copies ran while one was open for 0% of the time, Pallas kernels for 6%

profile of v6, /device:TPU:8, one launch (start us, length us, event | category | flops | bytes accessed | tf_op | source)
XLA Modules:
  0.0 267.6 jit_solution(458877422270993543)
XLA Ops:
  4.5 3.4 %collective-permute-start = (bf16[3072,256]{1,0:T(8,128)(2,1)}, bf16[3072,256]{1,0:T(8,128)(2,1)}, u32[]{:S(2)}, u32[]{:S(2)}) collective-permute-start(bf16[3072,256]{1,0:T(8,128)(2,1)} %get-tuple-element.26.refs_0_), channel_id=1, source_target_pairs={{0,256},{256,512},{512,768},{768,0},{1,257},{257,513},{513,769},{7... | collective-permute-start | bytes 4718600 | tf_op jit(solution)/shard_map/ppermute | solution.py:134
  7.9 3.7 %collective-permute-start.1 = (bf16[3072,256]{1,0:T(8,128)(2,1)S(1)}, bf16[3072,256]{1,0:T(8,128)(2,1)}, u32[]{:S(2)}, u32[]{:S(2)}) collective-permute-start(bf16[3072,256]{1,0:T(8,128)(2,1)S(1)} %get-tuple-element.25.refs_1_), channel_id=1, source_target_pairs={{0,768},{256,0},{512,256},{768,512},{1,769},{257,1},{513,257},{769... | collective-permute-start | bytes 4718600 | tf_op jit(solution)/shard_map/ppermute | solution.py:135
  11.6 2.2 collective-permute-start.2
  13.8 4.9 %collective-permute-start.3 = (bf16[3072,256]{1,0:T(8,128)(2,1)}, bf16[3072,256]{1,0:T(8,128)(2,1)}, u32[]{:S(2)}, u32[]{:S(2)}) collective-permute-start(bf16[3072,256]{1,0:T(8,128)(2,1)} %get-tuple-element.26.refs_0_), channel_id=1, source_target_pairs={{0,768},{256,0},{512,256},{768,512},{1,769},{257,1},{513,257},{769... | collective-permute-start | bytes 4718600 | tf_op jit(solution)/shard_map/ppermute | solution.py:137
  18.9 61.0 %all-gather = bf16[640,512]{1,0:T(8,128)(2,1)} all-gather(bf16[80,512]{1,0:T(8,128)(2,1)S(1)} %fusion.8), channel_id=2, replica_groups=mesh['x'=4,'core'=2,'narrow'=4,'high'=8,'low'=4] {'high'}, dimensions={0}, use_global_device_ids=true | all-gather | bytes 737280 | tf_op jit(solution)/shard_map/all_gather | solution.py:145
  79.9 4.0 %select.32 = (bf16[4,256,512]{2,1,0:T(8,128)(2,1)}, bf16[4,256,128]{2,1,0:T(8,128)(2,1)}) custom-call(s32[1]{0:T(128)} %bitcast.refs_0_, bf16[8,80,512]{2,1,0:T(8,128)(2,1)} %bitcast.48), custom_call_target="tpu_custom_call" | custom-call | tf_op jit(solution)/shard_map/select/pallas_call | solution.py:154
  84.0 7.5 %all-to-all-start = ((bf16[64,16,512]{2,1,0:T(8,128)(2,1)}), bf16[64,16,512]{2,1,0:T(8,128)(2,1)S(1)}, u32[]{:S(2)}, u32[]{:S(2)}) async-start(bf16[64,16,512]{2,1,0:T(8,128)(2,1)} %bitcast.55), calls=%async_computation | async-start | bytes 2097152 | tf_op jit(solution)/shard_map/all_to_all | solution.py:171
  91.4 3.4 %collective-permute-start.5 = (bf16[3072,256]{1,0:T(8,128)(2,1)}, bf16[3072,256]{1,0:T(8,128)(2,1)}, u32[]{:S(2)}, u32[]{:S(2)}) collective-permute-start(bf16[3072,256]{1,0:T(8,128)(2,1)} %collective-permute-done.refs_2_), channel_id=1, source_target_pairs={{0,256},{256,512},{512,768},{768,0},{1,257},{257,513},{513,769},{7... | collective-permute-start | bytes 4718600 | tf_op jit(solution)/shard_map/ppermute | solution.py:149
  94.8 3.7 %collective-permute-start.6 = (bf16[3072,256]{1,0:T(8,128)(2,1)}, bf16[3072,256]{1,0:T(8,128)(2,1)}, u32[]{:S(2)}, u32[]{:S(2)}) collective-permute-start(bf16[3072,256]{1,0:T(8,128)(2,1)} %collective-permute-done.1.refs_5_), channel_id=1, source_target_pairs={{0,768},{256,0},{512,256},{768,512},{1,769},{257,1},{513,257},{769... | collective-permute-start | bytes 4718600 | tf_op jit(solution)/shard_map/ppermute | solution.py:150
  98.5 20.3 %all-to-all-done = bf16[64,16,512]{2,1,0:T(8,128)(2,1)S(1)} async-done(((bf16[64,16,512]{2,1,0:T(8,128)(2,1)}), bf16[64,16,512]{2,1,0:T(8,128)(2,1)S(1)}, u32[]{:S(2)}, u32[]{:S(2)}) %all-to-all-start) | async-done | bytes 1048608 | tf_op jit(solution)/shard_map/all_to_all | solution.py:171
  118.9 1.9 collective-permute-start.4
  120.8 2.6 collective-permute-done.4.other_x
  124.4 10.8 %near.1.near_ref = f32[256,4096]{1,0:T(8,128)} custom-call(s32[1]{0:T(128)} %bitcast.8.core_ref, bf16[4,256,512]{2,1,0:T(8,128)(2,1)} %bitcast.43, bf16[4,256,512]{2,1,0:T(8,128)(2,1)} %copy-done.2, bf16[3072,256]{1,0:T(8,128)(2,1)} %get-tuple-element.26.refs_0_, bf16[3072,256]{1,0:T(8,128)(2,1)} %copy-done.1, ...), custom_call_target="tpu_custom_call" | custom-call | tf_op jit(solution)/shard_map/near/pallas_call | solution.py:182
  135.2 3.4 %collective-permute-done.5.refs_0_ = bf16[3072,256]{1,0:T(8,128)(2,1)} collective-permute-done((bf16[3072,256]{1,0:T(8,128)(2,1)}, bf16[3072,256]{1,0:T(8,128)(2,1)}, u32[]{:S(2)}, u32[]{:S(2)}) %collective-permute-start.5) | collective-permute-done | bytes 1572896 | tf_op jit(solution)/shard_map/ppermute | solution.py:149
  138.6 8.6 %far.1 = (bf16[4,256,512]{2,1,0:T(8,128)(2,1)}, bf16[4,256,512]{2,1,0:T(8,128)(2,1)}) custom-call(s32[1]{0:T(128)} %bitcast.8.core_ref, bf16[4,256,512]{2,1,0:T(8,128)(2,1)} %bitcast.44, bf16[4,256,512]{2,1,0:T(8,128)(2,1)} %copy-done.2, f32[256,4096]{1,0:T(8,128)} %near.1.near_ref, bf16[3072,256]{1,0:T(8,128)(2,1)} %collective-permute-done.5.refs_0_, ...), custom_call_target="tpu_custom_call" | custom-call | tf_op jit(solution)/shard_map/far/pallas_call | solution.py:191
  147.2 1.9 collective-permute-start.7
  149.1 2.8 %collective-permute-done.7 = bf16[4,256,512]{2,1,0:T(8,128)(2,1)S(1)} collective-permute-done((bf16[4,256,512]{2,1,0:T(8,128)(2,1)}, bf16[4,256,512]{2,1,0:T(8,128)(2,1)S(1)}, u32[]{:S(2)}, u32[]{:S(2)}) %collective-permute-start.7) | collective-permute-done | bytes 1048608 | tf_op jit(solution)/shard_map/ppermute | solution.py:201
  151.9 2.5 add_convert_fusion
  154.4 9.0 %all-to-all-start.1 = ((bf16[64,16,512]{2,1,0:T(8,128)(2,1)}), bf16[64,16,512]{2,1,0:T(8,128)(2,1)S(1)}, u32[]{:S(2)}, u32[]{:S(2)}) async-start(bf16[64,16,512]{2,1,0:T(8,128)(2,1)} %bitcast.11), calls=%async_computation.1 | async-start | bytes 2097152 | tf_op jit(solution)/shard_map/all_to_all | solution.py:203
  163.4 28.8 %all-to-all-done.1 = bf16[64,16,512]{2,1,0:T(8,128)(2,1)S(1)} async-done(((bf16[64,16,512]{2,1,0:T(8,128)(2,1)}), bf16[64,16,512]{2,1,0:T(8,128)(2,1)S(1)}, u32[]{:S(2)}, u32[]{:S(2)}) %all-to-all-start.1) | async-done | bytes 1048608 | tf_op jit(solution)/shard_map/all_to_all | solution.py:203
  193.3 3.7 %combine.1 = bf16[4,128,512]{2,1,0:T(8,128)(2,1)} custom-call(bf16[4,256,128]{2,1,0:T(8,128)(2,1)} %get-tuple-element.16.weight_ref, bf16[4,256,512]{2,1,0:T(8,128)(2,1)} %bitcast.45), custom_call_target="tpu_custom_call" | custom-call | tf_op jit(solution)/shard_map/combine/pallas_call | solution.py:206
  197.9 9.1 %collective-permute-start.8 = (bf16[64,512]{1,0:T(8,128)(2,1)S(1)}, bf16[64,512]{1,0:T(8,128)(2,1)S(1)}, u32[]{:S(2)}, u32[]{:S(2)}) collective-permute-start(bf16[64,512]{1,0:T(8,128)(2,1)S(1)} %get-tuple-element.31), channel_id=1, source_target_pairs={{0,4},{4,8},{8,12},{12,16},{16,20},{20,24},{24,28},{28,0},{1,5},{5... | collective-permute-start | bytes 196616 | tf_op jit(solution)/shard_map/ppermute | solution.py:227
  207.0 10.1 %collective-permute-start.12 = (bf16[64,512]{1,0:T(8,128)(2,1)S(1)}, bf16[64,512]{1,0:T(8,128)(2,1)S(1)}, u32[]{:S(2)}, u32[]{:S(2)}) collective-permute-start(bf16[64,512]{1,0:T(8,128)(2,1)S(1)} %get-tuple-element.32), channel_id=1, source_target_pairs={{0,28},{4,0},{8,4},{12,8},{16,12},{20,16},{24,20},{28,24},{1,29},{... | collective-permute-start | bytes 196616 | tf_op jit(solution)/shard_map/ppermute | solution.py:228
  217.1 4.4 %collective-permute-done.8 = bf16[64,512]{1,0:T(8,128)(2,1)S(1)} collective-permute-done((bf16[64,512]{1,0:T(8,128)(2,1)S(1)}, bf16[64,512]{1,0:T(8,128)(2,1)S(1)}, u32[]{:S(2)}, u32[]{:S(2)}) %collective-permute-start.8) | collective-permute-done | bytes 65568 | tf_op jit(solution)/shard_map/ppermute | solution.py:227
  222.4 1.9 collective-permute-start.9
  224.4 9.2 %collective-permute-done.9 = bf16[64,512]{1,0:T(8,128)(2,1)S(1)} collective-permute-done((bf16[64,512]{1,0:T(8,128)(2,1)S(1)}, bf16[64,512]{1,0:T(8,128)(2,1)S(1)}, u32[]{:S(2)}, u32[]{:S(2)}) %collective-permute-start.9) | collective-permute-done | bytes 65568 | tf_op jit(solution)/shard_map/ppermute | solution.py:231
  234.5 2.4 collective-permute-start.10
  236.9 7.4 %collective-permute-start.13 = (bf16[64,512]{1,0:T(8,128)(2,1)S(1)}, bf16[64,512]{1,0:T(8,128)(2,1)S(1)}, u32[]{:S(2)}, u32[]{:S(2)}) collective-permute-start(bf16[64,512]{1,0:T(8,128)(2,1)S(1)} %get-tuple-element.30), channel_id=1, source_target_pairs={{0,28},{4,0},{8,4},{12,8},{16,12},{20,16},{24,20},{28,24},{1,29},{... | collective-permute-start | bytes 196616 | tf_op jit(solution)/shard_map/ppermute | solution.py:234
  244.6 3.5 %collective-permute-done.13 = bf16[64,512]{1,0:T(8,128)(2,1)S(1)} collective-permute-done((bf16[64,512]{1,0:T(8,128)(2,1)S(1)}, bf16[64,512]{1,0:T(8,128)(2,1)S(1)}, u32[]{:S(2)}, u32[]{:S(2)}) %collective-permute-start.13) | collective-permute-done | bytes 65568 | tf_op jit(solution)/shard_map/ppermute | solution.py:234
  249.0 7.0 %collective-permute-start.14 = (bf16[64,512]{1,0:T(8,128)(2,1)S(1)}, bf16[64,512]{1,0:T(8,128)(2,1)S(1)}, u32[]{:S(2)}, u32[]{:S(2)}) collective-permute-start(bf16[64,512]{1,0:T(8,128)(2,1)S(1)} %get-tuple-element.28), channel_id=1, source_target_pairs={{0,28},{4,0},{8,4},{12,8},{16,12},{20,16},{24,20},{28,24},{1,29},{... | collective-permute-start | bytes 196616 | tf_op jit(solution)/shard_map/ppermute | solution.py:234
  256.0 2.7 %collective-permute-start.11 = (bf16[64,512]{1,0:T(8,128)(2,1)S(1)}, bf16[64,512]{1,0:T(8,128)(2,1)S(1)}, u32[]{:S(2)}, u32[]{:S(2)}) collective-permute-start(bf16[64,512]{1,0:T(8,128)(2,1)S(1)} %get-tuple-element.27), channel_id=1, source_target_pairs={{0,4},{4,8},{8,12},{12,16},{16,20},{20,24},{24,28},{28,0},{1,5},{5... | collective-permute-start | bytes 196616 | tf_op jit(solution)/shard_map/ppermute | solution.py:231
  259.0 7.0 %collective-permute-done.11 = bf16[64,512]{1,0:T(8,128)(2,1)S(1)} collective-permute-done((bf16[64,512]{1,0:T(8,128)(2,1)S(1)}, bf16[64,512]{1,0:T(8,128)(2,1)S(1)}, u32[]{:S(2)}, u32[]{:S(2)}) %collective-permute-start.11) | collective-permute-done | bytes 65568 | tf_op jit(solution)/shard_map/ppermute | solution.py:231
  (42 shorter events, 12.2 us)
Async XLA Ops:
  1.5 1.2 copy-start.4
  1.5 1.5 copy-start.5
  3.0 15.7 %copy-start.7 = (f32[64,8]{0,1:T(8,128)S(1)}, f32[64,8]{0,1:T(8,128)}, u32[]{:S(2)}) copy-start(f32[64,8]{0,1:T(8,128)} %param.8) | copy-start | bytes 6148
  3.0 15.7 %copy-start.8 = (s32[64,8]{0,1:T(8,128)S(1)}, s32[64,8]{0,1:T(8,128)}, u32[]{:S(2)}) copy-start(s32[64,8]{0,1:T(8,128)} %param.7) | copy-start | bytes 6148
  3.0 15.8 %copy-start.6 = (bf16[64,512]{1,0:T(8,128)(2,1)S(1)}, bf16[64,512]{1,0:T(8,128)(2,1)}, u32[]{:S(2)}) copy-start(bf16[64,512]{1,0:T(8,128)(2,1)} %param.6) | copy-start | bytes 196612
  4.5 79.4 %copy-start.1 = (bf16[3072,256]{1,0:T(8,128)(2,1)}, bf16[3072,256]{1,0:T(8,128)(2,1)S(1)}, u32[]{:S(2)}) copy-start(bf16[3072,256]{1,0:T(8,128)(2,1)S(1)} %get-tuple-element.25.refs_1_) | copy-start | bytes 4718596
  4.5 75.4 %collective-permute-start = (bf16[3072,256]{1,0:T(8,128)(2,1)}, bf16[3072,256]{1,0:T(8,128)(2,1)}, u32[]{:S(2)}, u32[]{:S(2)}) collective-permute-start(bf16[3072,256]{1,0:T(8,128)(2,1)} %get-tuple-element.26.refs_0_), channel_id=1, source_target_pairs={{0,256},{256,512},{512,768},{768,0},{1,257},{257,513},{513,769},{7... | collective-permute-start | bytes 4718600 | tf_op jit(solution)/shard_map/ppermute | solution.py:134
  7.9 72.0 %collective-permute-start.1 = (bf16[3072,256]{1,0:T(8,128)(2,1)S(1)}, bf16[3072,256]{1,0:T(8,128)(2,1)}, u32[]{:S(2)}, u32[]{:S(2)}) collective-permute-start(bf16[3072,256]{1,0:T(8,128)(2,1)S(1)} %get-tuple-element.25.refs_1_), channel_id=1, source_target_pairs={{0,768},{256,0},{512,256},{768,512},{1,769},{257,1},{513,257},{769... | collective-permute-start | bytes 4718600 | tf_op jit(solution)/shard_map/ppermute | solution.py:135
  11.6 72.4 %collective-permute-start.2 = (bf16[3072,256]{1,0:T(8,128)(2,1)S(1)}, bf16[3072,256]{1,0:T(8,128)(2,1)}, u32[]{:S(2)}, u32[]{:S(2)}) collective-permute-start(bf16[3072,256]{1,0:T(8,128)(2,1)S(1)} %get-tuple-element.25.refs_1_), channel_id=1, source_target_pairs={{0,256},{256,512},{512,768},{768,0},{1,257},{257,513},{513,769},{7... | collective-permute-start | bytes 4718600 | tf_op jit(solution)/shard_map/ppermute | solution.py:136
  13.8 70.2 %collective-permute-start.3 = (bf16[3072,256]{1,0:T(8,128)(2,1)}, bf16[3072,256]{1,0:T(8,128)(2,1)}, u32[]{:S(2)}, u32[]{:S(2)}) collective-permute-start(bf16[3072,256]{1,0:T(8,128)(2,1)} %get-tuple-element.26.refs_0_), channel_id=1, source_target_pairs={{0,768},{256,0},{512,256},{768,512},{1,769},{257,1},{513,257},{769... | collective-permute-start | bytes 4718600 | tf_op jit(solution)/shard_map/ppermute | solution.py:137
  84.0 34.9 %all-to-all-start = ((bf16[64,16,512]{2,1,0:T(8,128)(2,1)}), bf16[64,16,512]{2,1,0:T(8,128)(2,1)S(1)}, u32[]{:S(2)}, u32[]{:S(2)}) async-start(bf16[64,16,512]{2,1,0:T(8,128)(2,1)} %bitcast.55), calls=%async_computation | async-start | bytes 2097152 | tf_op jit(solution)/shard_map/all_to_all | solution.py:171
  91.4 47.1 %collective-permute-start.5 = (bf16[3072,256]{1,0:T(8,128)(2,1)}, bf16[3072,256]{1,0:T(8,128)(2,1)}, u32[]{:S(2)}, u32[]{:S(2)}) collective-permute-start(bf16[3072,256]{1,0:T(8,128)(2,1)} %collective-permute-done.refs_2_), channel_id=1, source_target_pairs={{0,256},{256,512},{512,768},{768,0},{1,257},{257,513},{513,769},{7... | collective-permute-start | bytes 4718600 | tf_op jit(solution)/shard_map/ppermute | solution.py:149
  94.8 43.7 %collective-permute-start.6 = (bf16[3072,256]{1,0:T(8,128)(2,1)}, bf16[3072,256]{1,0:T(8,128)(2,1)}, u32[]{:S(2)}, u32[]{:S(2)}) collective-permute-start(bf16[3072,256]{1,0:T(8,128)(2,1)} %collective-permute-done.1.refs_5_), channel_id=1, source_target_pairs={{0,768},{256,0},{512,256},{768,512},{1,769},{257,1},{513,257},{769... | collective-permute-start | bytes 4718600 | tf_op jit(solution)/shard_map/ppermute | solution.py:150
  118.9 4.5 %copy-start = (bf16[64,16,512]{2,1,0:T(8,128)(2,1)}, bf16[64,16,512]{2,1,0:T(8,128)(2,1)S(1)}, u32[]{:S(2)}) copy-start(bf16[64,16,512]{2,1,0:T(8,128)(2,1)S(1)} %all-to-all-done) | copy-start | bytes 3145732
  118.9 4.5 %collective-permute-start.4 = (bf16[4,256,512]{2,1,0:T(8,128)(2,1)S(1)}, bf16[4,256,512]{2,1,0:T(8,128)(2,1)S(1)}, u32[]{:S(2)}, u32[]{:S(2)}) collective-permute-start(bf16[4,256,512]{2,1,0:T(8,128)(2,1)S(1)} %bitcast.42), channel_id=1, source_target_pairs={{0,128},{128,0},{1,129},{129,1},{2,130},{130,2},{3,131},{131,3},{4... | collective-permute-start | bytes 3145736 | tf_op jit(solution)/shard_map/ppermute | solution.py:174
  123.4 1.0 copy-start.2
  147.2 4.8 %collective-permute-start.7 = (bf16[4,256,512]{2,1,0:T(8,128)(2,1)}, bf16[4,256,512]{2,1,0:T(8,128)(2,1)S(1)}, u32[]{:S(2)}, u32[]{:S(2)}) collective-permute-start(bf16[4,256,512]{2,1,0:T(8,128)(2,1)} %get-tuple-element.24), channel_id=1, source_target_pairs={{0,128},{128,0},{1,129},{129,1},{2,130},{130,2},{3,131},{131,3},{4... | collective-permute-start | bytes 3145736 | tf_op jit(solution)/shard_map/ppermute | solution.py:201
  154.4 37.8 %all-to-all-start.1 = ((bf16[64,16,512]{2,1,0:T(8,128)(2,1)}), bf16[64,16,512]{2,1,0:T(8,128)(2,1)S(1)}, u32[]{:S(2)}, u32[]{:S(2)}) async-start(bf16[64,16,512]{2,1,0:T(8,128)(2,1)} %bitcast.11), calls=%async_computation.1 | async-start | bytes 2097152 | tf_op jit(solution)/shard_map/all_to_all | solution.py:203
  192.3 1.0 copy-start.3
  197.9 23.7 %collective-permute-start.8 = (bf16[64,512]{1,0:T(8,128)(2,1)S(1)}, bf16[64,512]{1,0:T(8,128)(2,1)S(1)}, u32[]{:S(2)}, u32[]{:S(2)}) collective-permute-start(bf16[64,512]{1,0:T(8,128)(2,1)S(1)} %get-tuple-element.31), channel_id=1, source_target_pairs={{0,4},{4,8},{8,12},{12,16},{16,20},{20,24},{24,28},{28,0},{1,5},{5... | collective-permute-start | bytes 196616 | tf_op jit(solution)/shard_map/ppermute | solution.py:227
  207.0 17.4 %collective-permute-start.12 = (bf16[64,512]{1,0:T(8,128)(2,1)S(1)}, bf16[64,512]{1,0:T(8,128)(2,1)S(1)}, u32[]{:S(2)}, u32[]{:S(2)}) collective-permute-start(bf16[64,512]{1,0:T(8,128)(2,1)S(1)} %get-tuple-element.32), channel_id=1, source_target_pairs={{0,28},{4,0},{8,4},{12,8},{16,12},{20,16},{24,20},{28,24},{1,29},{... | collective-permute-start | bytes 196616 | tf_op jit(solution)/shard_map/ppermute | solution.py:228
  222.4 11.2 %collective-permute-start.9 = (bf16[64,512]{1,0:T(8,128)(2,1)S(1)}, bf16[64,512]{1,0:T(8,128)(2,1)S(1)}, u32[]{:S(2)}, u32[]{:S(2)}) collective-permute-start(bf16[64,512]{1,0:T(8,128)(2,1)S(1)} %fusion.5), channel_id=1, source_target_pairs={{0,4},{4,8},{8,12},{12,16},{16,20},{20,24},{24,28},{28,0},{1,5},{5... | collective-permute-start | bytes 196616 | tf_op jit(solution)/shard_map/ppermute | solution.py:231
  234.5 10.1 %collective-permute-start.10 = (bf16[64,512]{1,0:T(8,128)(2,1)S(1)}, bf16[64,512]{1,0:T(8,128)(2,1)S(1)}, u32[]{:S(2)}, u32[]{:S(2)}) collective-permute-start(bf16[64,512]{1,0:T(8,128)(2,1)S(1)} %get-tuple-element.29), channel_id=1, source_target_pairs={{0,4},{4,8},{8,12},{12,16},{16,20},{20,24},{24,28},{28,0},{1,5},{5... | collective-permute-start | bytes 196616 | tf_op jit(solution)/shard_map/ppermute | solution.py:231
  236.9 11.2 %collective-permute-start.13 = (bf16[64,512]{1,0:T(8,128)(2,1)S(1)}, bf16[64,512]{1,0:T(8,128)(2,1)S(1)}, u32[]{:S(2)}, u32[]{:S(2)}) collective-permute-start(bf16[64,512]{1,0:T(8,128)(2,1)S(1)} %get-tuple-element.30), channel_id=1, source_target_pairs={{0,28},{4,0},{8,4},{12,8},{16,12},{20,16},{24,20},{28,24},{1,29},{... | collective-permute-start | bytes 196616 | tf_op jit(solution)/shard_map/ppermute | solution.py:234
  249.0 10.1 %collective-permute-start.14 = (bf16[64,512]{1,0:T(8,128)(2,1)S(1)}, bf16[64,512]{1,0:T(8,128)(2,1)S(1)}, u32[]{:S(2)}, u32[]{:S(2)}) collective-permute-start(bf16[64,512]{1,0:T(8,128)(2,1)S(1)} %get-tuple-element.28), channel_id=1, source_target_pairs={{0,28},{4,0},{8,4},{12,8},{16,12},{20,16},{24,20},{28,24},{1,29},{... | collective-permute-start | bytes 196616 | tf_op jit(solution)/shard_map/ppermute | solution.py:234
  256.0 10.1 %collective-permute-start.11 = (bf16[64,512]{1,0:T(8,128)(2,1)S(1)}, bf16[64,512]{1,0:T(8,128)(2,1)S(1)}, u32[]{:S(2)}, u32[]{:S(2)}) collective-permute-start(bf16[64,512]{1,0:T(8,128)(2,1)S(1)} %get-tuple-element.27), channel_id=1, source_target_pairs={{0,4},{4,8},{8,12},{12,16},{16,20},{20,24},{24,28},{28,0},{1,5},{5... | collective-permute-start | bytes 196616 | tf_op jit(solution)/shard_map/ppermute | solution.py:231

commit v7 on v6

--- a/solution.py
+++ b/solution.py
@@ -87,7 +87,7 @@
 def near_kernel(core_ref, own_x, other_x, *refs):
     parts, (total_ref, weights, rows, hidden, sems) = refs[:-5], refs[-5:]
     for at, term in expert_work(core_ref, own_x, other_x, parts, weights, rows, hidden, sems):
-        total_ref[:, at] = term
+        total_ref[:, at] = term.astype(BF)
 
 
 def far_kernel(core_ref, own_x, other_x, near_ref, *refs):
@@ -95,7 +95,7 @@
     n_x, _, piece = own_x.shape
     core = core_ref[0]
     for at, term in expert_work(core_ref, own_x, other_x, parts, weights, rows, hidden, sems):
-        total[:, at] = (near_ref[:, at] + term).astype(BF)
+        total[:, at] = (near_ref[:, at].astype(F32) + term).astype(BF)
     for x in range(n_x):
         at = pl.multiple_of((2 * x + core) * piece, piece)
         keep_ref[x] = total[:, pl.ds(at, piece)]
@@ -119,18 +119,20 @@
     up_x = [(i, (i + 1) % n_x) for i in range(n_x)]
     down_x = [(i, (i - 1) % n_x) for i in range(n_x)]
 
-    own_w = jnp.concatenate(
+    width = 2 * ff
+    half = (d_model + d_model // 2) // 2
+    gate, up = gate_weight[0], up_weight[0]
+    own_a = jnp.concatenate([gate[:half], up[:half]], axis=1)
+    own_b = jnp.concatenate(
         [
-            jnp.concatenate([gate_weight[0], up_weight[0]], axis=1),
+            jnp.concatenate([gate[half:], up[half:]], axis=1),
             down_weight[0]
-            .reshape(ff, d_model // (2 * ff), 2 * ff)
+            .reshape(ff, d_model // width, width)
             .transpose(1, 0, 2)
-            .reshape(d_model // 2, 2 * ff),
+            .reshape(d_model // 2, width),
         ],
         axis=0,
     )
-    half = own_w.shape[0] // 2
-    own_a, own_b = own_w[:half], own_w[half:]
     prev_a = lax.ppermute(own_a, "x", up_x)
     next_b = lax.ppermute(own_b, "x", down_x)
     prev_b = lax.ppermute(own_b, "x", up_x)
@@ -174,7 +176,7 @@
     other_x = lax.ppermute(own_x, "core", swap)
     def scratch(blocks):
         return [
-            pltpu.VMEM((blocks,) + own_w.shape, BF),
+            pltpu.VMEM((blocks, 2 * half, width), BF),
             pltpu.VMEM((slots, d_model), BF),
             pltpu.VMEM((slots, blocks * ff), BF),
         ]
@@ -183,7 +185,7 @@
         near_kernel,
         in_specs=[smem, vmem, vmem] + [hbm] * 6,
         out_specs=vmem,
-        out_shape=jax.ShapeDtypeStruct((slots, d_model), F32),
+        out_shape=jax.ShapeDtypeStruct((slots, d_model), BF),
         scratch_shapes=scratch(3) + [pltpu.SemaphoreType.DMA((6,))],
         compiler_params=params,
         name="near",

time: 269 us -> 269 us (level)
  transfers between devices with their start and end apart: 17 -> 17, of which waited for: 11 -> 11; matrix products, arithmetic and copies ran while one was open for 0% -> 1% of each run, Pallas kernels for 6% -> 5%
where the time goes in v7:
time: 269 us; the launch traced here: 267 us
  waiting for transfers between devices  83.4 us (31%)
  starting transfers between devices  82.4 us (31%)
  blocking collectives  61 us (23%)
  Pallas kernels  25.9 us (10%)
  other arithmetic  8.24 us (3%)
  local copies, waits for them, and re-layouts  6.08 us (2%)
    all_gather x1, blocking collectives, shards(): lax.all_gather(jnp.concatenate([tokens, meta], axis=0), 'high', axis=0, t...  61 us
    all_to_all x1, waiting for transfers between devices, shards(): lax.all_to_all(out.reshape(-1, pair * CAP, piece), peers, split_axis=0, c...  28.8 us
    all_to_all x1, waiting for transfers between devices, shards(): lax.all_to_all(rows.reshape(-1, pair * CAP, piece), peers, split_axis=0,...  20.3 us
    ppermute x3, waiting for transfers between devices, shards(): rising = lax.ppermute(rising, 'high', up_z)  16.6 us
    ppermute x2, starting transfers between devices, shards(): falling = lax.ppermute(falling, 'high', down_z)  14.4 us
    pallas_call x1, Pallas kernels, shards(): pl.pallas_call(near_kernel, in_specs=[smem, vmem, vmem] + [hbm] * 6, out_...  10.2 us
    ppermute x1, starting transfers between devices, shards(): falling = lax.ppermute(mine_for(reach + 1).astype(BF), 'high', down_z)  10.1 us
    ppermute x1, starting transfers between devices, shards(): rising = lax.ppermute(mine_for(reach).astype(BF), 'high', up_z)  9.1 us
  transfers between devices with their start and end apart: 17, of which 11 were waited for; matrix products, arithmetic and copies ran while one was open for 1% of the time, Pallas kernels for 5%

profile of v7, /device:TPU:8, one launch (start us, length us, event | category | flops | bytes accessed | tf_op | source)
XLA Modules:
  0.0 267.5 jit_solution(10888382002545113379)
XLA Ops:
  1.7 3.5 %collective-permute-start = (bf16[3072,256]{1,0:T(8,128)(2,1)S(1)}, bf16[3072,256]{1,0:T(8,128)(2,1)}, u32[]{:S(2)}, u32[]{:S(2)}) collective-permute-start(bf16[3072,256]{1,0:T(8,128)(2,1)S(1)} %pad_maximum_fusion.refs_0_), channel_id=1, source_target_pairs={{0,256},{256,512},{512,768},{768,0},{1,257},{257,513},{513,769},{7... | collective-permute-start | bytes 4718600 | tf_op jit(solution)/shard_map/ppermute | solution.py:136
  8.3 3.6 %collective-permute-start.1 = (bf16[3072,256]{1,0:T(8,128)(2,1)}, bf16[3072,256]{1,0:T(8,128)(2,1)}, u32[]{:S(2)}, u32[]{:S(2)}) collective-permute-start(bf16[3072,256]{1,0:T(8,128)(2,1)} %pad_maximum_fusion.1.refs_1_), channel_id=1, source_target_pairs={{0,768},{256,0},{512,256},{768,512},{1,769},{257,1},{513,257},{769... | collective-permute-start | bytes 4718600 | tf_op jit(solution)/shard_map/ppermute | solution.py:137
  12.0 2.2 collective-permute-start.2
  14.2 4.9 %collective-permute-start.3 = (bf16[3072,256]{1,0:T(8,128)(2,1)S(1)}, bf16[3072,256]{1,0:T(8,128)(2,1)}, u32[]{:S(2)}, u32[]{:S(2)}) collective-permute-start(bf16[3072,256]{1,0:T(8,128)(2,1)S(1)} %pad_maximum_fusion.refs_0_), channel_id=1, source_target_pairs={{0,768},{256,0},{512,256},{768,512},{1,769},{257,1},{513,257},{769... | collective-permute-start | bytes 4718600 | tf_op jit(solution)/shard_map/ppermute | solution.py:139
  19.2 61.0 %all-gather = bf16[640,512]{1,0:T(8,128)(2,1)} all-gather(bf16[80,512]{1,0:T(8,128)(2,1)S(1)} %fusion.8), channel_id=2, replica_groups=mesh['x'=4,'core'=2,'narrow'=4,'high'=8,'low'=4] {'high'}, dimensions={0}, use_global_device_ids=true | all-gather | bytes 737280 | tf_op jit(solution)/shard_map/all_gather | solution.py:147
  80.3 4.0 %select.32 = (bf16[4,256,512]{2,1,0:T(8,128)(2,1)}, bf16[4,256,128]{2,1,0:T(8,128)(2,1)}) custom-call(s32[1]{0:T(128)} %bitcast.refs_0_, bf16[8,80,512]{2,1,0:T(8,128)(2,1)} %bitcast.54), custom_call_target="tpu_custom_call" | custom-call | tf_op jit(solution)/shard_map/select/pallas_call | solution.py:156
  84.3 7.7 %all-to-all-start = ((bf16[64,16,512]{2,1,0:T(8,128)(2,1)}), bf16[64,16,512]{2,1,0:T(8,128)(2,1)S(1)}, u32[]{:S(2)}, u32[]{:S(2)}) async-start(bf16[64,16,512]{2,1,0:T(8,128)(2,1)} %bitcast.61), calls=%async_computation | async-start | bytes 2097152 | tf_op jit(solution)/shard_map/all_to_all | solution.py:173
  92.0 3.4 %collective-permute-start.5 = (bf16[3072,256]{1,0:T(8,128)(2,1)}, bf16[3072,256]{1,0:T(8,128)(2,1)}, u32[]{:S(2)}, u32[]{:S(2)}) collective-permute-start(bf16[3072,256]{1,0:T(8,128)(2,1)} %collective-permute-done.refs_2_), channel_id=1, source_target_pairs={{0,256},{256,512},{512,768},{768,0},{1,257},{257,513},{513,769},{7... | collective-permute-start | bytes 4718600 | tf_op jit(solution)/shard_map/ppermute | solution.py:151
  95.4 3.7 %collective-permute-start.6 = (bf16[3072,256]{1,0:T(8,128)(2,1)}, bf16[3072,256]{1,0:T(8,128)(2,1)}, u32[]{:S(2)}, u32[]{:S(2)}) collective-permute-start(bf16[3072,256]{1,0:T(8,128)(2,1)} %collective-permute-done.1.refs_5_), channel_id=1, source_target_pairs={{0,768},{256,0},{512,256},{768,512},{1,769},{257,1},{513,257},{769... | collective-permute-start | bytes 4718600 | tf_op jit(solution)/shard_map/ppermute | solution.py:152
  99.1 20.3 %all-to-all-done = bf16[64,16,512]{2,1,0:T(8,128)(2,1)S(1)} async-done(((bf16[64,16,512]{2,1,0:T(8,128)(2,1)}), bf16[64,16,512]{2,1,0:T(8,128)(2,1)S(1)}, u32[]{:S(2)}, u32[]{:S(2)}) %all-to-all-start) | async-done | bytes 1048608 | tf_op jit(solution)/shard_map/all_to_all | solution.py:173
  119.4 1.9 collective-permute-start.4
  121.3 2.6 collective-permute-done.4.other_x
  124.9 10.2 %near.1.near_ref = bf16[256,4096]{1,0:T(8,128)(2,1)} custom-call(s32[1]{0:T(128)} %bitcast.10.core_ref, bf16[4,256,512]{2,1,0:T(8,128)(2,1)} %bitcast.49, bf16[4,256,512]{2,1,0:T(8,128)(2,1)} %copy-done.3, bf16[3072,256]{1,0:T(8,128)(2,1)} %copy-done.1, bf16[3072,256]{1,0:T(8,128)(2,1)} %pad_maximum_fusion.1.refs_1_, ...), custom_call_target="tpu_custom_call" | custom-call | tf_op jit(solution)/shard_map/near/pallas_call | solution.py:184
  135.2 4.0 %collective-permute-done.5.refs_0_ = bf16[3072,256]{1,0:T(8,128)(2,1)} collective-permute-done((bf16[3072,256]{1,0:T(8,128)(2,1)}, bf16[3072,256]{1,0:T(8,128)(2,1)}, u32[]{:S(2)}, u32[]{:S(2)}) %collective-permute-start.5) | collective-permute-done | bytes 1572896 | tf_op jit(solution)/shard_map/ppermute | solution.py:151
  139.1 8.0 %far.1 = (bf16[4,256,512]{2,1,0:T(8,128)(2,1)}, bf16[4,256,512]{2,1,0:T(8,128)(2,1)}) custom-call(s32[1]{0:T(128)} %bitcast.10.core_ref, bf16[4,256,512]{2,1,0:T(8,128)(2,1)} %bitcast.50, bf16[4,256,512]{2,1,0:T(8,128)(2,1)} %copy-done.3, bf16[256,4096]{1,0:T(8,128)(2,1)} %near.1.near_ref, bf16[3072,256]{1,0:T(8,128)(2,1)} %collective-permute-done.5.refs_0_, ...), custom_call_target="tpu_custom_call" | custom-call | tf_op jit(solution)/shard_map/far/pallas_call | solution.py:193
  147.1 1.9 collective-permute-start.7
  149.0 2.8 %collective-permute-done.7 = bf16[4,256,512]{2,1,0:T(8,128)(2,1)S(1)} collective-permute-done((bf16[4,256,512]{2,1,0:T(8,128)(2,1)}, bf16[4,256,512]{2,1,0:T(8,128)(2,1)S(1)}, u32[]{:S(2)}, u32[]{:S(2)}) %collective-permute-start.7) | collective-permute-done | bytes 1048608 | tf_op jit(solution)/shard_map/ppermute | solution.py:203
  151.8 2.5 add_convert_fusion
  154.3 9.0 %all-to-all-start.1 = ((bf16[64,16,512]{2,1,0:T(8,128)(2,1)}), bf16[64,16,512]{2,1,0:T(8,128)(2,1)S(1)}, u32[]{:S(2)}, u32[]{:S(2)}) async-start(bf16[64,16,512]{2,1,0:T(8,128)(2,1)} %bitcast.13), calls=%async_computation.1 | async-start | bytes 2097152 | tf_op jit(solution)/shard_map/all_to_all | solution.py:205
  163.3 28.8 %all-to-all-done.1 = bf16[64,16,512]{2,1,0:T(8,128)(2,1)S(1)} async-done(((bf16[64,16,512]{2,1,0:T(8,128)(2,1)}), bf16[64,16,512]{2,1,0:T(8,128)(2,1)S(1)}, u32[]{:S(2)}, u32[]{:S(2)}) %all-to-all-start.1) | async-done | bytes 1048608 | tf_op jit(solution)/shard_map/all_to_all | solution.py:205
  193.1 3.7 %combine.1 = bf16[4,128,512]{2,1,0:T(8,128)(2,1)} custom-call(bf16[4,256,128]{2,1,0:T(8,128)(2,1)} %get-tuple-element.16.weight_ref, bf16[4,256,512]{2,1,0:T(8,128)(2,1)} %bitcast.52), custom_call_target="tpu_custom_call" | custom-call | tf_op jit(solution)/shard_map/combine/pallas_call | solution.py:208
  197.7 9.1 %collective-permute-start.8 = (bf16[64,512]{1,0:T(8,128)(2,1)S(1)}, bf16[64,512]{1,0:T(8,128)(2,1)S(1)}, u32[]{:S(2)}, u32[]{:S(2)}) collective-permute-start(bf16[64,512]{1,0:T(8,128)(2,1)S(1)} %get-tuple-element.29), channel_id=1, source_target_pairs={{0,4},{4,8},{8,12},{12,16},{16,20},{20,24},{24,28},{28,0},{1,5},{5... | collective-permute-start | bytes 196616 | tf_op jit(solution)/shard_map/ppermute | solution.py:229
  206.9 10.1 %collective-permute-start.12 = (bf16[64,512]{1,0:T(8,128)(2,1)S(1)}, bf16[64,512]{1,0:T(8,128)(2,1)S(1)}, u32[]{:S(2)}, u32[]{:S(2)}) collective-permute-start(bf16[64,512]{1,0:T(8,128)(2,1)S(1)} %get-tuple-element.30), channel_id=1, source_target_pairs={{0,28},{4,0},{8,4},{12,8},{16,12},{20,16},{24,20},{28,24},{1,29},{... | collective-permute-start | bytes 196616 | tf_op jit(solution)/shard_map/ppermute | solution.py:230
  217.0 4.4 %collective-permute-done.8 = bf16[64,512]{1,0:T(8,128)(2,1)S(1)} collective-permute-done((bf16[64,512]{1,0:T(8,128)(2,1)S(1)}, bf16[64,512]{1,0:T(8,128)(2,1)S(1)}, u32[]{:S(2)}, u32[]{:S(2)}) %collective-permute-start.8) | collective-permute-done | bytes 65568 | tf_op jit(solution)/shard_map/ppermute | solution.py:229
  222.3 1.9 collective-permute-start.9
  224.3 9.2 %collective-permute-done.9 = bf16[64,512]{1,0:T(8,128)(2,1)S(1)} collective-permute-done((bf16[64,512]{1,0:T(8,128)(2,1)S(1)}, bf16[64,512]{1,0:T(8,128)(2,1)S(1)}, u32[]{:S(2)}, u32[]{:S(2)}) %collective-permute-start.9) | collective-permute-done | bytes 65568 | tf_op jit(solution)/shard_map/ppermute | solution.py:233
  234.4 2.4 collective-permute-start.10
  236.8 7.4 %collective-permute-start.13 = (bf16[64,512]{1,0:T(8,128)(2,1)S(1)}, bf16[64,512]{1,0:T(8,128)(2,1)S(1)}, u32[]{:S(2)}, u32[]{:S(2)}) collective-permute-start(bf16[64,512]{1,0:T(8,128)(2,1)S(1)} %get-tuple-element.28), channel_id=1, source_target_pairs={{0,28},{4,0},{8,4},{12,8},{16,12},{20,16},{24,20},{28,24},{1,29},{... | collective-permute-start | bytes 196616 | tf_op jit(solution)/shard_map/ppermute | solution.py:236
  244.5 3.5 %collective-permute-done.13 = bf16[64,512]{1,0:T(8,128)(2,1)S(1)} collective-permute-done((bf16[64,512]{1,0:T(8,128)(2,1)S(1)}, bf16[64,512]{1,0:T(8,128)(2,1)S(1)}, u32[]{:S(2)}, u32[]{:S(2)}) %collective-permute-start.13) | collective-permute-done | bytes 65568 | tf_op jit(solution)/shard_map/ppermute | solution.py:236
  248.9 7.0 %collective-permute-start.14 = (bf16[64,512]{1,0:T(8,128)(2,1)S(1)}, bf16[64,512]{1,0:T(8,128)(2,1)S(1)}, u32[]{:S(2)}, u32[]{:S(2)}) collective-permute-start(bf16[64,512]{1,0:T(8,128)(2,1)S(1)} %get-tuple-element.26), channel_id=1, source_target_pairs={{0,28},{4,0},{8,4},{12,8},{16,12},{20,16},{24,20},{28,24},{1,29},{... | collective-permute-start | bytes 196616 | tf_op jit(solution)/shard_map/ppermute | solution.py:236
  255.9 2.7 %collective-permute-start.11 = (bf16[64,512]{1,0:T(8,128)(2,1)S(1)}, bf16[64,512]{1,0:T(8,128)(2,1)S(1)}, u32[]{:S(2)}, u32[]{:S(2)}) collective-permute-start(bf16[64,512]{1,0:T(8,128)(2,1)S(1)} %get-tuple-element.25), channel_id=1, source_target_pairs={{0,4},{4,8},{8,12},{12,16},{16,20},{20,24},{24,28},{28,0},{1,5},{5... | collective-permute-start | bytes 196616 | tf_op jit(solution)/shard_map/ppermute | solution.py:233
  258.9 7.0 %collective-permute-done.11 = bf16[64,512]{1,0:T(8,128)(2,1)S(1)} collective-permute-done((bf16[64,512]{1,0:T(8,128)(2,1)S(1)}, bf16[64,512]{1,0:T(8,128)(2,1)S(1)}, u32[]{:S(2)}, u32[]{:S(2)}) %collective-permute-start.11) | collective-permute-done | bytes 65568 | tf_op jit(solution)/shard_map/ppermute | solution.py:233
  (43 shorter events, 12.4 us)
Async XLA Ops:
  1.5 4.8 %copy-start.4 = (bf16[1,128,4096]{2,1,0:T(8,128)(2,1)S(1)}, bf16[1,128,4096]{2,1,0:T(8,128)(2,1)}, u32[]{:S(2)}) copy-start(bf16[1,128,4096]{2,1,0:T(8,128)(2,1)} %param.11) | copy-start | bytes 3145732
  1.7 12.5 %copy-start.1 = (bf16[3072,256]{1,0:T(8,128)(2,1)}, bf16[3072,256]{1,0:T(8,128)(2,1)S(1)}, u32[]{:S(2)}) copy-start(bf16[3072,256]{1,0:T(8,128)(2,1)S(1)} %pad_maximum_fusion.refs_0_) | copy-start | bytes 4718596
  1.7 78.6 %collective-permute-start = (bf16[3072,256]{1,0:T(8,128)(2,1)S(1)}, bf16[3072,256]{1,0:T(8,128)(2,1)}, u32[]{:S(2)}, u32[]{:S(2)}) collective-permute-start(bf16[3072,256]{1,0:T(8,128)(2,1)S(1)} %pad_maximum_fusion.refs_0_), channel_id=1, source_target_pairs={{0,256},{256,512},{512,768},{768,0},{1,257},{257,513},{513,769},{7... | collective-permute-start | bytes 4718600 | tf_op jit(solution)/shard_map/ppermute | solution.py:136
  6.9 12.1 %copy-start.6 = (f32[64,8]{0,1:T(8,128)S(1)}, f32[64,8]{0,1:T(8,128)}, u32[]{:S(2)}) copy-start(f32[64,8]{0,1:T(8,128)} %param.8) | copy-start | bytes 6148
  6.9 12.2 %copy-start.7 = (s32[64,8]{0,1:T(8,128)S(1)}, s32[64,8]{0,1:T(8,128)}, u32[]{:S(2)}) copy-start(s32[64,8]{0,1:T(8,128)} %param.7) | copy-start | bytes 6148
  6.9 12.3 %copy-start.5 = (bf16[64,512]{1,0:T(8,128)(2,1)S(1)}, bf16[64,512]{1,0:T(8,128)(2,1)}, u32[]{:S(2)}) copy-start(bf16[64,512]{1,0:T(8,128)(2,1)} %param.6) | copy-start | bytes 196612
  8.3 72.0 %collective-permute-start.1 = (bf16[3072,256]{1,0:T(8,128)(2,1)}, bf16[3072,256]{1,0:T(8,128)(2,1)}, u32[]{:S(2)}, u32[]{:S(2)}) collective-permute-start(bf16[3072,256]{1,0:T(8,128)(2,1)} %pad_maximum_fusion.1.refs_1_), channel_id=1, source_target_pairs={{0,768},{256,0},{512,256},{768,512},{1,769},{257,1},{513,257},{769... | collective-permute-start | bytes 4718600 | tf_op jit(solution)/shard_map/ppermute | solution.py:137
  12.0 72.4 %collective-permute-start.2 = (bf16[3072,256]{1,0:T(8,128)(2,1)}, bf16[3072,256]{1,0:T(8,128)(2,1)}, u32[]{:S(2)}, u32[]{:S(2)}) collective-permute-start(bf16[3072,256]{1,0:T(8,128)(2,1)} %pad_maximum_fusion.1.refs_1_), channel_id=1, source_target_pairs={{0,256},{256,512},{512,768},{768,0},{1,257},{257,513},{513,769},{7... | collective-permute-start | bytes 4718600 | tf_op jit(solution)/shard_map/ppermute | solution.py:138
  14.2 70.2 %collective-permute-start.3 = (bf16[3072,256]{1,0:T(8,128)(2,1)S(1)}, bf16[3072,256]{1,0:T(8,128)(2,1)}, u32[]{:S(2)}, u32[]{:S(2)}) collective-permute-start(bf16[3072,256]{1,0:T(8,128)(2,1)S(1)} %pad_maximum_fusion.refs_0_), channel_id=1, source_target_pairs={{0,768},{256,0},{512,256},{768,512},{1,769},{257,1},{513,257},{769... | collective-permute-start | bytes 4718600 | tf_op jit(solution)/shard_map/ppermute | solution.py:139
  84.3 35.1 %all-to-all-start = ((bf16[64,16,512]{2,1,0:T(8,128)(2,1)}), bf16[64,16,512]{2,1,0:T(8,128)(2,1)S(1)}, u32[]{:S(2)}, u32[]{:S(2)}) async-start(bf16[64,16,512]{2,1,0:T(8,128)(2,1)} %bitcast.61), calls=%async_computation | async-start | bytes 2097152 | tf_op jit(solution)/shard_map/all_to_all | solution.py:173
  92.0 47.1 %collective-permute-start.5 = (bf16[3072,256]{1,0:T(8,128)(2,1)}, bf16[3072,256]{1,0:T(8,128)(2,1)}, u32[]{:S(2)}, u32[]{:S(2)}) collective-permute-start(bf16[3072,256]{1,0:T(8,128)(2,1)} %collective-permute-done.refs_2_), channel_id=1, source_target_pairs={{0,256},{256,512},{512,768},{768,0},{1,257},{257,513},{513,769},{7... | collective-permute-start | bytes 4718600 | tf_op jit(solution)/shard_map/ppermute | solution.py:151
  95.4 43.7 %collective-permute-start.6 = (bf16[3072,256]{1,0:T(8,128)(2,1)}, bf16[3072,256]{1,0:T(8,128)(2,1)}, u32[]{:S(2)}, u32[]{:S(2)}) collective-permute-start(bf16[3072,256]{1,0:T(8,128)(2,1)} %collective-permute-done.1.refs_5_), channel_id=1, source_target_pairs={{0,768},{256,0},{512,256},{768,512},{1,769},{257,1},{513,257},{769... | collective-permute-start | bytes 4718600 | tf_op jit(solution)/shard_map/ppermute | solution.py:152
  119.4 4.5 %copy-start = (bf16[64,16,512]{2,1,0:T(8,128)(2,1)}, bf16[64,16,512]{2,1,0:T(8,128)(2,1)S(1)}, u32[]{:S(2)}) copy-start(bf16[64,16,512]{2,1,0:T(8,128)(2,1)S(1)} %all-to-all-done) | copy-start | bytes 3145732
  119.4 4.5 %collective-permute-start.4 = (bf16[4,256,512]{2,1,0:T(8,128)(2,1)S(1)}, bf16[4,256,512]{2,1,0:T(8,128)(2,1)S(1)}, u32[]{:S(2)}, u32[]{:S(2)}) collective-permute-start(bf16[4,256,512]{2,1,0:T(8,128)(2,1)S(1)} %bitcast.48), channel_id=1, source_target_pairs={{0,128},{128,0},{1,129},{129,1},{2,130},{130,2},{3,131},{131,3},{4... | collective-permute-start | bytes 3145736 | tf_op jit(solution)/shard_map/ppermute | solution.py:176
  124.0 1.0 copy-start.3
  147.1 4.8 %collective-permute-start.7 = (bf16[4,256,512]{2,1,0:T(8,128)(2,1)}, bf16[4,256,512]{2,1,0:T(8,128)(2,1)S(1)}, u32[]{:S(2)}, u32[]{:S(2)}) collective-permute-start(bf16[4,256,512]{2,1,0:T(8,128)(2,1)} %get-tuple-element.24), channel_id=1, source_target_pairs={{0,128},{128,0},{1,129},{129,1},{2,130},{130,2},{3,131},{131,3},{4... | collective-permute-start | bytes 3145736 | tf_op jit(solution)/shard_map/ppermute | solution.py:203
  154.3 37.8 %all-to-all-start.1 = ((bf16[64,16,512]{2,1,0:T(8,128)(2,1)}), bf16[64,16,512]{2,1,0:T(8,128)(2,1)S(1)}, u32[]{:S(2)}, u32[]{:S(2)}) async-start(bf16[64,16,512]{2,1,0:T(8,128)(2,1)} %bitcast.13), calls=%async_computation.1 | async-start | bytes 2097152 | tf_op jit(solution)/shard_map/all_to_all | solution.py:205
  192.2 1.0 copy-start.2
  197.7 23.7 %collective-permute-start.8 = (bf16[64,512]{1,0:T(8,128)(2,1)S(1)}, bf16[64,512]{1,0:T(8,128)(2,1)S(1)}, u32[]{:S(2)}, u32[]{:S(2)}) collective-permute-start(bf16[64,512]{1,0:T(8,128)(2,1)S(1)} %get-tuple-element.29), channel_id=1, source_target_pairs={{0,4},{4,8},{8,12},{12,16},{16,20},{20,24},{24,28},{28,0},{1,5},{5... | collective-permute-start | bytes 196616 | tf_op jit(solution)/shard_map/ppermute | solution.py:229
  206.9 17.4 %collective-permute-start.12 = (bf16[64,512]{1,0:T(8,128)(2,1)S(1)}, bf16[64,512]{1,0:T(8,128)(2,1)S(1)}, u32[]{:S(2)}, u32[]{:S(2)}) collective-permute-start(bf16[64,512]{1,0:T(8,128)(2,1)S(1)} %get-tuple-element.30), channel_id=1, source_target_pairs={{0,28},{4,0},{8,4},{12,8},{16,12},{20,16},{24,20},{28,24},{1,29},{... | collective-permute-start | bytes 196616 | tf_op jit(solution)/shard_map/ppermute | solution.py:230
  222.3 11.2 %collective-permute-start.9 = (bf16[64,512]{1,0:T(8,128)(2,1)S(1)}, bf16[64,512]{1,0:T(8,128)(2,1)S(1)}, u32[]{:S(2)}, u32[]{:S(2)}) collective-permute-start(bf16[64,512]{1,0:T(8,128)(2,1)S(1)} %fusion.5), channel_id=1, source_target_pairs={{0,4},{4,8},{8,12},{12,16},{16,20},{20,24},{24,28},{28,0},{1,5},{5... | collective-permute-start | bytes 196616 | tf_op jit(solution)/shard_map/ppermute | solution.py:233
  234.4 10.1 %collective-permute-start.10 = (bf16[64,512]{1,0:T(8,128)(2,1)S(1)}, bf16[64,512]{1,0:T(8,128)(2,1)S(1)}, u32[]{:S(2)}, u32[]{:S(2)}) collective-permute-start(bf16[64,512]{1,0:T(8,128)(2,1)S(1)} %get-tuple-element.27), channel_id=1, source_target_pairs={{0,4},{4,8},{8,12},{12,16},{16,20},{20,24},{24,28},{28,0},{1,5},{5... | collective-permute-start | bytes 196616 | tf_op jit(solution)/shard_map/ppermute | solution.py:233
  236.8 11.2 %collective-permute-start.13 = (bf16[64,512]{1,0:T(8,128)(2,1)S(1)}, bf16[64,512]{1,0:T(8,128)(2,1)S(1)}, u32[]{:S(2)}, u32[]{:S(2)}) collective-permute-start(bf16[64,512]{1,0:T(8,128)(2,1)S(1)} %get-tuple-element.28), channel_id=1, source_target_pairs={{0,28},{4,0},{8,4},{12,8},{16,12},{20,16},{24,20},{28,24},{1,29},{... | collective-permute-start | bytes 196616 | tf_op jit(solution)/shard_map/ppermute | solution.py:236
  248.9 10.1 %collective-permute-start.14 = (bf16[64,512]{1,0:T(8,128)(2,1)S(1)}, bf16[64,512]{1,0:T(8,128)(2,1)S(1)}, u32[]{:S(2)}, u32[]{:S(2)}) collective-permute-start(bf16[64,512]{1,0:T(8,128)(2,1)S(1)} %get-tuple-element.26), channel_id=1, source_target_pairs={{0,28},{4,0},{8,4},{12,8},{16,12},{20,16},{24,20},{28,24},{1,29},{... | collective-permute-start | bytes 196616 | tf_op jit(solution)/shard_map/ppermute | solution.py:236
  255.9 10.1 %collective-permute-start.11 = (bf16[64,512]{1,0:T(8,128)(2,1)S(1)}, bf16[64,512]{1,0:T(8,128)(2,1)S(1)}, u32[]{:S(2)}, u32[]{:S(2)}) collective-permute-start(bf16[64,512]{1,0:T(8,128)(2,1)S(1)} %get-tuple-element.25), channel_id=1, source_target_pairs={{0,4},{4,8},{8,12},{12,16},{16,20},{20,24},{24,28},{28,0},{1,5},{5... | collective-permute-start | bytes 196616 | tf_op jit(solution)/shard_map/ppermute | solution.py:233
